TPU v7x, 32 devices: a whole 2x2x4 slice. The times are simulated.
32 devices in a mesh: runs: 2 (over y), sec: 4 (over z), mpo: 4 (over x, core), rep: 1.
Axes of the slice: x: 2, y: 2, z: 4, core: 2. Of those that a mesh axis runs over, the one named last changes fastest.
Arguments:
- wavefunction: float32 [8192, 256], P(('runs', 'sec'), 'rep'), parts along dimension 0, may hold values from -18 to 18
- left_blocks: float32 [64, 32, 128, 128], P(('runs', 'sec'), 'mpo'), parts along dimension 0, may hold values from -2 to 5
- right_blocks: float32 [64, 256, 256], P(('runs', 'mpo'), None, 'rep'), parts along dimension 0, may hold values from -2 to 5
- block_rows: int32 [64], P(('runs', 'sec')), parts along dimension 0, may hold values from 16 to 128, as said below
- term_charge: int32 [32], P('mpo'), may hold values from 0 to 4, as said below
Outputs:
- applied: float32 [8192, 256], P(('runs', 'sec'), 'rep'), parts along dimension 0
- correction: float32 [8192, 256], P(('runs', 'sec'), 'rep'), parts along dimension 0
There are 2 independent parts, one for each index of `runs`. A program takes and returns all parts, laid end to end along the dimension named above; an argument that names none is the same for every part. Nothing has to cross between parts.
Inputs may be any that keep to these rules, and one draw needn't show every extreme that they name: `block_rows`: some sector is full and some has the fewest rows. `term_charge`: every class occurs.
All inputs are finite; a program needn't handle non-finite values.
Results may differ from a plain program's by a relative error of at most 0.0003.
Values sent between devices are 32-bit elements; how exact they have to be, the bound alone decides.
No kernel may reach another device: no remote copies, remote signals or barrier semaphores. Data moves between devices by JAX's collectives and lax.ppermute only.
A program may use at most 64 MiB of HBM per device.

v0:
```python
import functools

import jax
import jax.numpy as jnp
from jax import lax
from jax.experimental import pallas as pl
from jax.experimental.pallas import tpu as pltpu
from jax.sharding import PartitionSpec as P

QD = 16
F32 = jnp.float32
BF16 = jnp.bfloat16
VMEM = pl.BlockSpec(memory_space=pltpu.VMEM)
SMEM = pl.BlockSpec(memory_space=pltpu.SMEM)
HBM = pl.BlockSpec(memory_space=pltpu.HBM)
ANY = pl.BlockSpec(memory_space=pl.ANY)


def split(x):
    high = x.astype(BF16)
    return high, (x - high.astype(F32)).astype(BF16)


def masked(rows, live):
    index = lax.broadcasted_iota(jnp.int32, rows.shape, 0)
    return jnp.where(index < live, rows, 0.0)


OWN_VMEM, PAIR_VMEM = 46, 32
GROUP = 2


def place():
    mpo = lax.axis_index("mpo")
    return lax.rem(mpo, 2), lax.rem(lax.div(mpo, 2), 2), lax.axis_index("sec")


def sector_rows(wave, sector, block):
    return wave.at[pl.ds(pl.multiple_of(sector * block, block), block), :]


def prepare_kernel(half, rows_hbm, wave, left, mine_a, mine_b, halo, left_send, rows_ref, sem):
    core, side, _ = place()
    block = halo.shape[0]
    count = rows_ref.shape[0]
    part = half // 2
    wanted = (
        (core * half + side, mine_a),
        ((1 - core) * (count - 1), halo),
        (core * half + part + side, mine_b),
    )
    moves = [pltpu.make_async_copy(rows_hbm, rows_ref, sem.at[0])]
    for i, (sector, ref) in enumerate(wanted):
        moves.append(pltpu.make_async_copy(sector_rows(wave, sector, block), ref, sem.at[i + 1]))
    moves.append(pltpu.make_async_copy(left.at[pl.ds((1 - core) * half, half)], left_send, sem.at[4]))
    for move in moves:
        move.start()
    moves[0].wait()
    for move, (sector, ref) in zip(moves[1:], wanted):
        move.wait()
        ref[...] = masked(ref[...], rows_ref[sector])
    moves[-1].wait()


def put(src, at, value):
    wide = value.shape[1]
    high, low = split(value)
    here = pl.ds(at, value.shape[0])
    src[here, 0:wide] = high
    src[here, wide : 2 * wide] = low
    src[here, 2 * wide : 3 * wide] = high


def pack(cls_ref, choose, order, offsets):
    n = jnp.int32(0)
    for t in range(cls_ref.shape[0]):
        chosen, at = choose(cls_ref[t])

        @pl.when(chosen)
        def _(n=n, t=t, at=at):
            order[n] = t
            offsets[n] = at

        n = n + chosen.astype(jnp.int32)
    return n


def add_terms(n, order, offsets, src, left, right, first, acc, tbuf, ready=None):
    rows = acc.shape[0]
    block = left.shape[-1]
    count = rows // block

    @pl.loop(0, lax.div(n + GROUP - 1, GROUP))
    def _(i):
        terms, real = [], []
        for j in range(GROUP):
            k = jnp.minimum(i * GROUP + j, n - 1)
            real.append(i * GROUP + j < n)
            terms.append(order[k])
            if ready is not None:

                @pl.when(real[j])
                def _(j=j):
                    ready(terms[j])

            at = pl.ds(pl.multiple_of(offsets[k], block), rows)
            high, low = split(right[terms[j]])
            wide = jnp.concatenate([high, high, low], 0)
            high, low = split(jnp.dot(src[at, :], wide, preferred_element_type=F32))
            for s in range(count):
                here = slice(s * block, (s + 1) * block)
                tbuf[s, j * block : (j + 1) * block, :] = high[here]
                tbuf[s, (GROUP + j) * block : (GROUP + j + 1) * block, :] = low[here]
        for s in range(count):
            blocks = [left[first + s, terms[0]]]
            for j in range(1, GROUP):
                blocks.append(jnp.where(real[j], left[first + s, terms[j]], 0.0))
            high, low = split(jnp.concatenate(blocks, 1))
            acc[s * block : (s + 1) * block, :] += jnp.dot(
                jnp.concatenate([high, high, low], 1),
                jnp.concatenate([tbuf[s], tbuf[s, 0 : GROUP * block]], 0),
                preferred_element_type=F32,
            )


def near_kernel(own, *refs):
    if own:
        cls, left_hbm, right_hbm, rows_hbm, whole, wave, halo, acc, left, right, src, live, *rest = refs
        rows_ref = rest.pop(0)
    else:
        cls, left_hbm, right_hbm, src, acc_in, acc, left, right, *rest = refs
    tbuf, cls_ref, order, offsets, sem = rest
    half, terms, block, _ = left.shape
    core, _, _ = place()

    fetch_cls = pltpu.make_async_copy(cls, cls_ref, sem.at[0, terms])
    fetch_cls.start()
    if own:
        fetch_rows = pltpu.make_async_copy(rows_hbm, rows_ref, sem.at[1, terms])
        fetch_rows.start()
    first = core * half if own else 0

    def fetch(t):
        return (
            pltpu.make_async_copy(left_hbm.at[pl.ds(first, half), t], left.at[:, t], sem.at[0, t]),
            pltpu.make_async_copy(right_hbm.at[t], right.at[t], sem.at[1, t]),
        )

    for t in range(terms):
        for move in fetch(t):
            move.start()

    if own:
        acc[...] = jnp.zeros_like(acc)
        fetch_rows.wait()
        count = rows_ref.shape[0]
        for s in range(count):
            here = pl.ds(s * block, block)
            live[here, :] = masked(wave[here, :], rows_ref[s])
        for i in range(half + 2):
            sector = core * half - 1 + i
            inside = jnp.logical_and(sector >= 0, sector < count)
            at = i * block
            if 0 < i < half + 1:
                put(src, at, masked(sector_rows(whole, sector, block)[...], rows_ref[sector]))
                continue

            @pl.when(inside)
            def _(sector=sector, at=at):
                put(src, at, masked(sector_rows(whole, sector, block)[...], rows_ref[sector]))

            @pl.when(jnp.logical_not(inside))
            def _(at=at):
                put(src, at, halo[...])
    else:
        acc[...] = acc_in[...]

    fetch_cls.wait()

    def near(c):
        at = jnp.where(c == 0, block, jnp.where(c == 3, 2 * block, 0))
        return jnp.logical_or(c == 0, c >= 3), at

    def wait(t):
        for move in fetch(t):
            move.wait()

    n = pack(cls_ref, near, order, offsets)
    add_terms(n, order, offsets, src, left, right, 0, acc, tbuf, ready=wait)
    for t in range(terms):

        @pl.when(jnp.logical_not(near(cls_ref[t])[0]))
        def _(t=t):
            wait(t)


def far_kernel(lo, shift, secs, chained, *refs):
    refs = list(refs)
    cls, cls_pair, rows_hbm, left, right, left_pair, right_pair, live, mine, other, acc_in = refs[:11]
    sums_in = refs.pop(11) if chained else None
    acc, sums, src, tbuf, rows_ref, cls_ref, order, offsets, sem = refs[11:]
    rows, cols = acc.shape
    half, terms, block, _ = left.shape
    count = rows // block
    core, side, sec = place()
    merged = mine.shape[0] == 1

    moves = [
        pltpu.make_async_copy(rows_hbm, rows_ref, sem.at[0]),
        pltpu.make_async_copy(cls, cls_ref.at[0], sem.at[1]),
        pltpu.make_async_copy(cls_pair, cls_ref.at[1], sem.at[2]),
    ]
    for move in moves:
        move.start()
    acc[...] = acc_in[pl.ds(lo * block, rows), :]
    for k in range(mine.shape[0]):
        for ref, x in ((mine, side), (other, 1 - side)):
            part = ref.shape[1]
            put(src, pl.multiple_of(k * rows + x * part, part), ref[k])
    for move in moves:
        move.wait()

    def far(c):
        above = jnp.logical_and(c == 1, sec + shift < secs)
        below = jnp.logical_and(c == 2, sec >= shift)
        return jnp.logical_or(above, below), jnp.where(c == 1, 0, 0 if merged else rows)

    for g, (l, r) in enumerate(((left, right), (left_pair, right_pair))):
        n = pack(cls_ref.at[g], far, order, offsets)
        add_terms(n, order, offsets, src, l, r, lo, acc, tbuf)

    cross = jnp.zeros((8, cols), F32)
    square = jnp.zeros((8, cols), F32)
    for s in range(count):
        sector = core * half + lo + s
        here = pl.ds(s * block, block)
        total = masked(acc[here, :], rows_ref[sector])
        acc[here, :] = total
        value = sector_rows(live, sector, block)[...]
        fold = lambda v: jnp.sum(v.reshape(block // 8, 8, cols), axis=0)
        cross += fold(value * total)
        square += fold(value * value)
    fold = lambda v: sum(v[:, i : i + 128] for i in range(0, cols, 128))
    cross, square = fold(cross), fold(square)
    if chained:
        cross, square = cross + sums_in[0:8, :], square + sums_in[8:16, :]
    sums[0:8, :] = cross
    sums[8:16, :] = square


def final_kernel(sides, block, sums, live, *refs):
    totals, (applied, correction, buf, sem) = refs[:-4], refs[-4:]
    core, _, _ = place()
    half = live.shape[0] // 2
    chunks = len(totals) // 2
    rows = totals[0].shape[0]
    places = []
    moves = []
    for i, total in enumerate(totals):
        c = core if i < chunks else 1 - core
        places.append(pl.ds(pl.multiple_of(c * half + i % chunks * rows, rows), rows))
        moves.append(pltpu.make_async_copy(total, applied.at[places[i], :], sem.at[0, i]))
        moves[-1].start()
    rayleigh = jnp.sum(sums[0:8, :]) / (jnp.sum(sums[8:16, :]) * (1.0 / sides))
    for i, total in enumerate(totals):
        buf[i] = total[...] - rayleigh * live[places[i], :]
        moves.append(pltpu.make_async_copy(buf.at[i], correction.at[places[i], :], sem.at[1, i]))
        moves[-1].start()
    for move in moves:
        move.wait()


def params(limit):
    return pltpu.CompilerParams(vmem_limit_bytes=limit * 2**20)


def cost(flops, moved):
    return pl.CostEstimate(flops=int(flops), bytes_accessed=int(moved), transcendentals=0)


def shape(*dims):
    return jax.ShapeDtypeStruct(dims, F32)


def swap(array, axis, bit):
    pairs = [(i, i ^ bit) for i in range(lax.axis_size(axis))]
    return lax.ppermute(array, axis, pairs)


def after(array, *others):
    return lax.optimization_barrier((array, *others))[0]


def local(wavefunction, left_blocks, right_blocks, block_rows, term_charge):
    sector_count = block_rows.shape[0]
    block = left_blocks.shape[2]
    terms = left_blocks.shape[1]
    cols = wavefunction.shape[1]
    secs, mpos, reps = (lax.axis_size(a) for a in ("sec", "mpo", "rep"))
    half = sector_count // 2
    part = half // 2
    shift = QD // sector_count
    merged = secs <= 2 * shift
    whole = wavefunction
    if reps > 1:
        whole = lax.all_gather(wavefunction, "rep", axis=1, tiled=True)
    wide = whole.shape[1]

    up = [(i, i - shift) for i in range(shift, secs)]
    down = [(i, i + shift) for i in range(secs - shift)]

    def far(array):
        if merged:
            return lax.ppermute(array, "sec", up + down)[None]
        return jnp.stack([lax.ppermute(array, "sec", p) for p in (up, down)])

    halo_pairs = []
    for m in range(mpos):
        for z in range(secs):
            to = z + 1 if m % 2 == 0 else z - 1
            if 0 <= to < secs:
                halo_pairs.append((z * mpos + m, to * mpos + m))

    rows = part * block
    blocks = shape(half, terms, block, block)
    mine_a, mine_b, halo, left_send = pl.pallas_call(
        functools.partial(prepare_kernel, half),
        out_shape=(shape(block, wide),) * 3 + (blocks,),
        in_specs=[ANY] * 3,
        out_specs=(VMEM,) * 4,
        scratch_shapes=[pltpu.SMEM((sector_count,), jnp.int32), pltpu.SemaphoreType.DMA((5,))],
        compiler_params=params(58),
        cost_estimate=cost(1, 1),
        name="prepare",
    )(block_rows, whole, left_blocks)
    far_a = far(mine_a)
    halo = lax.ppermute(halo, ("sec", "mpo"), halo_pairs)
    right_pair = swap(right_blocks, "mpo", 1)
    left_pair = swap(left_send, "mpo", 1)
    cls_pair = swap(term_charge, "mpo", 1)
    far_b = far(after(mine_b, halo))

    lists = [pltpu.SMEM((terms,), jnp.int32)] * 2

    def near(own, *args):
        outs = [shape(half * block, cols), blocks, shape(terms, wide, cols)]
        specs = [ANY, ANY, ANY] + ([ANY] + [VMEM] * 3 if own else [VMEM] * 2)
        if own:
            outs += [jax.ShapeDtypeStruct(((half + 2) * block, 3 * wide), BF16), shape(sector_count * block, cols)]
        return pl.pallas_call(
            functools.partial(near_kernel, own),
            out_shape=tuple(outs),
            in_specs=specs,
            out_specs=(VMEM,) * len(outs),
            scratch_shapes=([pltpu.SMEM((sector_count,), jnp.int32)] if own else [])
            + [pltpu.VMEM((half, 2 * GROUP * block, cols), BF16), pltpu.SMEM((terms,), jnp.int32)]
            + lists
            + [pltpu.SemaphoreType.DMA((2, terms + 1))],
            compiler_params=params(OWN_VMEM if own else PAIR_VMEM),
            cost_estimate=cost(1, 1),
            name="own_near" if own else "pair_near",
        )(*args)

    def add_far(lo, far, acc, sums):
        extra = () if sums is None else (sums,)
        return pl.pallas_call(
            functools.partial(far_kernel, lo, shift, secs, sums is not None),
            out_shape=(shape(rows, cols), shape(16, 128)),
            in_specs=[ANY] * 3 + [VMEM] * (8 + len(extra)),
            out_specs=(VMEM, VMEM),
            scratch_shapes=[
                pltpu.VMEM((far[0].shape[0] * rows, 3 * wide), BF16),
                pltpu.VMEM((part, 2 * GROUP * block, cols), BF16),
                pltpu.SMEM((sector_count,), jnp.int32),
                pltpu.SMEM((2, terms), jnp.int32),
                *lists,
                pltpu.SemaphoreType.DMA((3,)),
            ],
            compiler_params=params(32),
            cost_estimate=cost(1, 1),
            name="far",
        )(term_charge, cls_pair, block_rows, left, right, left_pair, right_pair, live, *far, acc, *extra)

    acc, left, right, src, live = near(
        True, term_charge, left_blocks, right_blocks, block_rows, whole, wavefunction, halo
    )
    other_a = swap(after(far_a, acc), "mpo", 2)
    acc, left_pair, right_pair = near(False, cls_pair, left_pair, right_pair, src, acc)
    other_b = swap(after(far_b, acc), "mpo", 2)
    part_a, sums = add_far(0, (far_a, other_a), acc, None)
    recv_a = swap(part_a, "mpo", 2)
    part_b, sums = add_far(part, (far_b, other_b), acc, sums)
    recv_b = swap(part_b, "mpo", 2)

    turned = [lax.ppermute(sums, "sec", [(i, (i + by) % secs) for i in range(secs)]) for by in range(1, min(secs, 4))]
    sums = sum(turned, sums) if secs <= 4 else lax.psum(sums, "sec")
    if reps > 1:
        sums = lax.psum(sums, "rep")
    sums = sums + swap(sums, "mpo", 2)
    sums = sums + swap(sums, "mpo", 1)
    totals = [part_a + recv_a, part_b + after(recv_b, sums)]
    totals += [swap(total, "mpo", 1) for total in totals]

    out = shape(sector_count * block, cols)
    return pl.pallas_call(
        functools.partial(final_kernel, mpos // 2, block),
        out_shape=(out, out),
        in_specs=[VMEM] * (2 + len(totals)),
        out_specs=(ANY, ANY),
        scratch_shapes=[
            pltpu.VMEM((len(totals), rows, cols), F32),
            pltpu.SemaphoreType.DMA((2, len(totals))),
        ],
        compiler_params=params(32),
        cost_estimate=cost(1, 1),
        name="residual",
    )(sums, live, *totals)


def solution(mesh):
    in_specs = (
        P(("runs", "sec"), "rep"),
        P(("runs", "sec"), "mpo", None, None),
        P(("runs", "mpo"), None, "rep"),
        P(("runs", "sec")),
        P("mpo"),
    )
    out_specs = (P(("runs", "sec"), "rep"), P(("runs", "sec"), "rep"))
    return jax.shard_map(local, mesh=mesh, in_specs=in_specs, out_specs=out_specs, check_vma=False)
```

profile of v0, /device:TPU:0, one launch (start us, length us, event | category | flops | bytes accessed | tf_op | source)
XLA Modules:
  0.0 55.3 jit_solution(6817170376877300239)
XLA Ops:
  0.6 0.0 copy-start.1
  0.6 0.0 copy-start
  0.6 0.0 copy-start.2
  0.7 0.5 collective-permute-start.3
  1.2 3.3 %prepare.1 = (f32[128,256]{1,0:T(8,128)}, f32[128,256]{1,0:T(8,128)}, f32[128,256]{1,0:T(8,128)}, f32[4,8,128,128]{3,2,1,0:T(8,128)}) custom-call(s32[8]{0:T(128)} %refs_2_.5, f32[1024,256]{1,0:T(8,128)} %refs_5_.1, f32[8,8,128,128]{3,2,1,0:T(8,128)} %refs_1_.1), custom_call_target="tpu_custom_call" | custom-call | flops 1 | bytes 1 | tf_op jit(solution)/shard_map/prepare/pallas_call | solution.py:326
  4.5 0.1 collective-permute-start.2
  4.6 4.9 %collective-permute-start.1 = (f32[128,256]{1,0:T(8,128)}, f32[128,256]{1,0:T(8,128)S(1)}, u32[]{:S(2)}, u32[]{:S(2)}) collective-permute-start(f32[128,256]{1,0:T(8,128)} %get-tuple-element.22), channel_id=1, source_target_pairs={{0,4},{4,8},{8,12},{5,1},{9,5},{13,9},{2,6},{6,10},{10,14},{7,3},{... | collective-permute-start | bytes 393224 | tf_op jit(solution)/shard_map/ppermute | solution.py:337
  9.6 2.7 %collective-permute-start.6 = (f32[128,256]{1,0:T(8,128)}, f32[128,256]{1,0:T(8,128)S(1)}, u32[]{:S(2)}, u32[]{:S(2)}) collective-permute-start(f32[128,256]{1,0:T(8,128)} %get-tuple-element.35), channel_id=1, source_target_pairs={{8,0},{12,4},{0,8},{4,12},{9,1},{13,5},{1,9},{5,13},{10,2},{14,6},... | collective-permute-start | bytes 393224 | tf_op jit(solution)/shard_map/ppermute | solution.py:314
  12.2 1.2 %collective-permute-done.1.refs_6_ = f32[128,256]{1,0:T(8,128)S(1)} collective-permute-done((f32[128,256]{1,0:T(8,128)}, f32[128,256]{1,0:T(8,128)S(1)}, u32[]{:S(2)}, u32[]{:S(2)}) %collective-permute-start.1) | collective-permute-done | bytes 131104 | tf_op jit(solution)/shard_map/ppermute | solution.py:337
  13.4 7.7 %collective-permute-start.4 = (f32[128,256]{1,0:T(8,128)}, f32[128,256]{1,0:T(8,128)S(1)}, u32[]{:S(2)}, u32[]{:S(2)}) collective-permute-start(f32[128,256]{1,0:T(8,128)} %get-tuple-element.32), channel_id=1, source_target_pairs={{8,0},{12,4},{0,8},{4,12},{9,1},{13,5},{1,9},{5,13},{10,2},{14,6},... | collective-permute-start | bytes 393224 | tf_op jit(solution)/shard_map/ppermute | solution.py:314
  21.1 0.0 copy-done.2
  21.1 0.0 collective-permute-start
  21.1 0.0 copy-done.1
  21.1 0.0 copy-done
  21.1 4.1 %own_near.1 = (f32[512,256]{1,0:T(8,128)S(1)}, f32[4,8,128,128]{3,2,1,0:T(8,128)S(1)}, f32[8,256,256]{2,1,0:T(8,128)S(1)}, bf16[768,768]{1,0:T(8,128)(2,1)S(1)}, f32[1024,256]{1,0:T(8,128)S(1)}) custom-call(s32[8]{0:T(128)S(1)} %copy-done.2, f32[8,8,128,128]{3,2,1,0:T(8,128)} %refs_1_.1, f32[8,256,256]{2,1,0:T(8,128)} %refs_2_.3, s32[8]{0:T(128)S(1)} %copy-done.1, ...), custom_call_target="tpu_custom_call" | custom-call | flops 1 | bytes 1 | tf_op jit(solution)/shard_map/own_near/pallas_call | solution.py:350
  25.2 0.0 collective-permute-done.6
  25.3 1.6 %collective-permute-start.7 = (f32[1,128,256]{2,1,0:T(8,128)S(1)}, f32[1,128,256]{2,1,0:T(8,128)S(1)}, u32[]{:S(2)}, u32[]{:S(2)}) collective-permute-start(f32[1,128,256]{2,1,0:T(8,128)S(1)} %bitcast.4), channel_id=1, source_target_pairs={{0,2},{1,3},{2,0},{3,1},{4,6},{5,7},{6,4},{7,5},{8,10},{9,11},{10,... | collective-permute-start | bytes 393224 | tf_op jit(solution)/shard_map/ppermute | solution.py:287
  26.9 0.0 collective-permute-done.refs_0_.refs_1_
  26.9 0.0 collective-permute-done.3.refs_2_
  26.9 0.0 collective-permute-done.2.refs_1_
  26.9 5.0 %pair_near.1 = (f32[512,256]{1,0:T(8,128)S(1)}, f32[4,8,128,128]{3,2,1,0:T(8,128)S(1)}, f32[8,256,256]{2,1,0:T(8,128)S(1)}) custom-call(s32[8]{0:T(128)S(1)} %collective-permute-done.refs_0_.refs_1_, f32[4,8,128,128]{3,2,1,0:T(8,128)S(1)} %collective-permute-done.2.refs_1_, f32[8,256,256]{2,1,0:T(8,128)S(1)} %collective-permute-done.3.refs_2_, ...), custom_call_target="tpu_custom_call" | custom-call | flops 1 | bytes 1 | tf_op jit(solution)/shard_map/pair_near/pallas_call | solution.py:350
  31.9 0.0 collective-permute-done.4
  31.9 0.5 collective-permute-start.5
  32.4 0.0 collective-permute-done.7.refs_9_
  32.4 2.0 %far.2 = (f32[256,256]{1,0:T(8,128)S(1)}, f32[16,128]{1,0:T(8,128)S(1)}) custom-call(s32[8]{0:T(128)S(1)} %copy-done.2, s32[8]{0:T(128)S(1)} %collective-permute-done.refs_0_.refs_1_, s32[8]{0:T(128)S(1)} %copy-done.1, f32[4,8,128,128]{3,2,1,0:T(8,128)S(1)} %get-tuple-element.23.refs_3_, f32[8,256,256]{2,1,0:T(8,128)S(1)} %get-tuple-element.24.refs_4_, ...), custom_call_target="tpu_custom_call" | custom-call | flops 1 | bytes 1 | tf_op jit(solution)/shard_map/far/pallas_call | solution.py:366
  34.5 2.3 %collective-permute-start.13 = (f32[256,256]{1,0:T(8,128)S(1)}, f32[256,256]{1,0:T(8,128)S(1)}, u32[]{:S(2)}, u32[]{:S(2)}) collective-permute-start(f32[256,256]{1,0:T(8,128)S(1)} %get-tuple-element.39), channel_id=1, source_target_pairs={{0,2},{1,3},{2,0},{3,1},{4,6},{5,7},{6,4},{7,5},{8,10},{9,11},{10,... | collective-permute-start | bytes 786440 | tf_op jit(solution)/shard_map/ppermute | solution.py:287
  36.8 0.7 %collective-permute-done.5.refs_9_ = f32[1,128,256]{2,1,0:T(8,128)S(1)} collective-permute-done((f32[1,128,256]{2,1,0:T(8,128)S(1)}, f32[1,128,256]{2,1,0:T(8,128)S(1)}, u32[]{:S(2)}, u32[]{:S(2)}) %collective-permute-start.5) | collective-permute-done | bytes 131104 | tf_op jit(solution)/shard_map/ppermute | solution.py:287
  37.4 2.0 %far.3 = (f32[256,256]{1,0:T(8,128)S(1)}, f32[16,128]{1,0:T(8,128)S(1)}) custom-call(s32[8]{0:T(128)S(1)} %copy-done.2, s32[8]{0:T(128)S(1)} %collective-permute-done.refs_0_.refs_1_, s32[8]{0:T(128)S(1)} %copy-done.1, f32[4,8,128,128]{3,2,1,0:T(8,128)S(1)} %get-tuple-element.23.refs_3_, f32[8,256,256]{2,1,0:T(8,128)S(1)} %get-tuple-element.24.refs_4_, ...), custom_call_target="tpu_custom_call" | custom-call | flops 1 | bytes 1 | tf_op jit(solution)/shard_map/far/pallas_call | solution.py:366
  39.5 1.4 %collective-permute-start.14 = (f32[256,256]{1,0:T(8,128)S(1)}, f32[256,256]{1,0:T(8,128)S(1)}, u32[]{:S(2)}, u32[]{:S(2)}) collective-permute-start(f32[256,256]{1,0:T(8,128)S(1)} %get-tuple-element.40), channel_id=1, source_target_pairs={{0,2},{1,3},{2,0},{3,1},{4,6},{5,7},{6,4},{7,5},{8,10},{9,11},{10,... | collective-permute-start | bytes 786440 | tf_op jit(solution)/shard_map/ppermute | solution.py:287
  40.9 0.0 collective-permute-start.10
  40.9 0.0 collective-permute-start.9
  40.9 2.0 %collective-permute-start.8 = (f32[16,128]{1,0:T(8,128)S(1)}, f32[16,128]{1,0:T(8,128)S(1)}, u32[]{:S(2)}, u32[]{:S(2)}) collective-permute-start(f32[16,128]{1,0:T(8,128)S(1)} %get-tuple-element.38), channel_id=1, source_target_pairs={{0,4},{4,8},{8,12},{12,0},{1,5},{5,9},{9,13},{13,1},{2,6},{6,10},{... | collective-permute-start | bytes 24584 | tf_op jit(solution)/shard_map/ppermute | solution.py:395
  43.0 1.6 %collective-permute-done.10 = f32[16,128]{1,0:T(8,128)S(1)} collective-permute-done((f32[16,128]{1,0:T(8,128)S(1)}, f32[16,128]{1,0:T(8,128)S(1)}, u32[]{:S(2)}, u32[]{:S(2)}) %collective-permute-start.10) | collective-permute-done | bytes 8224 | tf_op jit(solution)/shard_map/ppermute | solution.py:395
  44.6 0.9 %collective-permute-done.9 = f32[16,128]{1,0:T(8,128)S(1)} collective-permute-done((f32[16,128]{1,0:T(8,128)S(1)}, f32[16,128]{1,0:T(8,128)S(1)}, u32[]{:S(2)}, u32[]{:S(2)}) %collective-permute-start.9) | collective-permute-done | bytes 8224 | tf_op jit(solution)/shard_map/ppermute | solution.py:395
  45.5 1.5 %collective-permute-done.8 = f32[16,128]{1,0:T(8,128)S(1)} collective-permute-done((f32[16,128]{1,0:T(8,128)S(1)}, f32[16,128]{1,0:T(8,128)S(1)}, u32[]{:S(2)}, u32[]{:S(2)}) %collective-permute-start.8) | collective-permute-done | bytes 8224 | tf_op jit(solution)/shard_map/ppermute | solution.py:395
  47.0 1.2 %collective-permute-start.11 = (f32[16,128]{1,0:T(8,128)S(1)}, f32[16,128]{1,0:T(8,128)S(1)}, u32[]{:S(2)}, u32[]{:S(2)}) collective-permute-start(f32[16,128]{1,0:T(8,128)S(1)} %add_add_fusion), channel_id=1, source_target_pairs={{0,2},{1,3},{2,0},{3,1},{4,6},{5,7},{6,4},{7,5},{8,10},{9,11},{10,... | collective-permute-start | bytes 24584 | tf_op jit(solution)/shard_map/ppermute | solution.py:287
  48.3 2.4 %collective-permute-done.11 = f32[16,128]{1,0:T(8,128)S(1)} collective-permute-done((f32[16,128]{1,0:T(8,128)S(1)}, f32[16,128]{1,0:T(8,128)S(1)}, u32[]{:S(2)}, u32[]{:S(2)}) %collective-permute-start.11) | collective-permute-done | bytes 8224 | tf_op jit(solution)/shard_map/ppermute | solution.py:287
  50.7 0.0 collective-permute-start.12
  50.7 1.2 %collective-permute-done.12 = f32[16,128]{1,0:T(8,128)S(1)} collective-permute-done((f32[16,128]{1,0:T(8,128)S(1)}, f32[16,128]{1,0:T(8,128)S(1)}, u32[]{:S(2)}, u32[]{:S(2)}) %collective-permute-start.12) | collective-permute-done | bytes 8224 | tf_op jit(solution)/shard_map/ppermute | solution.py:287
  51.9 0.0 collective-permute-done.13
  51.9 0.2 collective-permute-start.15
  52.1 0.0 collective-permute-done.14
  52.2 0.4 collective-permute-start.16
  52.6 0.9 %collective-permute-done.15.refs_2_ = f32[256,256]{1,0:T(8,128)S(1)} collective-permute-done((f32[256,256]{1,0:T(8,128)S(1)}, f32[256,256]{1,0:T(8,128)S(1)}, u32[]{:S(2)}, u32[]{:S(2)}) %collective-permute-start.15) | collective-permute-done | bytes 262176 | tf_op jit(solution)/shard_map/ppermute | solution.py:287
  53.5 0.4 collective-permute-done.16.refs_3_
  53.9 1.4 %residual.1 = (f32[1024,256]{1,0:T(8,128)}, f32[1024,256]{1,0:T(8,128)}) custom-call(f32[16,128]{1,0:T(8,128)S(1)} %add.25.sums, f32[1024,256]{1,0:T(8,128)S(1)} %get-tuple-element.30.refs_7_.live, f32[256,256]{1,0:T(8,128)S(1)} %add.26.refs_0_, f32[256,256]{1,0:T(8,128)S(1)} %add.27.refs_1_, f32[256,256]{1,0:T(8,128)S(1)} %collective-permute-done.15.refs_2_, ...), custom_call_target="tpu_custom_call" | custom-call | flops 1 | bytes 1 | tf_op jit(solution)/shard_map/residual/pallas_call | solution.py:405
  (5 shorter events, 0.1 us)
Async XLA Ops:
  0.6 20.4 %copy-start.1 = (s32[8]{0:T(128)S(1)}, s32[8]{0:T(128)}, u32[]{:S(2)}) copy-start(s32[8]{0:T(128)} %refs_2_.5) | copy-start | bytes 100
  0.6 20.4 %copy-start = (f32[1024,256]{1,0:T(8,128)S(1)}, f32[1024,256]{1,0:T(8,128)}, u32[]{:S(2)}) copy-start(f32[1024,256]{1,0:T(8,128)} %refs_5_.1) | copy-start | bytes 3145732
  0.6 20.4 %copy-start.2 = (s32[8]{0:T(128)S(1)}, s32[8]{0:T(128)}, u32[]{:S(2)}) copy-start(s32[8]{0:T(128)} %refs_0_.5) | copy-start | bytes 100
  0.7 26.2 %collective-permute-start.3 = (f32[8,256,256]{2,1,0:T(8,128)}, f32[8,256,256]{2,1,0:T(8,128)S(1)}, u32[]{:S(2)}, u32[]{:S(2)}) collective-permute-start(f32[8,256,256]{2,1,0:T(8,128)} %refs_2_.3), channel_id=1, source_target_pairs={{0,1},{1,0},{2,3},{3,2},{4,5},{5,4},{6,7},{7,6},{8,9},{9,8},{10,11... | collective-permute-start | bytes 6291464 | tf_op jit(solution)/shard_map/ppermute | solution.py:287
  4.5 22.4 %collective-permute-start.2 = (f32[4,8,128,128]{3,2,1,0:T(8,128)}, f32[4,8,128,128]{3,2,1,0:T(8,128)S(1)}, u32[]{:S(2)}, u32[]{:S(2)}) collective-permute-start(f32[4,8,128,128]{3,2,1,0:T(8,128)} %get-tuple-element.25), channel_id=1, source_target_pairs={{0,1},{1,0},{2,3},{3,2},{4,5},{5,4},{6,7},{7,6},{8,9},{9,8},{10,11... | collective-permute-start | bytes 6291464 | tf_op jit(solution)/shard_map/ppermute | solution.py:287
  4.6 8.8 %collective-permute-start.1 = (f32[128,256]{1,0:T(8,128)}, f32[128,256]{1,0:T(8,128)S(1)}, u32[]{:S(2)}, u32[]{:S(2)}) collective-permute-start(f32[128,256]{1,0:T(8,128)} %get-tuple-element.22), channel_id=1, source_target_pairs={{0,4},{4,8},{8,12},{5,1},{9,5},{13,9},{2,6},{6,10},{10,14},{7,3},{... | collective-permute-start | bytes 393224 | tf_op jit(solution)/shard_map/ppermute | solution.py:337
  9.6 15.7 %collective-permute-start.6 = (f32[128,256]{1,0:T(8,128)}, f32[128,256]{1,0:T(8,128)S(1)}, u32[]{:S(2)}, u32[]{:S(2)}) collective-permute-start(f32[128,256]{1,0:T(8,128)} %get-tuple-element.35), channel_id=1, source_target_pairs={{8,0},{12,4},{0,8},{4,12},{9,1},{13,5},{1,9},{5,13},{10,2},{14,6},... | collective-permute-start | bytes 393224 | tf_op jit(solution)/shard_map/ppermute | solution.py:314
  13.4 18.5 %collective-permute-start.4 = (f32[128,256]{1,0:T(8,128)}, f32[128,256]{1,0:T(8,128)S(1)}, u32[]{:S(2)}, u32[]{:S(2)}) collective-permute-start(f32[128,256]{1,0:T(8,128)} %get-tuple-element.32), channel_id=1, source_target_pairs={{8,0},{12,4},{0,8},{4,12},{9,1},{13,5},{1,9},{5,13},{10,2},{14,6},... | collective-permute-start | bytes 393224 | tf_op jit(solution)/shard_map/ppermute | solution.py:314
  21.1 5.8 %collective-permute-start = (s32[8]{0:T(128)S(1)}, s32[8]{0:T(128)S(1)}, u32[]{:S(2)}, u32[]{:S(2)}) collective-permute-start(s32[8]{0:T(128)S(1)} %copy-done.2), channel_id=1, source_target_pairs={{0,1},{1,0},{2,3},{3,2},{4,5},{5,4},{6,7},{7,6},{8,9},{9,8},{10,11... | collective-permute-start | bytes 104 | tf_op jit(solution)/shard_map/ppermute | solution.py:287
  25.3 7.2 %collective-permute-start.7 = (f32[1,128,256]{2,1,0:T(8,128)S(1)}, f32[1,128,256]{2,1,0:T(8,128)S(1)}, u32[]{:S(2)}, u32[]{:S(2)}) collective-permute-start(f32[1,128,256]{2,1,0:T(8,128)S(1)} %bitcast.4), channel_id=1, source_target_pairs={{0,2},{1,3},{2,0},{3,1},{4,6},{5,7},{6,4},{7,5},{8,10},{9,11},{10,... | collective-permute-start | bytes 393224 | tf_op jit(solution)/shard_map/ppermute | solution.py:287
  31.9 5.5 %collective-permute-start.5 = (f32[1,128,256]{2,1,0:T(8,128)S(1)}, f32[1,128,256]{2,1,0:T(8,128)S(1)}, u32[]{:S(2)}, u32[]{:S(2)}) collective-permute-start(f32[1,128,256]{2,1,0:T(8,128)S(1)} %bitcast.2), channel_id=1, source_target_pairs={{0,2},{1,3},{2,0},{3,1},{4,6},{5,7},{6,4},{7,5},{8,10},{9,11},{10,... | collective-permute-start | bytes 393224 | tf_op jit(solution)/shard_map/ppermute | solution.py:287
  34.5 17.4 %collective-permute-start.13 = (f32[256,256]{1,0:T(8,128)S(1)}, f32[256,256]{1,0:T(8,128)S(1)}, u32[]{:S(2)}, u32[]{:S(2)}) collective-permute-start(f32[256,256]{1,0:T(8,128)S(1)} %get-tuple-element.39), channel_id=1, source_target_pairs={{0,2},{1,3},{2,0},{3,1},{4,6},{5,7},{6,4},{7,5},{8,10},{9,11},{10,... | collective-permute-start | bytes 786440 | tf_op jit(solution)/shard_map/ppermute | solution.py:287
  39.5 12.6 %collective-permute-start.14 = (f32[256,256]{1,0:T(8,128)S(1)}, f32[256,256]{1,0:T(8,128)S(1)}, u32[]{:S(2)}, u32[]{:S(2)}) collective-permute-start(f32[256,256]{1,0:T(8,128)S(1)} %get-tuple-element.40), channel_id=1, source_target_pairs={{0,2},{1,3},{2,0},{3,1},{4,6},{5,7},{6,4},{7,5},{8,10},{9,11},{10,... | collective-permute-start | bytes 786440 | tf_op jit(solution)/shard_map/ppermute | solution.py:287
  40.9 3.7 %collective-permute-start.10 = (f32[16,128]{1,0:T(8,128)S(1)}, f32[16,128]{1,0:T(8,128)S(1)}, u32[]{:S(2)}, u32[]{:S(2)}) collective-permute-start(f32[16,128]{1,0:T(8,128)S(1)} %get-tuple-element.38), channel_id=1, source_target_pairs={{0,12},{4,0},{8,4},{12,8},{1,13},{5,1},{9,5},{13,9},{2,14},{6,2},{... | collective-permute-start | bytes 24584 | tf_op jit(solution)/shard_map/ppermute | solution.py:395
  40.9 4.5 %collective-permute-start.9 = (f32[16,128]{1,0:T(8,128)S(1)}, f32[16,128]{1,0:T(8,128)S(1)}, u32[]{:S(2)}, u32[]{:S(2)}) collective-permute-start(f32[16,128]{1,0:T(8,128)S(1)} %get-tuple-element.38), channel_id=1, source_target_pairs={{0,8},{4,12},{8,0},{12,4},{1,9},{5,13},{9,1},{13,5},{2,10},{6,14},... | collective-permute-start | bytes 24584 | tf_op jit(solution)/shard_map/ppermute | solution.py:395
  40.9 6.1 %collective-permute-start.8 = (f32[16,128]{1,0:T(8,128)S(1)}, f32[16,128]{1,0:T(8,128)S(1)}, u32[]{:S(2)}, u32[]{:S(2)}) collective-permute-start(f32[16,128]{1,0:T(8,128)S(1)} %get-tuple-element.38), channel_id=1, source_target_pairs={{0,4},{4,8},{8,12},{12,0},{1,5},{5,9},{9,13},{13,1},{2,6},{6,10},{... | collective-permute-start | bytes 24584 | tf_op jit(solution)/shard_map/ppermute | solution.py:395
  47.0 3.7 %collective-permute-start.11 = (f32[16,128]{1,0:T(8,128)S(1)}, f32[16,128]{1,0:T(8,128)S(1)}, u32[]{:S(2)}, u32[]{:S(2)}) collective-permute-start(f32[16,128]{1,0:T(8,128)S(1)} %add_add_fusion), channel_id=1, source_target_pairs={{0,2},{1,3},{2,0},{3,1},{4,6},{5,7},{6,4},{7,5},{8,10},{9,11},{10,... | collective-permute-start | bytes 24584 | tf_op jit(solution)/shard_map/ppermute | solution.py:287
  50.7 1.2 %collective-permute-start.12 = (f32[16,128]{1,0:T(8,128)S(1)}, f32[16,128]{1,0:T(8,128)S(1)}, u32[]{:S(2)}, u32[]{:S(2)}) collective-permute-start(f32[16,128]{1,0:T(8,128)S(1)} %add.24), channel_id=1, source_target_pairs={{0,1},{1,0},{2,3},{3,2},{4,5},{5,4},{6,7},{7,6},{8,9},{9,8},{10,11... | collective-permute-start | bytes 24584 | tf_op jit(solution)/shard_map/ppermute | solution.py:287
  51.9 1.6 %collective-permute-start.15 = (f32[256,256]{1,0:T(8,128)S(1)}, f32[256,256]{1,0:T(8,128)S(1)}, u32[]{:S(2)}, u32[]{:S(2)}) collective-permute-start(f32[256,256]{1,0:T(8,128)S(1)} %add.26.refs_0_), channel_id=1, source_target_pairs={{0,1},{1,0},{2,3},{3,2},{4,5},{5,4},{6,7},{7,6},{8,9},{9,8},{10,11... | collective-permute-start | bytes 786440 | tf_op jit(solution)/shard_map/ppermute | solution.py:287
  52.2 1.7 %collective-permute-start.16 = (f32[256,256]{1,0:T(8,128)S(1)}, f32[256,256]{1,0:T(8,128)S(1)}, u32[]{:S(2)}, u32[]{:S(2)}) collective-permute-start(f32[256,256]{1,0:T(8,128)S(1)} %add.27.refs_1_), channel_id=1, source_target_pairs={{0,1},{1,0},{2,3},{3,2},{4,5},{5,4},{6,7},{7,6},{8,9},{9,8},{10,11... | collective-permute-start | bytes 786440 | tf_op jit(solution)/shard_map/ppermute | solution.py:287
where the time goes:
time: 56 us; the launch traced here: 55.3 us
  starting transfers between devices  25.7 us (46%)
  Pallas kernels  17.9 us (32%)
  waiting for transfers between devices  10.8 us (19%)
  between operations  0.76 us (1%)
    ppermute x2, starting transfers between devices, far(): return lax.ppermute(array, 'sec', up + down)[None]  10.3 us
    pallas_call x2, Pallas kernels, near(): pl.pallas_call(functools.partial(near_kernel, own), out_shape=tuple(outs)...  9.13 us
    ppermute x11, starting transfers between devices, swap(): return lax.ppermute(array, axis, pairs)  8.4 us
    ppermute x11, waiting for transfers between devices, swap(): return lax.ppermute(array, axis, pairs)  5.56 us
    ppermute x1, starting transfers between devices, local(): halo = lax.ppermute(halo, ('sec', 'mpo'), halo_pairs)  4.92 us
    pallas_call x2, Pallas kernels, add_far(): pl.pallas_call(functools.partial(far_kernel, lo, shift, secs, sums is not...  4.09 us
    ppermute x3, waiting for transfers between devices, local(): lax.ppermute(sums, 'sec', [(i, (i + by) % secs) for i in range(secs)])  4.07 us
    pallas_call x1, Pallas kernels, local(): pl.pallas_call(functools.partial(prepare_kernel, half), out_shape=(shape(...  3.32 us
  transfers between devices with their start and end apart: 17, of which 9 were waited for; matrix products, arithmetic and copies ran while one was open for 0% of the time, Pallas kernels for 30%

commit v1 on v0

--- a/solution.py
+++ b/solution.py
@@ -26,7 +26,7 @@
     return jnp.where(index < live, rows, 0.0)
 
 
-OWN_VMEM, PAIR_VMEM = 46, 32
+PREPARE_VMEM, OWN_VMEM, PAIR_VMEM = 46, 46, 32
 GROUP = 2
 
 
@@ -39,27 +39,29 @@
     return wave.at[pl.ds(pl.multiple_of(sector * block, block), block), :]
 
 
-def prepare_kernel(half, rows_hbm, wave, left, mine_a, mine_b, halo, left_send, rows_ref, sem):
+def prepare_kernel(half, rows_hbm, whole, wave, left, mine_a, mine_b, halo, left_send, src, live, *rest):
+    rows_ref, sem = rest
     core, side, _ = place()
     block = halo.shape[0]
-    count = rows_ref.shape[0]
-    part = half // 2
-    wanted = (
-        (core * half + side, mine_a),
-        ((1 - core) * (count - 1), halo),
-        (core * half + part + side, mine_b),
-    )
-    moves = [pltpu.make_async_copy(rows_hbm, rows_ref, sem.at[0])]
-    for i, (sector, ref) in enumerate(wanted):
-        moves.append(pltpu.make_async_copy(sector_rows(wave, sector, block), ref, sem.at[i + 1]))
-    moves.append(pltpu.make_async_copy(left.at[pl.ds((1 - core) * half, half)], left_send, sem.at[4]))
-    for move in moves:
-        move.start()
-    moves[0].wait()
-    for move, (sector, ref) in zip(moves[1:], wanted):
-        move.wait()
-        ref[...] = masked(ref[...], rows_ref[sector])
-    moves[-1].wait()
+    rows = pltpu.make_async_copy(rows_hbm, rows_ref, sem.at[0])
+    rows.start()
+    send = pltpu.make_async_copy(left.at[pl.ds((1 - core) * half, half)], left_send, sem.at[1])
+    send.start()
+    src[pl.ds(pl.multiple_of(core * (half + 1) * block, block), block), :] = jnp.zeros((block, src.shape[1]), BF16)
+    rows.wait()
+
+    def source(sector):
+        return masked(sector_rows(whole, sector, block)[...], rows_ref[sector])
+
+    mine_a[...] = source(core * half + side)
+    mine_b[...] = source(core * half + half // 2 + side)
+    halo[...] = source((1 - core) * (2 * half - 1))
+    for s in range(2 * half):
+        here = pl.ds(s * block, block)
+        live[here, :] = masked(wave[here, :], rows_ref[s])
+    for i in range(half + 1):
+        put(src, pl.multiple_of((i + 1 - core) * block, block), source(core * (half - 1) + i))
+    send.wait()
 
 
 def put(src, at, value):
@@ -125,19 +127,19 @@
 
 def near_kernel(own, *refs):
     if own:
-        cls, left_hbm, right_hbm, rows_hbm, whole, wave, halo, acc, left, right, src, live, *rest = refs
-        rows_ref = rest.pop(0)
+        cls, left_hbm, right_hbm, src, acc, left, right, *rest = refs
     else:
-        cls, left_hbm, right_hbm, src, acc_in, acc, left, right, *rest = refs
+        cls, left_hbm, right_hbm, cls_own, left_own, right_own, halo, src_in, acc_in, acc, left, right, *rest = refs
+        src, *rest = rest
     tbuf, cls_ref, order, offsets, sem = rest
     half, terms, block, _ = left.shape
     core, _, _ = place()
 
-    fetch_cls = pltpu.make_async_copy(cls, cls_ref, sem.at[0, terms])
-    fetch_cls.start()
-    if own:
-        fetch_rows = pltpu.make_async_copy(rows_hbm, rows_ref, sem.at[1, terms])
-        fetch_rows.start()
+    fetch_cls = [pltpu.make_async_copy(cls, cls_ref.at[0], sem.at[0, terms])]
+    if not own:
+        fetch_cls.append(pltpu.make_async_copy(cls_own, cls_ref.at[1], sem.at[1, terms]))
+    for move in fetch_cls:
+        move.start()
     first = core * half if own else 0
 
     def fetch(t):
@@ -150,32 +152,15 @@
         for move in fetch(t):
             move.start()
 
+    halo_at = pl.multiple_of(core * (half + 1) * block, block)
     if own:
         acc[...] = jnp.zeros_like(acc)
-        fetch_rows.wait()
-        count = rows_ref.shape[0]
-        for s in range(count):
-            here = pl.ds(s * block, block)
-            live[here, :] = masked(wave[here, :], rows_ref[s])
-        for i in range(half + 2):
-            sector = core * half - 1 + i
-            inside = jnp.logical_and(sector >= 0, sector < count)
-            at = i * block
-            if 0 < i < half + 1:
-                put(src, at, masked(sector_rows(whole, sector, block)[...], rows_ref[sector]))
-                continue
-
-            @pl.when(inside)
-            def _(sector=sector, at=at):
-                put(src, at, masked(sector_rows(whole, sector, block)[...], rows_ref[sector]))
-
-            @pl.when(jnp.logical_not(inside))
-            def _(at=at):
-                put(src, at, halo[...])
     else:
         acc[...] = acc_in[...]
-
-    fetch_cls.wait()
+        src[...] = src_in[...]
+        put(src, halo_at, halo[...])
+    for move in fetch_cls:
+        move.wait()
 
     def near(c):
         at = jnp.where(c == 0, block, jnp.where(c == 3, 2 * block, 0))
@@ -185,11 +170,16 @@
         for move in fetch(t):
             move.wait()
 
-    n = pack(cls_ref, near, order, offsets)
+    if not own:
+        edge = core * (half - 1)
+        n = pack(cls_ref.at[1], lambda c: (c == 4 - core, halo_at), order, offsets)
+        part = acc.at[pl.ds(pl.multiple_of(edge * block, block), block), :]
+        add_terms(n, order, offsets, src, left_own, right_own, edge, part, tbuf)
+    n = pack(cls_ref.at[0], near, order, offsets)
     add_terms(n, order, offsets, src, left, right, 0, acc, tbuf, ready=wait)
     for t in range(terms):
 
-        @pl.when(jnp.logical_not(near(cls_ref[t])[0]))
+        @pl.when(jnp.logical_not(near(cls_ref[0, t])[0]))
         def _(t=t):
             wait(t)
 
@@ -287,6 +277,10 @@
     return lax.ppermute(array, axis, pairs)
 
 
+def everyone(array, axis):
+    return (array + swap(array, axis, 1)) + (swap(array, axis, 2) + swap(array, axis, 3))
+
+
 def after(array, *others):
     return lax.optimization_barrier((array, *others))[0]
 
@@ -323,37 +317,36 @@
 
     rows = part * block
     blocks = shape(half, terms, block, block)
-    mine_a, mine_b, halo, left_send = pl.pallas_call(
+    source_shape = ((half + 2) * block, 3 * wide)
+    mine_a, mine_b, halo, left_send, src, live = pl.pallas_call(
         functools.partial(prepare_kernel, half),
-        out_shape=(shape(block, wide),) * 3 + (blocks,),
-        in_specs=[ANY] * 3,
-        out_specs=(VMEM,) * 4,
-        scratch_shapes=[pltpu.SMEM((sector_count,), jnp.int32), pltpu.SemaphoreType.DMA((5,))],
-        compiler_params=params(58),
+        out_shape=(shape(block, wide),) * 3
+        + (blocks, jax.ShapeDtypeStruct(source_shape, BF16), shape(sector_count * block, cols)),
+        in_specs=[ANY, VMEM, VMEM, ANY],
+        out_specs=(VMEM,) * 6,
+        scratch_shapes=[pltpu.SMEM((sector_count,), jnp.int32), pltpu.SemaphoreType.DMA((2,))],
+        compiler_params=params(PREPARE_VMEM),
         cost_estimate=cost(1, 1),
         name="prepare",
-    )(block_rows, whole, left_blocks)
+    )(block_rows, whole, wavefunction, left_blocks)
     far_a = far(mine_a)
     halo = lax.ppermute(halo, ("sec", "mpo"), halo_pairs)
     right_pair = swap(right_blocks, "mpo", 1)
+    cls_pair = swap(term_charge, "mpo", 1)
     left_pair = swap(left_send, "mpo", 1)
-    cls_pair = swap(term_charge, "mpo", 1)
-    far_b = far(after(mine_b, halo))
+    far_b = far(after(mine_b, right_pair, cls_pair))
 
     lists = [pltpu.SMEM((terms,), jnp.int32)] * 2
 
     def near(own, *args):
         outs = [shape(half * block, cols), blocks, shape(terms, wide, cols)]
-        specs = [ANY, ANY, ANY] + ([ANY] + [VMEM] * 3 if own else [VMEM] * 2)
-        if own:
-            outs += [jax.ShapeDtypeStruct(((half + 2) * block, 3 * wide), BF16), shape(sector_count * block, cols)]
         return pl.pallas_call(
             functools.partial(near_kernel, own),
             out_shape=tuple(outs),
-            in_specs=specs,
+            in_specs=[ANY] * 3 + ([VMEM] if own else [ANY] + [VMEM] * 5),
             out_specs=(VMEM,) * len(outs),
-            scratch_shapes=([pltpu.SMEM((sector_count,), jnp.int32)] if own else [])
-            + [pltpu.VMEM((half, 2 * GROUP * block, cols), BF16), pltpu.SMEM((terms,), jnp.int32)]
+            scratch_shapes=([] if own else [pltpu.VMEM(source_shape, BF16)])
+            + [pltpu.VMEM((half, 2 * GROUP * block, cols), BF16), pltpu.SMEM((2, terms), jnp.int32)]
             + lists
             + [pltpu.SemaphoreType.DMA((2, terms + 1))],
             compiler_params=params(OWN_VMEM if own else PAIR_VMEM),
@@ -381,23 +374,24 @@
             name="far",
         )(term_charge, cls_pair, block_rows, left, right, left_pair, right_pair, live, *far, acc, *extra)
 
-    acc, left, right, src, live = near(
-        True, term_charge, left_blocks, right_blocks, block_rows, whole, wavefunction, halo
+    acc, left, right = near(True, term_charge, left_blocks, right_blocks, src)
+    other_a = swap(after(far_a, acc), "mpo", 2)
+    acc, left_pair, right_pair = near(
+        False, cls_pair, left_pair, right_pair, term_charge, left, right, halo, src, acc
     )
-    other_a = swap(after(far_a, acc), "mpo", 2)
-    acc, left_pair, right_pair = near(False, cls_pair, left_pair, right_pair, src, acc)
     other_b = swap(after(far_b, acc), "mpo", 2)
     part_a, sums = add_far(0, (far_a, other_a), acc, None)
     recv_a = swap(part_a, "mpo", 2)
     part_b, sums = add_far(part, (far_b, other_b), acc, sums)
     recv_b = swap(part_b, "mpo", 2)
 
-    turned = [lax.ppermute(sums, "sec", [(i, (i + by) % secs) for i in range(secs)]) for by in range(1, min(secs, 4))]
-    sums = sum(turned, sums) if secs <= 4 else lax.psum(sums, "sec")
+    if secs == 4:
+        sums = everyone(sums, "sec")
+    else:
+        sums = lax.psum(sums, "sec")
     if reps > 1:
         sums = lax.psum(sums, "rep")
-    sums = sums + swap(sums, "mpo", 2)
-    sums = sums + swap(sums, "mpo", 1)
+    sums = everyone(sums, "mpo")
     totals = [part_a + recv_a, part_b + after(recv_b, sums)]
     totals += [swap(total, "mpo", 1) for total in totals]
 

time: 56 us -> 49.2 us (0.88); the launches traced: 55.3 us -> 49.3 us
  starting transfers between devices: 25.7 us -> 21 us
  waiting for transfers between devices: 10.8 us -> 7.24 us
  local copies, waits for them, and re-layouts: 0.01 us -> 1.89 us
    ppermute x2, starting transfers between devices: 10.3 us -> 4.43 us  [far(): return lax.ppermute(array, 'sec', up + down)[None]]
    ppermute x11 -> x15, starting transfers between devices: 8.4 us -> 13.1 us  [swap(): return lax.ppermute(array, axis, pairs)]
    ppermute x3 -> x0, waiting for transfers between devices: 4.07 us -> none  [local(): lax.ppermute(sums, 'sec', [(i, (i + by) % secs) for i in range(secs)])]
    ppermute x3 -> x0, starting transfers between devices: 2.03 us -> none  [local(): lax.ppermute(sums, 'sec', [(i, (i + by) % secs) for i in range(secs)])]
    pallas_call x2, Pallas kernels: 9.13 us -> 11 us  [near(): pl.pallas_call(functools.partial(near_kernel, own), out_shape=tuple(outs)...]
    unnamed x6 -> x10, local copies, waits for them, and re-layouts: 0.01 us -> 1.89 us
    ppermute x11 -> x15, waiting for transfers between devices: 5.56 us -> 7.23 us  [swap(): return lax.ppermute(array, axis, pairs)]
    pallas_call x1, Pallas kernels: 3.32 us -> 1.76 us  [local(): pl.pallas_call(functools.partial(prepare_kernel, half), out_shape=(shape(...]
  transfers between devices with their start and end apart: 17 -> 18, of which waited for: 9 -> 6; matrix products, arithmetic and copies ran while one was open for 0% -> 0% of each run, Pallas kernels for 30% -> 34%
where the time goes in v1:
time: 49.2 us; the launch traced here: 49.3 us
  starting transfers between devices  21 us (43%)
  Pallas kernels  18.2 us (37%)
  waiting for transfers between devices  7.24 us (15%)
  local copies, waits for them, and re-layouts  1.89 us (4%)
  between operations  0.8 us (2%)
    ppermute x15, starting transfers between devices, swap(): return lax.ppermute(array, axis, pairs)  13.1 us
    pallas_call x2, Pallas kernels, near(): pl.pallas_call(functools.partial(near_kernel, own), out_shape=tuple(outs)...  11 us
    ppermute x15, waiting for transfers between devices, swap(): return lax.ppermute(array, axis, pairs)  7.23 us
    ppermute x2, starting transfers between devices, far(): return lax.ppermute(array, 'sec', up + down)[None]  4.43 us
    pallas_call x2, Pallas kernels, add_far(): pl.pallas_call(functools.partial(far_kernel, lo, shift, secs, sums is not...  4.07 us
    ppermute x1, starting transfers between devices, local(): halo = lax.ppermute(halo, ('sec', 'mpo'), halo_pairs)  3.48 us
    unnamed x10, local copies, waits for them, and re-layouts  1.89 us
    pallas_call x1, Pallas kernels, local(): pl.pallas_call(functools.partial(prepare_kernel, half), out_shape=(shape(...  1.76 us
  transfers between devices with their start and end apart: 18, of which 6 were waited for; matrix products, arithmetic and copies ran while one was open for 0% of the time, Pallas kernels for 34%

profile of v1, /device:TPU:0, one launch (start us, length us, event | category | flops | bytes accessed | tf_op | source)
XLA Modules:
  0.0 49.3 jit_solution(11836059053487006831)
XLA Ops:
  0.6 0.5 %collective-permute-start.2 = (f32[8,256,256]{2,1,0:T(8,128)}, f32[8,256,256]{2,1,0:T(8,128)S(1)}, u32[]{:S(2)}, u32[]{:S(2)}) collective-permute-start(f32[8,256,256]{2,1,0:T(8,128)} %refs_2_.3), channel_id=1, source_target_pairs={{0,1},{1,0},{2,3},{3,2},{4,5},{5,4},{6,7},{7,6},{8,9},{9,8},{10,11... | collective-permute-start | bytes 6291464 | tf_op jit(solution)/shard_map/ppermute | solution.py:277
  1.1 0.0 copy-start
  1.1 1.2 %copy-done = f32[1024,256]{1,0:T(8,128)S(1)} copy-done((f32[1024,256]{1,0:T(8,128)S(1)}, f32[1024,256]{1,0:T(8,128)}, u32[]{:S(2)}) %copy-start) | copy-done | bytes 1048600
  2.4 0.7 %copy-done.3 = s32[8]{0:T(128)S(1)} copy-done((s32[8]{0:T(128)S(1)}, s32[8]{0:T(128)}, u32[]{:S(2)}) %copy-start.3) | copy-done | bytes 56
  3.0 1.8 %prepare.1 = (f32[128,256]{1,0:T(8,128)S(1)}, f32[128,256]{1,0:T(8,128)S(1)}, f32[128,256]{1,0:T(8,128)S(1)}, f32[4,8,128,128]{3,2,1,0:T(8,128)S(1)}, bf16[768,7...) custom-call(s32[8]{0:T(128)S(1)} %copy-done.3, f32[1024,256]{1,0:T(8,128)S(1)} %copy-done, f32[1024,256]{1,0:T(8,128)S(1)} %copy-done, ...), custom_call_target="tpu_custom_call" | custom-call | flops 1 | bytes 1 | tf_op jit(solution)/shard_map/prepare/pallas_call | solution.py:321
  4.8 0.1 collective-permute-start.1
  4.9 4.0 %collective-permute-start.6 = (f32[128,256]{1,0:T(8,128)S(1)}, f32[128,256]{1,0:T(8,128)S(1)}, u32[]{:S(2)}, u32[]{:S(2)}) collective-permute-start(f32[128,256]{1,0:T(8,128)S(1)} %get-tuple-element.35), channel_id=1, source_target_pairs={{8,0},{12,4},{0,8},{4,12},{9,1},{13,5},{1,9},{5,13},{10,2},{14,6},... | collective-permute-start | bytes 393224 | tf_op jit(solution)/shard_map/ppermute | solution.py:308
  9.0 0.0 copy-done.2
  9.0 0.0 collective-permute-start
  9.0 3.5 %collective-permute-start.3 = (f32[128,256]{1,0:T(8,128)S(1)}, f32[128,256]{1,0:T(8,128)S(1)}, u32[]{:S(2)}, u32[]{:S(2)}) collective-permute-start(f32[128,256]{1,0:T(8,128)S(1)} %get-tuple-element.26), channel_id=1, source_target_pairs={{0,4},{4,8},{8,12},{5,1},{9,5},{13,9},{2,6},{6,10},{10,14},{7,3},{... | collective-permute-start | bytes 393224 | tf_op jit(solution)/shard_map/ppermute | solution.py:333
  12.4 0.0 collective-permute-done.refs_0_.refs_1_
  12.5 0.0 collective-permute-done.2.refs_2_
  12.5 0.4 collective-permute-start.4
  12.9 0.0 copy-done.1
  12.9 4.0 %own_near.1 = (f32[512,256]{1,0:T(8,128)S(1)}, f32[4,8,128,128]{3,2,1,0:T(8,128)S(1)}, f32[8,256,256]{2,1,0:T(8,128)S(1)}) custom-call(s32[8]{0:T(128)S(1)} %copy-done.2, f32[8,8,128,128]{3,2,1,0:T(8,128)} %refs_1_.1, f32[8,256,256]{2,1,0:T(8,128)S(1)} %copy-done.1, bf16[768,768]{1,0:T(8,128)(2,1)S(1)} %get-tuple-element.22.refs_3_.refs_7_), custom_call_target="tpu_custom_call" | custom-call | flops 1 | bytes 1 | tf_op jit(solution)/shard_map/own_near/pallas_call | solution.py:343
  16.9 0.0 collective-permute-done.6
  16.9 1.5 %collective-permute-start.7 = (f32[1,128,256]{2,1,0:T(8,128)S(1)}, f32[1,128,256]{2,1,0:T(8,128)S(1)}, u32[]{:S(2)}, u32[]{:S(2)}) collective-permute-start(f32[1,128,256]{2,1,0:T(8,128)S(1)} %bitcast.2), channel_id=1, source_target_pairs={{0,2},{1,3},{2,0},{3,1},{4,6},{5,7},{6,4},{7,5},{8,10},{9,11},{10,... | collective-permute-start | bytes 393224 | tf_op jit(solution)/shard_map/ppermute | solution.py:277
  18.4 0.0 collective-permute-done.3.refs_6_
  18.4 0.0 collective-permute-done.1.refs_1_
  18.4 7.0 %pair_near.1 = (f32[512,256]{1,0:T(8,128)S(1)}, f32[4,8,128,128]{3,2,1,0:T(8,128)S(1)}, f32[8,256,256]{2,1,0:T(8,128)S(1)}) custom-call(s32[8]{0:T(128)S(1)} %collective-permute-done.refs_0_.refs_1_, f32[4,8,128,128]{3,2,1,0:T(8,128)S(1)} %collective-permute-done.1.refs_1_, f32[8,256,256]{2,1,0:T(8,128)S(1)} %collective-permute-done.2.refs_2_, ...), custom_call_target="tpu_custom_call" | custom-call | flops 1 | bytes 1 | tf_op jit(solution)/shard_map/pair_near/pallas_call | solution.py:343
  25.4 0.0 collective-permute-done.4
  25.4 0.1 collective-permute-start.5
  25.5 0.0 collective-permute-done.7.refs_9_
  25.5 0.0 copy-done.4
  25.5 2.0 %far.2 = (f32[256,256]{1,0:T(8,128)S(1)}, f32[16,128]{1,0:T(8,128)S(1)}) custom-call(s32[8]{0:T(128)S(1)} %copy-done.2, s32[8]{0:T(128)S(1)} %collective-permute-done.refs_0_.refs_1_, s32[8]{0:T(128)S(1)} %copy-done.4, f32[4,8,128,128]{3,2,1,0:T(8,128)S(1)} %get-tuple-element.23.refs_4_.refs_3_, f32[8,256,256]{2,1,0:T(8,128)S(1)} %get-tuple-element.24.refs_5_.refs_4_, ...), custom_call_target="tpu_custom_call" | custom-call | flops 1 | bytes 1 | tf_op jit(solution)/shard_map/far/pallas_call | solution.py:359
  27.6 2.7 %collective-permute-start.14 = (f32[256,256]{1,0:T(8,128)S(1)}, f32[256,256]{1,0:T(8,128)S(1)}, u32[]{:S(2)}, u32[]{:S(2)}) collective-permute-start(f32[256,256]{1,0:T(8,128)S(1)} %get-tuple-element.39), channel_id=1, source_target_pairs={{0,2},{1,3},{2,0},{3,1},{4,6},{5,7},{6,4},{7,5},{8,10},{9,11},{10,... | collective-permute-start | bytes 786440 | tf_op jit(solution)/shard_map/ppermute | solution.py:277
  30.3 0.7 %collective-permute-done.5.refs_9_ = f32[1,128,256]{2,1,0:T(8,128)S(1)} collective-permute-done((f32[1,128,256]{2,1,0:T(8,128)S(1)}, f32[1,128,256]{2,1,0:T(8,128)S(1)}, u32[]{:S(2)}, u32[]{:S(2)}) %collective-permute-start.5) | collective-permute-done | bytes 131104 | tf_op jit(solution)/shard_map/ppermute | solution.py:277
  31.0 2.0 %far.3 = (f32[256,256]{1,0:T(8,128)S(1)}, f32[16,128]{1,0:T(8,128)S(1)}) custom-call(s32[8]{0:T(128)S(1)} %copy-done.2, s32[8]{0:T(128)S(1)} %collective-permute-done.refs_0_.refs_1_, s32[8]{0:T(128)S(1)} %copy-done.4, f32[4,8,128,128]{3,2,1,0:T(8,128)S(1)} %get-tuple-element.23.refs_4_.refs_3_, f32[8,256,256]{2,1,0:T(8,128)S(1)} %get-tuple-element.24.refs_5_.refs_4_, ...), custom_call_target="tpu_custom_call" | custom-call | flops 1 | bytes 1 | tf_op jit(solution)/shard_map/far/pallas_call | solution.py:359
  33.0 2.6 %collective-permute-start.10 = (f32[16,128]{1,0:T(8,128)S(1)}, f32[16,128]{1,0:T(8,128)S(1)}, u32[]{:S(2)}, u32[]{:S(2)}) collective-permute-start(f32[16,128]{1,0:T(8,128)S(1)} %get-tuple-element.38), channel_id=1, source_target_pairs={{0,12},{4,8},{8,4},{12,0},{1,13},{5,9},{9,5},{13,1},{2,14},{6,10},... | collective-permute-start | bytes 24584 | tf_op jit(solution)/shard_map/ppermute | solution.py:277
  35.6 3.2 %collective-permute-start.9 = (f32[16,128]{1,0:T(8,128)S(1)}, f32[16,128]{1,0:T(8,128)S(1)}, u32[]{:S(2)}, u32[]{:S(2)}) collective-permute-start(f32[16,128]{1,0:T(8,128)S(1)} %get-tuple-element.38), channel_id=1, source_target_pairs={{0,8},{4,12},{8,0},{12,4},{1,9},{5,13},{9,1},{13,5},{2,10},{6,14},... | collective-permute-start | bytes 24584 | tf_op jit(solution)/shard_map/ppermute | solution.py:277
  38.8 0.1 collective-permute-start.8
  38.9 0.3 collective-permute-start.15
  39.2 0.0 collective-permute-done.10
  39.2 1.3 %collective-permute-done.9 = f32[16,128]{1,0:T(8,128)S(1)} collective-permute-done((f32[16,128]{1,0:T(8,128)S(1)}, f32[16,128]{1,0:T(8,128)S(1)}, u32[]{:S(2)}, u32[]{:S(2)}) %collective-permute-start.9) | collective-permute-done | bytes 8224 | tf_op jit(solution)/shard_map/ppermute | solution.py:277
  40.6 1.9 %collective-permute-done.8 = f32[16,128]{1,0:T(8,128)S(1)} collective-permute-done((f32[16,128]{1,0:T(8,128)S(1)}, f32[16,128]{1,0:T(8,128)S(1)}, u32[]{:S(2)}, u32[]{:S(2)}) %collective-permute-start.8) | collective-permute-done | bytes 8224 | tf_op jit(solution)/shard_map/ppermute | solution.py:277
  42.5 0.0 collective-permute-start.13
  42.5 0.4 collective-permute-start.12
  42.9 1.4 %collective-permute-start.11 = (f32[16,128]{1,0:T(8,128)S(1)}, f32[16,128]{1,0:T(8,128)S(1)}, u32[]{:S(2)}, u32[]{:S(2)}) collective-permute-start(f32[16,128]{1,0:T(8,128)S(1)} %add_add_fusion.1), channel_id=1, source_target_pairs={{0,1},{1,0},{2,3},{3,2},{4,5},{5,4},{6,7},{7,6},{8,9},{9,8},{10,11... | collective-permute-start | bytes 24584 | tf_op jit(solution)/shard_map/ppermute | solution.py:277
  44.4 0.0 collective-permute-done.14
  44.4 0.1 collective-permute-start.16
  44.5 1.1 %collective-permute-done.13 = f32[16,128]{1,0:T(8,128)S(1)} collective-permute-done((f32[16,128]{1,0:T(8,128)S(1)}, f32[16,128]{1,0:T(8,128)S(1)}, u32[]{:S(2)}, u32[]{:S(2)}) %collective-permute-start.13) | collective-permute-done | bytes 8224 | tf_op jit(solution)/shard_map/ppermute | solution.py:277
  45.6 0.7 %collective-permute-done.12 = f32[16,128]{1,0:T(8,128)S(1)} collective-permute-done((f32[16,128]{1,0:T(8,128)S(1)}, f32[16,128]{1,0:T(8,128)S(1)}, u32[]{:S(2)}, u32[]{:S(2)}) %collective-permute-start.12) | collective-permute-done | bytes 8224 | tf_op jit(solution)/shard_map/ppermute | solution.py:277
  46.2 0.0 collective-permute-done.11
  46.3 0.0 collective-permute-done.15
  46.3 0.1 collective-permute-start.17
  46.4 0.0 collective-permute-done.16.refs_2_
  46.4 1.5 %collective-permute-done.17.refs_3_ = f32[256,256]{1,0:T(8,128)S(1)} collective-permute-done((f32[256,256]{1,0:T(8,128)S(1)}, f32[256,256]{1,0:T(8,128)S(1)}, u32[]{:S(2)}, u32[]{:S(2)}) %collective-permute-start.17) | collective-permute-done | bytes 262176 | tf_op jit(solution)/shard_map/ppermute | solution.py:277
  47.9 1.4 %residual.1 = (f32[1024,256]{1,0:T(8,128)}, f32[1024,256]{1,0:T(8,128)}) custom-call(f32[16,128]{1,0:T(8,128)S(1)} %add_add_fusion.sums, f32[1024,256]{1,0:T(8,128)S(1)} %get-tuple-element.30.refs_7_.live, f32[256,256]{1,0:T(8,128)S(1)} %add.30.refs_0_, f32[256,256]{1,0:T(8,128)S(1)} %add.31.refs_1_, f32[256,256]{1,0:T(8,128)S(1)} %collective-permute-done.16.refs_2_, ...), custom_call_target="tpu_custom_call" | custom-call | flops 1 | bytes 1 | tf_op jit(solution)/shard_map/residual/pallas_call | solution.py:399
  (8 shorter events, 0.1 us)
Async XLA Ops:
  0.6 11.8 %collective-permute-start.2 = (f32[8,256,256]{2,1,0:T(8,128)}, f32[8,256,256]{2,1,0:T(8,128)S(1)}, u32[]{:S(2)}, u32[]{:S(2)}) collective-permute-start(f32[8,256,256]{2,1,0:T(8,128)} %refs_2_.3), channel_id=1, source_target_pairs={{0,1},{1,0},{2,3},{3,2},{4,5},{5,4},{6,7},{7,6},{8,9},{9,8},{10,11... | collective-permute-start | bytes 6291464 | tf_op jit(solution)/shard_map/ppermute | solution.py:277
  1.1 1.2 %copy-start = (f32[1024,256]{1,0:T(8,128)S(1)}, f32[1024,256]{1,0:T(8,128)}, u32[]{:S(2)}) copy-start(f32[1024,256]{1,0:T(8,128)} %wave.1) | copy-start | bytes 3145732
  2.4 0.7 %copy-start.3 = (s32[8]{0:T(128)S(1)}, s32[8]{0:T(128)}, u32[]{:S(2)}) copy-start(s32[8]{0:T(128)} %refs_2_.5) | copy-start | bytes 100
  3.0 5.9 %copy-start.2 = (s32[8]{0:T(128)S(1)}, s32[8]{0:T(128)}, u32[]{:S(2)}) copy-start(s32[8]{0:T(128)} %refs_0_.5) | copy-start | bytes 100
  3.0 9.8 %copy-start.1 = (f32[8,256,256]{2,1,0:T(8,128)S(1)}, f32[8,256,256]{2,1,0:T(8,128)}, u32[]{:S(2)}) copy-start(f32[8,256,256]{2,1,0:T(8,128)} %refs_2_.3) | copy-start | bytes 6291460
  4.8 13.6 %collective-permute-start.1 = (f32[4,8,128,128]{3,2,1,0:T(8,128)S(1)}, f32[4,8,128,128]{3,2,1,0:T(8,128)S(1)}, u32[]{:S(2)}, u32[]{:S(2)}) collective-permute-start(f32[4,8,128,128]{3,2,1,0:T(8,128)S(1)} %get-tuple-element.25), channel_id=1, source_target_pairs={{0,1},{1,0},{2,3},{3,2},{4,5},{5,4},{6,7},{7,6},{8,9},{9,8},{10,11... | collective-permute-start | bytes 6291464 | tf_op jit(solution)/shard_map/ppermute | solution.py:277
  4.9 12.0 %collective-permute-start.6 = (f32[128,256]{1,0:T(8,128)S(1)}, f32[128,256]{1,0:T(8,128)S(1)}, u32[]{:S(2)}, u32[]{:S(2)}) collective-permute-start(f32[128,256]{1,0:T(8,128)S(1)} %get-tuple-element.35), channel_id=1, source_target_pairs={{8,0},{12,4},{0,8},{4,12},{9,1},{13,5},{1,9},{5,13},{10,2},{14,6},... | collective-permute-start | bytes 393224 | tf_op jit(solution)/shard_map/ppermute | solution.py:308
  9.0 3.5 %collective-permute-start = (s32[8]{0:T(128)S(1)}, s32[8]{0:T(128)S(1)}, u32[]{:S(2)}, u32[]{:S(2)}) collective-permute-start(s32[8]{0:T(128)S(1)} %copy-done.2), channel_id=1, source_target_pairs={{0,1},{1,0},{2,3},{3,2},{4,5},{5,4},{6,7},{7,6},{8,9},{9,8},{10,11... | collective-permute-start | bytes 104 | tf_op jit(solution)/shard_map/ppermute | solution.py:277
  9.0 9.4 %collective-permute-start.3 = (f32[128,256]{1,0:T(8,128)S(1)}, f32[128,256]{1,0:T(8,128)S(1)}, u32[]{:S(2)}, u32[]{:S(2)}) collective-permute-start(f32[128,256]{1,0:T(8,128)S(1)} %get-tuple-element.26), channel_id=1, source_target_pairs={{0,4},{4,8},{8,12},{5,1},{9,5},{13,9},{2,6},{6,10},{10,14},{7,3},{... | collective-permute-start | bytes 393224 | tf_op jit(solution)/shard_map/ppermute | solution.py:333
  12.5 12.9 %collective-permute-start.4 = (f32[128,256]{1,0:T(8,128)S(1)}, f32[128,256]{1,0:T(8,128)S(1)}, u32[]{:S(2)}, u32[]{:S(2)}) collective-permute-start(f32[128,256]{1,0:T(8,128)S(1)} %get-tuple-element.32), channel_id=1, source_target_pairs={{8,0},{12,4},{0,8},{4,12},{9,1},{13,5},{1,9},{5,13},{10,2},{14,6},... | collective-permute-start | bytes 393224 | tf_op jit(solution)/shard_map/ppermute | solution.py:308
  16.9 8.6 %collective-permute-start.7 = (f32[1,128,256]{2,1,0:T(8,128)S(1)}, f32[1,128,256]{2,1,0:T(8,128)S(1)}, u32[]{:S(2)}, u32[]{:S(2)}) collective-permute-start(f32[1,128,256]{2,1,0:T(8,128)S(1)} %bitcast.2), channel_id=1, source_target_pairs={{0,2},{1,3},{2,0},{3,1},{4,6},{5,7},{6,4},{7,5},{8,10},{9,11},{10,... | collective-permute-start | bytes 393224 | tf_op jit(solution)/shard_map/ppermute | solution.py:277
  18.4 7.1 %copy-start.4 = (s32[8]{0:T(128)S(1)}, s32[8]{0:T(128)}, u32[]{:S(2)}) copy-start(s32[8]{0:T(128)} %refs_2_.5) | copy-start | bytes 100
  25.4 5.5 %collective-permute-start.5 = (f32[1,128,256]{2,1,0:T(8,128)S(1)}, f32[1,128,256]{2,1,0:T(8,128)S(1)}, u32[]{:S(2)}, u32[]{:S(2)}) collective-permute-start(f32[1,128,256]{2,1,0:T(8,128)S(1)} %bitcast.4), channel_id=1, source_target_pairs={{0,2},{1,3},{2,0},{3,1},{4,6},{5,7},{6,4},{7,5},{8,10},{9,11},{10,... | collective-permute-start | bytes 393224 | tf_op jit(solution)/shard_map/ppermute | solution.py:277
  27.6 16.8 %collective-permute-start.14 = (f32[256,256]{1,0:T(8,128)S(1)}, f32[256,256]{1,0:T(8,128)S(1)}, u32[]{:S(2)}, u32[]{:S(2)}) collective-permute-start(f32[256,256]{1,0:T(8,128)S(1)} %get-tuple-element.39), channel_id=1, source_target_pairs={{0,2},{1,3},{2,0},{3,1},{4,6},{5,7},{6,4},{7,5},{8,10},{9,11},{10,... | collective-permute-start | bytes 786440 | tf_op jit(solution)/shard_map/ppermute | solution.py:277
  33.0 6.2 %collective-permute-start.10 = (f32[16,128]{1,0:T(8,128)S(1)}, f32[16,128]{1,0:T(8,128)S(1)}, u32[]{:S(2)}, u32[]{:S(2)}) collective-permute-start(f32[16,128]{1,0:T(8,128)S(1)} %get-tuple-element.38), channel_id=1, source_target_pairs={{0,12},{4,8},{8,4},{12,0},{1,13},{5,9},{9,5},{13,1},{2,14},{6,10},... | collective-permute-start | bytes 24584 | tf_op jit(solution)/shard_map/ppermute | solution.py:277
  35.6 4.9 %collective-permute-start.9 = (f32[16,128]{1,0:T(8,128)S(1)}, f32[16,128]{1,0:T(8,128)S(1)}, u32[]{:S(2)}, u32[]{:S(2)}) collective-permute-start(f32[16,128]{1,0:T(8,128)S(1)} %get-tuple-element.38), channel_id=1, source_target_pairs={{0,8},{4,12},{8,0},{12,4},{1,9},{5,13},{9,1},{13,5},{2,10},{6,14},... | collective-permute-start | bytes 24584 | tf_op jit(solution)/shard_map/ppermute | solution.py:277
  38.8 3.7 %collective-permute-start.8 = (f32[16,128]{1,0:T(8,128)S(1)}, f32[16,128]{1,0:T(8,128)S(1)}, u32[]{:S(2)}, u32[]{:S(2)}) collective-permute-start(f32[16,128]{1,0:T(8,128)S(1)} %get-tuple-element.38), channel_id=1, source_target_pairs={{0,4},{4,0},{8,12},{12,8},{1,5},{5,1},{9,13},{13,9},{2,6},{6,2},{1... | collective-permute-start | bytes 24584 | tf_op jit(solution)/shard_map/ppermute | solution.py:277
  38.9 7.3 %collective-permute-start.15 = (f32[256,256]{1,0:T(8,128)S(1)}, f32[256,256]{1,0:T(8,128)S(1)}, u32[]{:S(2)}, u32[]{:S(2)}) collective-permute-start(f32[256,256]{1,0:T(8,128)S(1)} %get-tuple-element.40), channel_id=1, source_target_pairs={{0,2},{1,3},{2,0},{3,1},{4,6},{5,7},{6,4},{7,5},{8,10},{9,11},{10,... | collective-permute-start | bytes 786440 | tf_op jit(solution)/shard_map/ppermute | solution.py:277
  42.5 3.1 %collective-permute-start.13 = (f32[16,128]{1,0:T(8,128)S(1)}, f32[16,128]{1,0:T(8,128)S(1)}, u32[]{:S(2)}, u32[]{:S(2)}) collective-permute-start(f32[16,128]{1,0:T(8,128)S(1)} %add_add_fusion.1), channel_id=1, source_target_pairs={{0,3},{1,2},{2,1},{3,0},{4,7},{5,6},{6,5},{7,4},{8,11},{9,10},{10,... | collective-permute-start | bytes 24584 | tf_op jit(solution)/shard_map/ppermute | solution.py:277
  42.5 3.7 %collective-permute-start.12 = (f32[16,128]{1,0:T(8,128)S(1)}, f32[16,128]{1,0:T(8,128)S(1)}, u32[]{:S(2)}, u32[]{:S(2)}) collective-permute-start(f32[16,128]{1,0:T(8,128)S(1)} %add_add_fusion.1), channel_id=1, source_target_pairs={{0,2},{1,3},{2,0},{3,1},{4,6},{5,7},{6,4},{7,5},{8,10},{9,11},{10,... | collective-permute-start | bytes 24584 | tf_op jit(solution)/shard_map/ppermute | solution.py:277
  42.9 3.3 %collective-permute-start.11 = (f32[16,128]{1,0:T(8,128)S(1)}, f32[16,128]{1,0:T(8,128)S(1)}, u32[]{:S(2)}, u32[]{:S(2)}) collective-permute-start(f32[16,128]{1,0:T(8,128)S(1)} %add_add_fusion.1), channel_id=1, source_target_pairs={{0,1},{1,0},{2,3},{3,2},{4,5},{5,4},{6,7},{7,6},{8,9},{9,8},{10,11... | collective-permute-start | bytes 24584 | tf_op jit(solution)/shard_map/ppermute | solution.py:277
  44.4 2.0 %collective-permute-start.16 = (f32[256,256]{1,0:T(8,128)S(1)}, f32[256,256]{1,0:T(8,128)S(1)}, u32[]{:S(2)}, u32[]{:S(2)}) collective-permute-start(f32[256,256]{1,0:T(8,128)S(1)} %add.30.refs_0_), channel_id=1, source_target_pairs={{0,1},{1,0},{2,3},{3,2},{4,5},{5,4},{6,7},{7,6},{8,9},{9,8},{10,11... | collective-permute-start | bytes 786440 | tf_op jit(solution)/shard_map/ppermute | solution.py:277
  46.3 1.6 %collective-permute-start.17 = (f32[256,256]{1,0:T(8,128)S(1)}, f32[256,256]{1,0:T(8,128)S(1)}, u32[]{:S(2)}, u32[]{:S(2)}) collective-permute-start(f32[256,256]{1,0:T(8,128)S(1)} %add.31.refs_1_), channel_id=1, source_target_pairs={{0,1},{1,0},{2,3},{3,2},{4,5},{5,4},{6,7},{7,6},{8,9},{9,8},{10,11... | collective-permute-start | bytes 786440 | tf_op jit(solution)/shard_map/ppermute | solution.py:277

commit v2 on v1

--- a/solution.py
+++ b/solution.py
@@ -26,7 +26,7 @@
     return jnp.where(index < live, rows, 0.0)
 
 
-PREPARE_VMEM, OWN_VMEM, PAIR_VMEM = 46, 46, 32
+PREPARE_VMEM, NEAR_VMEM = 46, 32
 GROUP = 2
 
 
@@ -87,7 +87,7 @@
     return n
 
 
-def add_terms(n, order, offsets, src, left, right, first, acc, tbuf, ready=None):
+def add_terms(n, order, offsets, src, left, right, first, acc, tbuf):
     rows = acc.shape[0]
     block = left.shape[-1]
     count = rows // block
@@ -99,12 +99,6 @@
             k = jnp.minimum(i * GROUP + j, n - 1)
             real.append(i * GROUP + j < n)
             terms.append(order[k])
-            if ready is not None:
-
-                @pl.when(real[j])
-                def _(j=j):
-                    ready(terms[j])
-
             at = pl.ds(pl.multiple_of(offsets[k], block), rows)
             high, low = split(right[terms[j]])
             wide = jnp.concatenate([high, high, low], 0)
@@ -127,31 +121,19 @@
 
 def near_kernel(own, *refs):
     if own:
-        cls, left_hbm, right_hbm, src, acc, left, right, *rest = refs
+        cls, left, right, src, acc, *rest = refs
     else:
-        cls, left_hbm, right_hbm, cls_own, left_own, right_own, halo, src_in, acc_in, acc, left, right, *rest = refs
-        src, *rest = rest
+        cls, left, right, cls_own, left_own, right_own, halo, src_in, acc_in, acc, src, *rest = refs
     tbuf, cls_ref, order, offsets, sem = rest
-    half, terms, block, _ = left.shape
+    block = left.shape[-1]
+    half = acc.shape[0] // block
     core, _, _ = place()
 
-    fetch_cls = [pltpu.make_async_copy(cls, cls_ref.at[0], sem.at[0, terms])]
+    fetch = [pltpu.make_async_copy(cls, cls_ref.at[0], sem.at[0])]
     if not own:
-        fetch_cls.append(pltpu.make_async_copy(cls_own, cls_ref.at[1], sem.at[1, terms]))
-    for move in fetch_cls:
+        fetch.append(pltpu.make_async_copy(cls_own, cls_ref.at[1], sem.at[1]))
+    for move in fetch:
         move.start()
-    first = core * half if own else 0
-
-    def fetch(t):
-        return (
-            pltpu.make_async_copy(left_hbm.at[pl.ds(first, half), t], left.at[:, t], sem.at[0, t]),
-            pltpu.make_async_copy(right_hbm.at[t], right.at[t], sem.at[1, t]),
-        )
-
-    for t in range(terms):
-        for move in fetch(t):
-            move.start()
-
     halo_at = pl.multiple_of(core * (half + 1) * block, block)
     if own:
         acc[...] = jnp.zeros_like(acc)
@@ -159,29 +141,20 @@
         acc[...] = acc_in[...]
         src[...] = src_in[...]
         put(src, halo_at, halo[...])
-    for move in fetch_cls:
+    for move in fetch:
         move.wait()
 
     def near(c):
         at = jnp.where(c == 0, block, jnp.where(c == 3, 2 * block, 0))
         return jnp.logical_or(c == 0, c >= 3), at
-
-    def wait(t):
-        for move in fetch(t):
-            move.wait()
 
     if not own:
         edge = core * (half - 1)
         n = pack(cls_ref.at[1], lambda c: (c == 4 - core, halo_at), order, offsets)
         part = acc.at[pl.ds(pl.multiple_of(edge * block, block), block), :]
-        add_terms(n, order, offsets, src, left_own, right_own, edge, part, tbuf)
+        add_terms(n, order, offsets, src, left_own, right_own, core * half + edge, part, tbuf)
     n = pack(cls_ref.at[0], near, order, offsets)
-    add_terms(n, order, offsets, src, left, right, 0, acc, tbuf, ready=wait)
-    for t in range(terms):
-
-        @pl.when(jnp.logical_not(near(cls_ref[0, t])[0]))
-        def _(t=t):
-            wait(t)
+    add_terms(n, order, offsets, src, left, right, core * half if own else 0, acc, tbuf)
 
 
 def far_kernel(lo, shift, secs, chained, *refs):
@@ -190,7 +163,7 @@
     sums_in = refs.pop(11) if chained else None
     acc, sums, src, tbuf, rows_ref, cls_ref, order, offsets, sem = refs[11:]
     rows, cols = acc.shape
-    half, terms, block, _ = left.shape
+    half, _, block, _ = left_pair.shape
     count = rows // block
     core, side, sec = place()
     merged = mine.shape[0] == 1
@@ -215,9 +188,9 @@
         below = jnp.logical_and(c == 2, sec >= shift)
         return jnp.logical_or(above, below), jnp.where(c == 1, 0, 0 if merged else rows)
 
-    for g, (l, r) in enumerate(((left, right), (left_pair, right_pair))):
+    for g, (l, r, first) in enumerate(((left, right, core * half + lo), (left_pair, right_pair, lo))):
         n = pack(cls_ref.at[g], far, order, offsets)
-        add_terms(n, order, offsets, src, l, r, lo, acc, tbuf)
+        add_terms(n, order, offsets, src, l, r, first, acc, tbuf)
 
     cross = jnp.zeros((8, cols), F32)
     square = jnp.zeros((8, cols), F32)
@@ -339,17 +312,16 @@
     lists = [pltpu.SMEM((terms,), jnp.int32)] * 2
 
     def near(own, *args):
-        outs = [shape(half * block, cols), blocks, shape(terms, wide, cols)]
         return pl.pallas_call(
             functools.partial(near_kernel, own),
-            out_shape=tuple(outs),
-            in_specs=[ANY] * 3 + ([VMEM] if own else [ANY] + [VMEM] * 5),
-            out_specs=(VMEM,) * len(outs),
+            out_shape=shape(half * block, cols),
+            in_specs=[ANY] + [VMEM] * 3 if own else [ANY, VMEM, VMEM] * 2 + [VMEM] * 3,
+            out_specs=VMEM,
             scratch_shapes=([] if own else [pltpu.VMEM(source_shape, BF16)])
             + [pltpu.VMEM((half, 2 * GROUP * block, cols), BF16), pltpu.SMEM((2, terms), jnp.int32)]
             + lists
-            + [pltpu.SemaphoreType.DMA((2, terms + 1))],
-            compiler_params=params(OWN_VMEM if own else PAIR_VMEM),
+            + [pltpu.SemaphoreType.DMA((2,))],
+            compiler_params=params(NEAR_VMEM),
             cost_estimate=cost(1, 1),
             name="own_near" if own else "pair_near",
         )(*args)
@@ -372,13 +344,11 @@
             compiler_params=params(32),
             cost_estimate=cost(1, 1),
             name="far",
-        )(term_charge, cls_pair, block_rows, left, right, left_pair, right_pair, live, *far, acc, *extra)
-
-    acc, left, right = near(True, term_charge, left_blocks, right_blocks, src)
+        )(term_charge, cls_pair, block_rows, left_blocks, right_blocks, left_pair, right_pair, live, *far, acc, *extra)
+
+    acc = near(True, term_charge, left_blocks, right_blocks, src)
     other_a = swap(after(far_a, acc), "mpo", 2)
-    acc, left_pair, right_pair = near(
-        False, cls_pair, left_pair, right_pair, term_charge, left, right, halo, src, acc
-    )
+    acc = near(False, cls_pair, left_pair, right_pair, term_charge, left_blocks, right_blocks, halo, src, acc)
     other_b = swap(after(far_b, acc), "mpo", 2)
     part_a, sums = add_far(0, (far_a, other_a), acc, None)
     recv_a = swap(part_a, "mpo", 2)

time: 49.2 us -> 49.3 us (level)
  Pallas kernels: 18.2 us -> 12.5 us
  starting transfers between devices: 21 us -> 25 us
  waiting for transfers between devices: 7.24 us -> 8.46 us
    pallas_call x2, Pallas kernels: 11 us -> 6.74 us  [near(): pl.pallas_call(functools.partial(near_kernel, own), out_shape=shape(half...]
    ppermute x15, starting transfers between devices: 13.1 us -> 16.8 us  [swap(): return lax.ppermute(array, axis, pairs)]
    pallas_call x2, Pallas kernels: 4.07 us -> 2.75 us  [add_far(): pl.pallas_call(functools.partial(far_kernel, lo, shift, secs, sums is not...]
    ppermute x15, waiting for transfers between devices: 7.23 us -> 8.45 us  [swap(): return lax.ppermute(array, axis, pairs)]
  transfers between devices with their start and end apart: 18 -> 18, of which waited for: 6 -> 6; matrix products, arithmetic and copies ran while one was open for 0% -> 0% of each run, Pallas kernels for 34% -> 23%
where the time goes in v2:
time: 49.3 us; the launch traced here: 49 us
  starting transfers between devices  25 us (51%)
  Pallas kernels  12.5 us (25%)
  waiting for transfers between devices  8.46 us (17%)
  local copies, waits for them, and re-layouts  2.28 us (5%)
  between operations  0.77 us (2%)
    ppermute x15, starting transfers between devices, swap(): return lax.ppermute(array, axis, pairs)  16.8 us
    ppermute x15, waiting for transfers between devices, swap(): return lax.ppermute(array, axis, pairs)  8.45 us
    pallas_call x2, Pallas kernels, near(): pl.pallas_call(functools.partial(near_kernel, own), out_shape=shape(half...  6.74 us
    ppermute x2, starting transfers between devices, far(): return lax.ppermute(array, 'sec', up + down)[None]  4.71 us
    ppermute x1, starting transfers between devices, local(): halo = lax.ppermute(halo, ('sec', 'mpo'), halo_pairs)  3.48 us
    pallas_call x2, Pallas kernels, add_far(): pl.pallas_call(functools.partial(far_kernel, lo, shift, secs, sums is not...  2.75 us
    unnamed x10, local copies, waits for them, and re-layouts  2.28 us
    pallas_call x1, Pallas kernels, local(): pl.pallas_call(functools.partial(prepare_kernel, half), out_shape=(shape(...  1.62 us
  transfers between devices with their start and end apart: 18, of which 6 were waited for; matrix products, arithmetic and copies ran while one was open for 0% of the time, Pallas kernels for 23%

profile of v2, /device:TPU:0, one launch (start us, length us, event | category | flops | bytes accessed | tf_op | source)
XLA Modules:
  0.0 49.0 jit_solution(13444275285640499923)
XLA Ops:
  0.6 0.0 copy-start.1
  0.6 0.0 copy-start
  0.7 0.5 %collective-permute-start.2 = (f32[8,256,256]{2,1,0:T(8,128)}, f32[8,256,256]{2,1,0:T(8,128)S(1)}, u32[]{:S(2)}, u32[]{:S(2)}) collective-permute-start(f32[8,256,256]{2,1,0:T(8,128)} %refs_4_.5), channel_id=1, source_target_pairs={{0,1},{1,0},{2,3},{3,2},{4,5},{5,4},{6,7},{7,6},{8,9},{9,8},{10,11... | collective-permute-start | bytes 6291464 | tf_op jit(solution)/shard_map/ppermute | solution.py:250
  1.2 1.5 %copy-done.2 = f32[1024,256]{1,0:T(8,128)S(1)} copy-done((f32[1024,256]{1,0:T(8,128)S(1)}, f32[1024,256]{1,0:T(8,128)}, u32[]{:S(2)}) %copy-start.2) | copy-done | bytes 1048600
  2.7 0.8 %copy-done.4 = s32[8]{0:T(128)S(1)} copy-done((s32[8]{0:T(128)S(1)}, s32[8]{0:T(128)}, u32[]{:S(2)}) %copy-start.4) | copy-done | bytes 56
  3.4 1.6 %prepare.1 = (f32[128,256]{1,0:T(8,128)S(1)}, f32[128,256]{1,0:T(8,128)S(1)}, f32[128,256]{1,0:T(8,128)S(1)}, f32[4,8,128,128]{3,2,1,0:T(8,128)S(1)}, bf16[768,7...) custom-call(s32[8]{0:T(128)S(1)} %copy-done.4, f32[1024,256]{1,0:T(8,128)S(1)} %copy-done.2, f32[1024,256]{1,0:T(8,128)S(1)} %copy-done.2, ...), custom_call_target="tpu_custom_call" | custom-call | flops 1 | bytes 1 | tf_op jit(solution)/shard_map/prepare/pallas_call | solution.py:294
  5.1 0.5 %collective-permute-start.1 = (f32[4,8,128,128]{3,2,1,0:T(8,128)S(1)}, f32[4,8,128,128]{3,2,1,0:T(8,128)S(1)}, u32[]{:S(2)}, u32[]{:S(2)}) collective-permute-start(f32[4,8,128,128]{3,2,1,0:T(8,128)S(1)} %get-tuple-element.16), channel_id=1, source_target_pairs={{0,1},{1,0},{2,3},{3,2},{4,5},{5,4},{6,7},{7,6},{8,9},{9,8},{10,11... | collective-permute-start | bytes 6291464 | tf_op jit(solution)/shard_map/ppermute | solution.py:250
  5.6 3.7 %collective-permute-start.6 = (f32[128,256]{1,0:T(8,128)S(1)}, f32[128,256]{1,0:T(8,128)S(1)}, u32[]{:S(2)}, u32[]{:S(2)}) collective-permute-start(f32[128,256]{1,0:T(8,128)S(1)} %get-tuple-element.23), channel_id=1, source_target_pairs={{8,0},{12,4},{0,8},{4,12},{9,1},{13,5},{1,9},{5,13},{10,2},{14,6},... | collective-permute-start | bytes 393224 | tf_op jit(solution)/shard_map/ppermute | solution.py:281
  9.3 3.5 %collective-permute-start.4 = (f32[128,256]{1,0:T(8,128)S(1)}, f32[128,256]{1,0:T(8,128)S(1)}, u32[]{:S(2)}, u32[]{:S(2)}) collective-permute-start(f32[128,256]{1,0:T(8,128)S(1)} %get-tuple-element.20), channel_id=1, source_target_pairs={{0,4},{4,8},{8,12},{5,1},{9,5},{13,9},{2,6},{6,10},{10,14},{7,3},{... | collective-permute-start | bytes 393224 | tf_op jit(solution)/shard_map/ppermute | solution.py:306
  12.7 0.0 copy-done.3
  12.7 0.1 collective-permute-start
  12.8 1.1 %collective-permute-done.refs_0_.refs_1_ = s32[8]{0:T(128)S(1)} collective-permute-done((s32[8]{0:T(128)S(1)}, s32[8]{0:T(128)S(1)}, u32[]{:S(2)}, u32[]{:S(2)}) %collective-permute-start) | collective-permute-done | bytes 64 | tf_op jit(solution)/shard_map/ppermute | solution.py:250
  13.9 0.0 collective-permute-done.2.refs_2_.refs_6_
  13.9 1.0 %collective-permute-start.3 = (f32[128,256]{1,0:T(8,128)S(1)}, f32[128,256]{1,0:T(8,128)S(1)}, u32[]{:S(2)}, u32[]{:S(2)}) collective-permute-start(f32[128,256]{1,0:T(8,128)S(1)} %get-tuple-element.19), channel_id=1, source_target_pairs={{8,0},{12,4},{0,8},{4,12},{9,1},{13,5},{1,9},{5,13},{10,2},{14,6},... | collective-permute-start | bytes 393224 | tf_op jit(solution)/shard_map/ppermute | solution.py:281
  15.0 0.0 copy-done
  15.0 3.2 %own_near.1.refs_8_ = f32[512,256]{1,0:T(8,128)S(1)} custom-call(s32[8]{0:T(128)S(1)} %copy-done.3, f32[8,8,128,128]{3,2,1,0:T(8,128)S(1)} %copy-done, f32[8,256,256]{2,1,0:T(8,128)S(1)} %copy-done.1, bf16[768,768]{1,0:T(8,128)(2,1)S(1)} %get-tuple-element.21.refs_3_.refs_7_), custom_call_target="tpu_custom_call" | custom-call | flops 1 | bytes 1 | tf_op jit(solution)/shard_map/own_near/pallas_call | solution.py:315
  18.2 0.0 collective-permute-done.6
  18.2 1.6 %collective-permute-start.7 = (f32[1,128,256]{2,1,0:T(8,128)S(1)}, f32[1,128,256]{2,1,0:T(8,128)S(1)}, u32[]{:S(2)}, u32[]{:S(2)}) collective-permute-start(f32[1,128,256]{2,1,0:T(8,128)S(1)} %bitcast.2), channel_id=1, source_target_pairs={{0,2},{1,3},{2,0},{3,1},{4,6},{5,7},{6,4},{7,5},{8,10},{9,11},{10,... | collective-permute-start | bytes 393224 | tf_op jit(solution)/shard_map/ppermute | solution.py:250
  19.8 0.0 collective-permute-done.4.refs_6_
  19.8 0.0 collective-permute-done.1.refs_1_.refs_5_
  19.8 3.5 %pair_near.1.refs_10_ = f32[512,256]{1,0:T(8,128)S(1)} custom-call(s32[8]{0:T(128)S(1)} %collective-permute-done.refs_0_.refs_1_, f32[4,8,128,128]{3,2,1,0:T(8,128)S(1)} %collective-permute-done.1.refs_1_.refs_5_, f32[8,256,256]{2,1,0:T(8,128)S(1)} %collective-permute-done.2.refs_2_.refs_6_, s32[8]{0:T(128)S(1)} %copy-done.3, ...), custom_call_target="tpu_custom_call" | custom-call | flops 1 | bytes 1 | tf_op jit(solution)/shard_map/pair_near/pallas_call | solution.py:315
  23.3 0.0 collective-permute-done.3
  23.3 1.1 %collective-permute-start.5 = (f32[1,128,256]{2,1,0:T(8,128)S(1)}, f32[1,128,256]{2,1,0:T(8,128)S(1)}, u32[]{:S(2)}, u32[]{:S(2)}) collective-permute-start(f32[1,128,256]{2,1,0:T(8,128)S(1)} %bitcast.4), channel_id=1, source_target_pairs={{0,2},{1,3},{2,0},{3,1},{4,6},{5,7},{6,4},{7,5},{8,10},{9,11},{10,... | collective-permute-start | bytes 393224 | tf_op jit(solution)/shard_map/ppermute | solution.py:250
  24.5 0.0 collective-permute-done.7.refs_9_
  24.5 1.4 %far.2 = (f32[256,256]{1,0:T(8,128)S(1)}, f32[16,128]{1,0:T(8,128)S(1)}) custom-call(s32[8]{0:T(128)S(1)} %copy-done.3, s32[8]{0:T(128)S(1)} %collective-permute-done.refs_0_.refs_1_, s32[8]{0:T(128)S(1)} %copy-done.4, f32[8,8,128,128]{3,2,1,0:T(8,128)S(1)} %copy-done, f32[8,256,256]{2,1,0:T(8,128)S(1)} %copy-done.1, ...), custom_call_target="tpu_custom_call" | custom-call | flops 1 | bytes 1 | tf_op jit(solution)/shard_map/far/pallas_call | solution.py:331
  25.9 3.0 %collective-permute-start.14 = (f32[256,256]{1,0:T(8,128)S(1)}, f32[256,256]{1,0:T(8,128)S(1)}, u32[]{:S(2)}, u32[]{:S(2)}) collective-permute-start(f32[256,256]{1,0:T(8,128)S(1)} %get-tuple-element.27), channel_id=1, source_target_pairs={{0,2},{1,3},{2,0},{3,1},{4,6},{5,7},{6,4},{7,5},{8,10},{9,11},{10,... | collective-permute-start | bytes 786440 | tf_op jit(solution)/shard_map/ppermute | solution.py:250
  28.8 0.0 collective-permute-done.5.refs_9_
  28.8 1.4 %far.3 = (f32[256,256]{1,0:T(8,128)S(1)}, f32[16,128]{1,0:T(8,128)S(1)}) custom-call(s32[8]{0:T(128)S(1)} %copy-done.3, s32[8]{0:T(128)S(1)} %collective-permute-done.refs_0_.refs_1_, s32[8]{0:T(128)S(1)} %copy-done.4, f32[8,8,128,128]{3,2,1,0:T(8,128)S(1)} %copy-done, f32[8,256,256]{2,1,0:T(8,128)S(1)} %copy-done.1, ...), custom_call_target="tpu_custom_call" | custom-call | flops 1 | bytes 1 | tf_op jit(solution)/shard_map/far/pallas_call | solution.py:331
  30.2 6.2 %collective-permute-start.10 = (f32[16,128]{1,0:T(8,128)S(1)}, f32[16,128]{1,0:T(8,128)S(1)}, u32[]{:S(2)}, u32[]{:S(2)}) collective-permute-start(f32[16,128]{1,0:T(8,128)S(1)} %get-tuple-element.26), channel_id=1, source_target_pairs={{0,12},{4,8},{8,4},{12,0},{1,13},{5,9},{9,5},{13,1},{2,14},{6,10},... | collective-permute-start | bytes 24584 | tf_op jit(solution)/shard_map/ppermute | solution.py:250
  36.4 1.3 %collective-permute-start.8 = (f32[16,128]{1,0:T(8,128)S(1)}, f32[16,128]{1,0:T(8,128)S(1)}, u32[]{:S(2)}, u32[]{:S(2)}) collective-permute-start(f32[16,128]{1,0:T(8,128)S(1)} %get-tuple-element.26), channel_id=1, source_target_pairs={{0,4},{4,0},{8,12},{12,8},{1,5},{5,1},{9,13},{13,9},{2,6},{6,2},{1... | collective-permute-start | bytes 24584 | tf_op jit(solution)/shard_map/ppermute | solution.py:250
  37.7 0.0 collective-permute-start.9
  37.7 0.1 collective-permute-start.15
  37.8 0.3 collective-permute-done.10
  38.0 2.0 %collective-permute-done.8 = f32[16,128]{1,0:T(8,128)S(1)} collective-permute-done((f32[16,128]{1,0:T(8,128)S(1)}, f32[16,128]{1,0:T(8,128)S(1)}, u32[]{:S(2)}, u32[]{:S(2)}) %collective-permute-start.8) | collective-permute-done | bytes 8224 | tf_op jit(solution)/shard_map/ppermute | solution.py:250
  40.1 2.2 %collective-permute-done.9 = f32[16,128]{1,0:T(8,128)S(1)} collective-permute-done((f32[16,128]{1,0:T(8,128)S(1)}, f32[16,128]{1,0:T(8,128)S(1)}, u32[]{:S(2)}, u32[]{:S(2)}) %collective-permute-start.9) | collective-permute-done | bytes 8224 | tf_op jit(solution)/shard_map/ppermute | solution.py:250
  42.3 0.0 collective-permute-start.11
  42.3 0.1 collective-permute-start.12
  42.4 1.8 %collective-permute-start.13 = (f32[16,128]{1,0:T(8,128)S(1)}, f32[16,128]{1,0:T(8,128)S(1)}, u32[]{:S(2)}, u32[]{:S(2)}) collective-permute-start(f32[16,128]{1,0:T(8,128)S(1)} %add_add_fusion.1), channel_id=1, source_target_pairs={{0,3},{1,2},{2,1},{3,0},{4,7},{5,6},{6,5},{7,4},{8,11},{9,10},{10,... | collective-permute-start | bytes 24584 | tf_op jit(solution)/shard_map/ppermute | solution.py:250
  44.1 0.0 collective-permute-done.14
  44.2 0.4 collective-permute-start.16
  44.6 0.0 collective-permute-done.11
  44.6 1.4 %collective-permute-done.12 = f32[16,128]{1,0:T(8,128)S(1)} collective-permute-done((f32[16,128]{1,0:T(8,128)S(1)}, f32[16,128]{1,0:T(8,128)S(1)}, u32[]{:S(2)}, u32[]{:S(2)}) %collective-permute-start.12) | collective-permute-done | bytes 8224 | tf_op jit(solution)/shard_map/ppermute | solution.py:250
  46.0 0.0 collective-permute-done.13
  46.0 0.0 collective-permute-done.15
  46.1 0.2 collective-permute-start.17
  46.2 0.0 collective-permute-done.16.refs_2_
  46.2 1.4 %collective-permute-done.17.refs_3_ = f32[256,256]{1,0:T(8,128)S(1)} collective-permute-done((f32[256,256]{1,0:T(8,128)S(1)}, f32[256,256]{1,0:T(8,128)S(1)}, u32[]{:S(2)}, u32[]{:S(2)}) %collective-permute-start.17) | collective-permute-done | bytes 262176 | tf_op jit(solution)/shard_map/ppermute | solution.py:250
  47.7 1.4 %residual.1 = (f32[1024,256]{1,0:T(8,128)}, f32[1024,256]{1,0:T(8,128)}) custom-call(f32[16,128]{1,0:T(8,128)S(1)} %add_add_fusion.sums, f32[1024,256]{1,0:T(8,128)S(1)} %get-tuple-element.17.refs_7_.live, f32[256,256]{1,0:T(8,128)S(1)} %add.30.refs_0_, f32[256,256]{1,0:T(8,128)S(1)} %add.31.refs_1_, f32[256,256]{1,0:T(8,128)S(1)} %collective-permute-done.16.refs_2_, ...), custom_call_target="tpu_custom_call" | custom-call | flops 1 | bytes 1 | tf_op jit(solution)/shard_map/residual/pallas_call | solution.py:369
  (8 shorter events, 0.1 us)
Async XLA Ops:
  0.6 14.4 %copy-start.1 = (f32[8,256,256]{2,1,0:T(8,128)S(1)}, f32[8,256,256]{2,1,0:T(8,128)}, u32[]{:S(2)}) copy-start(f32[8,256,256]{2,1,0:T(8,128)} %refs_4_.5) | copy-start | bytes 6291460
  0.6 14.3 %copy-start = (f32[8,8,128,128]{3,2,1,0:T(8,128)S(1)}, f32[8,8,128,128]{3,2,1,0:T(8,128)}, u32[]{:S(2)}) copy-start(f32[8,8,128,128]{3,2,1,0:T(8,128)} %refs_3_.5) | copy-start | bytes 12582916
  0.7 13.3 %collective-permute-start.2 = (f32[8,256,256]{2,1,0:T(8,128)}, f32[8,256,256]{2,1,0:T(8,128)S(1)}, u32[]{:S(2)}, u32[]{:S(2)}) collective-permute-start(f32[8,256,256]{2,1,0:T(8,128)} %refs_4_.5), channel_id=1, source_target_pairs={{0,1},{1,0},{2,3},{3,2},{4,5},{5,4},{6,7},{7,6},{8,9},{9,8},{10,11... | collective-permute-start | bytes 6291464 | tf_op jit(solution)/shard_map/ppermute | solution.py:250
  1.2 1.5 %copy-start.2 = (f32[1024,256]{1,0:T(8,128)S(1)}, f32[1024,256]{1,0:T(8,128)}, u32[]{:S(2)}) copy-start(f32[1024,256]{1,0:T(8,128)} %wave.1) | copy-start | bytes 3145732
  2.6 0.8 %copy-start.4 = (s32[8]{0:T(128)S(1)}, s32[8]{0:T(128)}, u32[]{:S(2)}) copy-start(s32[8]{0:T(128)} %refs_2_.5) | copy-start | bytes 100
  3.4 9.3 %copy-start.3 = (s32[8]{0:T(128)S(1)}, s32[8]{0:T(128)}, u32[]{:S(2)}) copy-start(s32[8]{0:T(128)} %refs_0_.5) | copy-start | bytes 100
  5.1 14.7 %collective-permute-start.1 = (f32[4,8,128,128]{3,2,1,0:T(8,128)S(1)}, f32[4,8,128,128]{3,2,1,0:T(8,128)S(1)}, u32[]{:S(2)}, u32[]{:S(2)}) collective-permute-start(f32[4,8,128,128]{3,2,1,0:T(8,128)S(1)} %get-tuple-element.16), channel_id=1, source_target_pairs={{0,1},{1,0},{2,3},{3,2},{4,5},{5,4},{6,7},{7,6},{8,9},{9,8},{10,11... | collective-permute-start | bytes 6291464 | tf_op jit(solution)/shard_map/ppermute | solution.py:250
  5.6 12.6 %collective-permute-start.6 = (f32[128,256]{1,0:T(8,128)S(1)}, f32[128,256]{1,0:T(8,128)S(1)}, u32[]{:S(2)}, u32[]{:S(2)}) collective-permute-start(f32[128,256]{1,0:T(8,128)S(1)} %get-tuple-element.23), channel_id=1, source_target_pairs={{8,0},{12,4},{0,8},{4,12},{9,1},{13,5},{1,9},{5,13},{10,2},{14,6},... | collective-permute-start | bytes 393224 | tf_op jit(solution)/shard_map/ppermute | solution.py:281
  9.3 10.6 %collective-permute-start.4 = (f32[128,256]{1,0:T(8,128)S(1)}, f32[128,256]{1,0:T(8,128)S(1)}, u32[]{:S(2)}, u32[]{:S(2)}) collective-permute-start(f32[128,256]{1,0:T(8,128)S(1)} %get-tuple-element.20), channel_id=1, source_target_pairs={{0,4},{4,8},{8,12},{5,1},{9,5},{13,9},{2,6},{6,10},{10,14},{7,3},{... | collective-permute-start | bytes 393224 | tf_op jit(solution)/shard_map/ppermute | solution.py:306
  12.7 1.2 %collective-permute-start = (s32[8]{0:T(128)S(1)}, s32[8]{0:T(128)S(1)}, u32[]{:S(2)}, u32[]{:S(2)}) collective-permute-start(s32[8]{0:T(128)S(1)} %copy-done.3), channel_id=1, source_target_pairs={{0,1},{1,0},{2,3},{3,2},{4,5},{5,4},{6,7},{7,6},{8,9},{9,8},{10,11... | collective-permute-start | bytes 104 | tf_op jit(solution)/shard_map/ppermute | solution.py:250
  13.9 9.4 %collective-permute-start.3 = (f32[128,256]{1,0:T(8,128)S(1)}, f32[128,256]{1,0:T(8,128)S(1)}, u32[]{:S(2)}, u32[]{:S(2)}) collective-permute-start(f32[128,256]{1,0:T(8,128)S(1)} %get-tuple-element.19), channel_id=1, source_target_pairs={{8,0},{12,4},{0,8},{4,12},{9,1},{13,5},{1,9},{5,13},{10,2},{14,6},... | collective-permute-start | bytes 393224 | tf_op jit(solution)/shard_map/ppermute | solution.py:281
  18.2 6.2 %collective-permute-start.7 = (f32[1,128,256]{2,1,0:T(8,128)S(1)}, f32[1,128,256]{2,1,0:T(8,128)S(1)}, u32[]{:S(2)}, u32[]{:S(2)}) collective-permute-start(f32[1,128,256]{2,1,0:T(8,128)S(1)} %bitcast.2), channel_id=1, source_target_pairs={{0,2},{1,3},{2,0},{3,1},{4,6},{5,7},{6,4},{7,5},{8,10},{9,11},{10,... | collective-permute-start | bytes 393224 | tf_op jit(solution)/shard_map/ppermute | solution.py:250
  23.3 5.5 %collective-permute-start.5 = (f32[1,128,256]{2,1,0:T(8,128)S(1)}, f32[1,128,256]{2,1,0:T(8,128)S(1)}, u32[]{:S(2)}, u32[]{:S(2)}) collective-permute-start(f32[1,128,256]{2,1,0:T(8,128)S(1)} %bitcast.4), channel_id=1, source_target_pairs={{0,2},{1,3},{2,0},{3,1},{4,6},{5,7},{6,4},{7,5},{8,10},{9,11},{10,... | collective-permute-start | bytes 393224 | tf_op jit(solution)/shard_map/ppermute | solution.py:250
  25.9 18.3 %collective-permute-start.14 = (f32[256,256]{1,0:T(8,128)S(1)}, f32[256,256]{1,0:T(8,128)S(1)}, u32[]{:S(2)}, u32[]{:S(2)}) collective-permute-start(f32[256,256]{1,0:T(8,128)S(1)} %get-tuple-element.27), channel_id=1, source_target_pairs={{0,2},{1,3},{2,0},{3,1},{4,6},{5,7},{6,4},{7,5},{8,10},{9,11},{10,... | collective-permute-start | bytes 786440 | tf_op jit(solution)/shard_map/ppermute | solution.py:250
  30.2 7.8 %collective-permute-start.10 = (f32[16,128]{1,0:T(8,128)S(1)}, f32[16,128]{1,0:T(8,128)S(1)}, u32[]{:S(2)}, u32[]{:S(2)}) collective-permute-start(f32[16,128]{1,0:T(8,128)S(1)} %get-tuple-element.26), channel_id=1, source_target_pairs={{0,12},{4,8},{8,4},{12,0},{1,13},{5,9},{9,5},{13,1},{2,14},{6,10},... | collective-permute-start | bytes 24584 | tf_op jit(solution)/shard_map/ppermute | solution.py:250
  36.4 3.7 %collective-permute-start.8 = (f32[16,128]{1,0:T(8,128)S(1)}, f32[16,128]{1,0:T(8,128)S(1)}, u32[]{:S(2)}, u32[]{:S(2)}) collective-permute-start(f32[16,128]{1,0:T(8,128)S(1)} %get-tuple-element.26), channel_id=1, source_target_pairs={{0,4},{4,0},{8,12},{12,8},{1,5},{5,1},{9,13},{13,9},{2,6},{6,2},{1... | collective-permute-start | bytes 24584 | tf_op jit(solution)/shard_map/ppermute | solution.py:250
  37.7 4.5 %collective-permute-start.9 = (f32[16,128]{1,0:T(8,128)S(1)}, f32[16,128]{1,0:T(8,128)S(1)}, u32[]{:S(2)}, u32[]{:S(2)}) collective-permute-start(f32[16,128]{1,0:T(8,128)S(1)} %get-tuple-element.26), channel_id=1, source_target_pairs={{0,8},{4,12},{8,0},{12,4},{1,9},{5,13},{9,1},{13,5},{2,10},{6,14},... | collective-permute-start | bytes 24584 | tf_op jit(solution)/shard_map/ppermute | solution.py:250
  37.7 8.3 %collective-permute-start.15 = (f32[256,256]{1,0:T(8,128)S(1)}, f32[256,256]{1,0:T(8,128)S(1)}, u32[]{:S(2)}, u32[]{:S(2)}) collective-permute-start(f32[256,256]{1,0:T(8,128)S(1)} %get-tuple-element.28), channel_id=1, source_target_pairs={{0,2},{1,3},{2,0},{3,1},{4,6},{5,7},{6,4},{7,5},{8,10},{9,11},{10,... | collective-permute-start | bytes 786440 | tf_op jit(solution)/shard_map/ppermute | solution.py:250
  42.3 2.3 %collective-permute-start.11 = (f32[16,128]{1,0:T(8,128)S(1)}, f32[16,128]{1,0:T(8,128)S(1)}, u32[]{:S(2)}, u32[]{:S(2)}) collective-permute-start(f32[16,128]{1,0:T(8,128)S(1)} %add_add_fusion.1), channel_id=1, source_target_pairs={{0,1},{1,0},{2,3},{3,2},{4,5},{5,4},{6,7},{7,6},{8,9},{9,8},{10,11... | collective-permute-start | bytes 24584 | tf_op jit(solution)/shard_map/ppermute | solution.py:250
  42.3 3.7 %collective-permute-start.12 = (f32[16,128]{1,0:T(8,128)S(1)}, f32[16,128]{1,0:T(8,128)S(1)}, u32[]{:S(2)}, u32[]{:S(2)}) collective-permute-start(f32[16,128]{1,0:T(8,128)S(1)} %add_add_fusion.1), channel_id=1, source_target_pairs={{0,2},{1,3},{2,0},{3,1},{4,6},{5,7},{6,4},{7,5},{8,10},{9,11},{10,... | collective-permute-start | bytes 24584 | tf_op jit(solution)/shard_map/ppermute | solution.py:250
  42.4 3.6 %collective-permute-start.13 = (f32[16,128]{1,0:T(8,128)S(1)}, f32[16,128]{1,0:T(8,128)S(1)}, u32[]{:S(2)}, u32[]{:S(2)}) collective-permute-start(f32[16,128]{1,0:T(8,128)S(1)} %add_add_fusion.1), channel_id=1, source_target_pairs={{0,3},{1,2},{2,1},{3,0},{4,7},{5,6},{6,5},{7,4},{8,11},{9,10},{10,... | collective-permute-start | bytes 24584 | tf_op jit(solution)/shard_map/ppermute | solution.py:250
  44.2 2.1 %collective-permute-start.16 = (f32[256,256]{1,0:T(8,128)S(1)}, f32[256,256]{1,0:T(8,128)S(1)}, u32[]{:S(2)}, u32[]{:S(2)}) collective-permute-start(f32[256,256]{1,0:T(8,128)S(1)} %add.30.refs_0_), channel_id=1, source_target_pairs={{0,1},{1,0},{2,3},{3,2},{4,5},{5,4},{6,7},{7,6},{8,9},{9,8},{10,11... | collective-permute-start | bytes 786440 | tf_op jit(solution)/shard_map/ppermute | solution.py:250
  46.1 1.6 %collective-permute-start.17 = (f32[256,256]{1,0:T(8,128)S(1)}, f32[256,256]{1,0:T(8,128)S(1)}, u32[]{:S(2)}, u32[]{:S(2)}) collective-permute-start(f32[256,256]{1,0:T(8,128)S(1)} %add.31.refs_1_), channel_id=1, source_target_pairs={{0,1},{1,0},{2,3},{3,2},{4,5},{5,4},{6,7},{7,6},{8,9},{9,8},{10,11... | collective-permute-start | bytes 786440 | tf_op jit(solution)/shard_map/ppermute | solution.py:250

commit v3 on v2

--- a/solution.py
+++ b/solution.py
@@ -39,28 +39,18 @@
     return wave.at[pl.ds(pl.multiple_of(sector * block, block), block), :]
 
 
-def prepare_kernel(half, rows_hbm, whole, wave, left, mine_a, mine_b, halo, left_send, src, live, *rest):
-    rows_ref, sem = rest
+def prepare_kernel(half, live, left, mine_a, mine_b, halo, left_send, src, sem):
     core, side, _ = place()
     block = halo.shape[0]
-    rows = pltpu.make_async_copy(rows_hbm, rows_ref, sem.at[0])
-    rows.start()
-    send = pltpu.make_async_copy(left.at[pl.ds((1 - core) * half, half)], left_send, sem.at[1])
+    send = pltpu.make_async_copy(left.at[pl.ds((1 - core) * half, half)], left_send, sem.at[0])
     send.start()
+    mine_a[...] = sector_rows(live, core * half + side, block)[...]
+    mine_b[...] = sector_rows(live, core * half + half // 2 + side, block)[...]
+    halo[...] = sector_rows(live, (1 - core) * (2 * half - 1), block)[...]
     src[pl.ds(pl.multiple_of(core * (half + 1) * block, block), block), :] = jnp.zeros((block, src.shape[1]), BF16)
-    rows.wait()
-
-    def source(sector):
-        return masked(sector_rows(whole, sector, block)[...], rows_ref[sector])
-
-    mine_a[...] = source(core * half + side)
-    mine_b[...] = source(core * half + half // 2 + side)
-    halo[...] = source((1 - core) * (2 * half - 1))
-    for s in range(2 * half):
-        here = pl.ds(s * block, block)
-        live[here, :] = masked(wave[here, :], rows_ref[s])
     for i in range(half + 1):
-        put(src, pl.multiple_of((i + 1 - core) * block, block), source(core * (half - 1) + i))
+        rows = sector_rows(live, core * (half - 1) + i, block)[...]
+        put(src, pl.multiple_of((i + 1 - core) * block, block), rows)
     send.wait()
 
 
@@ -268,9 +258,12 @@
     part = half // 2
     shift = QD // sector_count
     merged = secs <= 2 * shift
-    whole = wavefunction
+    row = jnp.arange(block, dtype=jnp.int32)
+    live = jnp.where((row < block_rows[:, None])[:, :, None], wavefunction.reshape(sector_count, block, cols), 0.0)
+    live = live.reshape(sector_count * block, cols)
+    whole = live
     if reps > 1:
-        whole = lax.all_gather(wavefunction, "rep", axis=1, tiled=True)
+        whole = lax.all_gather(live, "rep", axis=1, tiled=True)
     wide = whole.shape[1]
 
     up = [(i, i - shift) for i in range(shift, secs)]
@@ -291,23 +284,21 @@
     rows = part * block
     blocks = shape(half, terms, block, block)
     source_shape = ((half + 2) * block, 3 * wide)
-    mine_a, mine_b, halo, left_send, src, live = pl.pallas_call(
+    cls_pair = swap(term_charge, "mpo", 1)
+    mine_a, mine_b, halo, left_send, src = pl.pallas_call(
         functools.partial(prepare_kernel, half),
-        out_shape=(shape(block, wide),) * 3
-        + (blocks, jax.ShapeDtypeStruct(source_shape, BF16), shape(sector_count * block, cols)),
-        in_specs=[ANY, VMEM, VMEM, ANY],
-        out_specs=(VMEM,) * 6,
-        scratch_shapes=[pltpu.SMEM((sector_count,), jnp.int32), pltpu.SemaphoreType.DMA((2,))],
+        out_shape=(shape(block, wide),) * 3 + (blocks, jax.ShapeDtypeStruct(source_shape, BF16)),
+        in_specs=[VMEM, ANY],
+        out_specs=(VMEM,) * 5,
+        scratch_shapes=[pltpu.SemaphoreType.DMA((1,))],
         compiler_params=params(PREPARE_VMEM),
         cost_estimate=cost(1, 1),
         name="prepare",
-    )(block_rows, whole, wavefunction, left_blocks)
+    )(after(whole, cls_pair), left_blocks)
     far_a = far(mine_a)
     halo = lax.ppermute(halo, ("sec", "mpo"), halo_pairs)
     right_pair = swap(right_blocks, "mpo", 1)
-    cls_pair = swap(term_charge, "mpo", 1)
     left_pair = swap(left_send, "mpo", 1)
-    far_b = far(after(mine_b, right_pair, cls_pair))
 
     lists = [pltpu.SMEM((terms,), jnp.int32)] * 2
 
@@ -347,8 +338,9 @@
         )(term_charge, cls_pair, block_rows, left_blocks, right_blocks, left_pair, right_pair, live, *far, acc, *extra)
 
     acc = near(True, term_charge, left_blocks, right_blocks, src)
+    far_b = far(after(mine_b, acc))
+    acc = near(False, cls_pair, left_pair, right_pair, term_charge, left_blocks, right_blocks, halo, src, acc)
     other_a = swap(after(far_a, acc), "mpo", 2)
-    acc = near(False, cls_pair, left_pair, right_pair, term_charge, left_blocks, right_blocks, halo, src, acc)
     other_b = swap(after(far_b, acc), "mpo", 2)
     part_a, sums = add_far(0, (far_a, other_a), acc, None)
     recv_a = swap(part_a, "mpo", 2)
@@ -361,7 +353,7 @@
         sums = lax.psum(sums, "sec")
     if reps > 1:
         sums = lax.psum(sums, "rep")
-    sums = everyone(sums, "mpo")
+    sums = everyone(after(sums, recv_a), "mpo")
     totals = [part_a + recv_a, part_b + after(recv_b, sums)]
     totals += [swap(total, "mpo", 1) for total in totals]
 

time: 49.3 us -> 51 us (1.034); the launches traced: 49 us -> 51.3 us
  waiting for transfers between devices: 8.46 us -> 12.4 us
  starting transfers between devices: 25 us -> 21.6 us
  other arithmetic: 0.08 us -> 2.38 us
  local copies, waits for them, and re-layouts: 2.28 us -> 0.02 us
  Pallas kernels: 12.5 us -> 14.1 us
    ppermute x2, waiting for transfers between devices: 0.01 us -> 3.53 us  [far(): return lax.ppermute(array, 'sec', up + down)[None]]
    ppermute x15, starting transfers between devices: 16.8 us -> 14 us  [swap(): return lax.ppermute(array, axis, pairs)]
    unnamed x10 -> x8, local copies, waits for them, and re-layouts: 2.28 us -> 0.02 us
    ppermute x2, starting transfers between devices: 4.71 us -> 3.05 us  [far(): return lax.ppermute(array, 'sec', up + down)[None]]
    select_n x0 -> x1, other arithmetic: none -> 1.57 us  [local(): jnp.where((row < block_rows[:, None])[:, :, None], wavefunction.reshape(s...]
    pallas_call x2, Pallas kernels: 2.75 us -> 4.01 us  [add_far(): pl.pallas_call(functools.partial(far_kernel, lo, shift, secs, sums is not...]
    ppermute x1, starting transfers between devices: 3.48 us -> 4.55 us  [local(): halo = lax.ppermute(halo, ('sec', 'mpo'), halo_pairs)]
    lt x0 -> x1, other arithmetic: none -> 0.73 us  [local(): row < block_rows[:, None]]
  transfers between devices with their start and end apart: 18 -> 18, of which waited for: 6 -> 9; matrix products, arithmetic and copies ran while one was open for 0% -> 5% of each run, Pallas kernels for 23% -> 25%
where the time goes in v3:
time: 51 us; the launch traced here: 51.3 us
  starting transfers between devices  21.6 us (42%)
  Pallas kernels  14.1 us (28%)
  waiting for transfers between devices  12.4 us (24%)
  other arithmetic  2.38 us (5%)
  between operations  0.76 us (1%)
    ppermute x15, starting transfers between devices, swap(): return lax.ppermute(array, axis, pairs)  14 us
    ppermute x15, waiting for transfers between devices, swap(): return lax.ppermute(array, axis, pairs)  8.9 us
    pallas_call x2, Pallas kernels, near(): pl.pallas_call(functools.partial(near_kernel, own), out_shape=shape(half...  6.95 us
    ppermute x1, starting transfers between devices, local(): halo = lax.ppermute(halo, ('sec', 'mpo'), halo_pairs)  4.55 us
    pallas_call x2, Pallas kernels, add_far(): pl.pallas_call(functools.partial(far_kernel, lo, shift, secs, sums is not...  4.01 us
    ppermute x2, waiting for transfers between devices, far(): return lax.ppermute(array, 'sec', up + down)[None]  3.53 us
    ppermute x2, starting transfers between devices, far(): return lax.ppermute(array, 'sec', up + down)[None]  3.05 us
    pallas_call x1, Pallas kernels, local(): pl.pallas_call(functools.partial(prepare_kernel, half), out_shape=(shape(...  1.77 us
  transfers between devices with their start and end apart: 18, of which 9 were waited for; matrix products, arithmetic and copies ran while one was open for 5% of the time, Pallas kernels for 25%

profile of v3, /device:TPU:0, one launch (start us, length us, event | category | flops | bytes accessed | tf_op | source)
XLA Modules:
  0.0 51.3 jit_solution(11640297339990282985)
XLA Ops:
  0.6 0.5 %collective-permute-start = (s32[8]{0:T(128)}, s32[8]{0:T(128)S(1)}, u32[]{:S(2)}, u32[]{:S(2)}) collective-permute-start(s32[8]{0:T(128)} %refs_0_.5), channel_id=1, source_target_pairs={{0,1},{1,0},{2,3},{3,2},{4,5},{5,4},{6,7},{7,6},{8,9},{9,8},{10,11... | collective-permute-start | bytes 104 | tf_op jit(solution)/shard_map/ppermute | solution.py:240
  1.1 0.1 collective-permute-start.2
  1.2 0.7 %fusion = pred[1024]{0:T(1024)(128)(4,1)S(1)} fusion(s32[8]{0:T(128)} %refs_2_.5), kind=kLoop, calls=%fused_computation.4 | loop fusion | flops 1024 | bytes 1056 | tf_op jit(solution)/shard_map/lt | solution.py:262
  2.0 1.6 %broadcast_select_fusion.live.refs_7_ = f32[1024,256]{1,0:T(8,128)S(1)} fusion(f32[1024,256]{1,0:T(8,128)} %param.5, pred[1024]{0:T(1024)(128)(4,1)S(1)} %fusion), kind=kLoop, calls=%fused_computation | loop fusion | flops 262144 | bytes 2098176 | tf_op jit(solution)/shard_map/jit(_where)/select_n | solution.py:262
  3.5 0.0 copy-start
  3.5 0.0 copy-start.2
  3.6 0.0 collective-permute-done.refs_0_.refs_1_
  3.6 1.8 %prepare.1 = (f32[128,256]{1,0:T(8,128)S(1)}, f32[128,256]{1,0:T(8,128)S(1)}, f32[128,256]{1,0:T(8,128)S(1)}, f32[4,8,128,128]{3,2,1,0:T(8,128)S(1)}, bf16[768,768]{1,0:T(8,128)(2,1)S(1)}) custom-call(f32[1024,256]{1,0:T(8,128)S(1)} %broadcast_select_fusion.live.refs_7_, f32[8,8,128,128]{3,2,1,0:T(8,128)} %refs_3_.5), custom_call_target="tpu_custom_call" | custom-call | flops 1 | bytes 1 | tf_op jit(solution)/shard_map/prepare/pallas_call | solution.py:288
  5.3 0.5 collective-permute-start.1
  5.8 4.6 %collective-permute-start.4 = (f32[128,256]{1,0:T(8,128)S(1)}, f32[128,256]{1,0:T(8,128)S(1)}, u32[]{:S(2)}, u32[]{:S(2)}) collective-permute-start(f32[128,256]{1,0:T(8,128)S(1)} %get-tuple-element.22), channel_id=1, source_target_pairs={{0,4},{4,8},{8,12},{5,1},{9,5},{13,9},{2,6},{6,10},{10,14},{7,3},{... | collective-permute-start | bytes 393224 | tf_op jit(solution)/shard_map/ppermute | solution.py:299
  10.4 2.7 %collective-permute-start.6 = (f32[128,256]{1,0:T(8,128)S(1)}, f32[128,256]{1,0:T(8,128)S(1)}, u32[]{:S(2)}, u32[]{:S(2)}) collective-permute-start(f32[128,256]{1,0:T(8,128)S(1)} %get-tuple-element.24), channel_id=1, source_target_pairs={{8,0},{12,4},{0,8},{4,12},{9,1},{13,5},{1,9},{5,13},{10,2},{14,6},... | collective-permute-start | bytes 393224 | tf_op jit(solution)/shard_map/ppermute | solution.py:274
  13.1 0.0 copy-done.1
  13.1 2.3 %own_near.1.refs_8_ = f32[512,256]{1,0:T(8,128)S(1)} custom-call(s32[8]{0:T(128)S(1)} %copy-done.2, f32[8,8,128,128]{3,2,1,0:T(8,128)S(1)} %copy-done, f32[8,256,256]{2,1,0:T(8,128)S(1)} %copy-done.1, bf16[768,768]{1,0:T(8,128)(2,1)S(1)} %get-tuple-element.20.refs_3_.refs_7_), custom_call_target="tpu_custom_call" | custom-call | flops 1 | bytes 1 | tf_op jit(solution)/shard_map/own_near/pallas_call | solution.py:306
  15.4 0.0 copy-start.3
  15.4 0.4 collective-permute-start.3
  15.8 0.0 collective-permute-done.4.refs_6_
  15.8 0.0 collective-permute-done.2.refs_2_.refs_6_
  15.8 0.0 collective-permute-done.1.refs_1_.refs_5_
  15.8 4.6 %pair_near.1.refs_10_ = f32[512,256]{1,0:T(8,128)S(1)} custom-call(s32[8]{0:T(128)S(1)} %collective-permute-done.refs_0_.refs_1_, f32[4,8,128,128]{3,2,1,0:T(8,128)S(1)} %collective-permute-done.1.refs_1_.refs_5_, f32[8,256,256]{2,1,0:T(8,128)S(1)} %collective-permute-done.2.refs_2_.refs_6_, s32[8]{0:T(128)S(1)} %copy-done.2, ...), custom_call_target="tpu_custom_call" | custom-call | flops 1 | bytes 1 | tf_op jit(solution)/shard_map/pair_near/pallas_call | solution.py:306
  20.5 3.0 %collective-permute-done.6 = f32[128,256]{1,0:T(8,128)S(1)} collective-permute-done((f32[128,256]{1,0:T(8,128)S(1)}, f32[128,256]{1,0:T(8,128)S(1)}, u32[]{:S(2)}, u32[]{:S(2)}) %collective-permute-start.6) | collective-permute-done | bytes 131104 | tf_op jit(solution)/shard_map/ppermute | solution.py:274
  23.4 1.5 %collective-permute-start.7 = (f32[1,128,256]{2,1,0:T(8,128)S(1)}, f32[1,128,256]{2,1,0:T(8,128)S(1)}, u32[]{:S(2)}, u32[]{:S(2)}) collective-permute-start(f32[1,128,256]{2,1,0:T(8,128)S(1)} %bitcast.6), channel_id=1, source_target_pairs={{0,2},{1,3},{2,0},{3,1},{4,6},{5,7},{6,4},{7,5},{8,10},{9,11},{10,... | collective-permute-start | bytes 393224 | tf_op jit(solution)/shard_map/ppermute | solution.py:240
  24.9 0.6 %collective-permute-done.3 = f32[128,256]{1,0:T(8,128)S(1)} collective-permute-done((f32[128,256]{1,0:T(8,128)S(1)}, f32[128,256]{1,0:T(8,128)S(1)}, u32[]{:S(2)}, u32[]{:S(2)}) %collective-permute-start.3) | collective-permute-done | bytes 131104 | tf_op jit(solution)/shard_map/ppermute | solution.py:274
  25.5 1.5 %collective-permute-start.5 = (f32[1,128,256]{2,1,0:T(8,128)S(1)}, f32[1,128,256]{2,1,0:T(8,128)S(1)}, u32[]{:S(2)}, u32[]{:S(2)}) collective-permute-start(f32[1,128,256]{2,1,0:T(8,128)S(1)} %bitcast.4), channel_id=1, source_target_pairs={{0,2},{1,3},{2,0},{3,1},{4,6},{5,7},{6,4},{7,5},{8,10},{9,11},{10,... | collective-permute-start | bytes 393224 | tf_op jit(solution)/shard_map/ppermute | solution.py:240
  27.0 2.5 %collective-permute-done.7.refs_9_ = f32[1,128,256]{2,1,0:T(8,128)S(1)} collective-permute-done((f32[1,128,256]{2,1,0:T(8,128)S(1)}, f32[1,128,256]{2,1,0:T(8,128)S(1)}, u32[]{:S(2)}, u32[]{:S(2)}) %collective-permute-start.7) | collective-permute-done | bytes 131104 | tf_op jit(solution)/shard_map/ppermute | solution.py:240
  29.4 2.0 %far.2 = (f32[256,256]{1,0:T(8,128)S(1)}, f32[16,128]{1,0:T(8,128)S(1)}) custom-call(s32[8]{0:T(128)S(1)} %copy-done.2, s32[8]{0:T(128)S(1)} %collective-permute-done.refs_0_.refs_1_, s32[8]{0:T(128)S(1)} %copy-done.3, f32[8,8,128,128]{3,2,1,0:T(8,128)S(1)} %copy-done, f32[8,256,256]{2,1,0:T(8,128)S(1)} %copy-done.1, ...), custom_call_target="tpu_custom_call" | custom-call | flops 1 | bytes 1 | tf_op jit(solution)/shard_map/far/pallas_call | solution.py:322
  31.4 2.2 %collective-permute-start.11 = (f32[256,256]{1,0:T(8,128)S(1)}, f32[256,256]{1,0:T(8,128)S(1)}, u32[]{:S(2)}, u32[]{:S(2)}) collective-permute-start(f32[256,256]{1,0:T(8,128)S(1)} %get-tuple-element.28), channel_id=1, source_target_pairs={{0,2},{1,3},{2,0},{3,1},{4,6},{5,7},{6,4},{7,5},{8,10},{9,11},{10,... | collective-permute-start | bytes 786440 | tf_op jit(solution)/shard_map/ppermute | solution.py:240
  33.6 0.0 collective-permute-done.5.refs_9_
  33.6 2.0 %far.3 = (f32[256,256]{1,0:T(8,128)S(1)}, f32[16,128]{1,0:T(8,128)S(1)}) custom-call(s32[8]{0:T(128)S(1)} %copy-done.2, s32[8]{0:T(128)S(1)} %collective-permute-done.refs_0_.refs_1_, s32[8]{0:T(128)S(1)} %copy-done.3, f32[8,8,128,128]{3,2,1,0:T(8,128)S(1)} %copy-done, f32[8,256,256]{2,1,0:T(8,128)S(1)} %copy-done.1, ...), custom_call_target="tpu_custom_call" | custom-call | flops 1 | bytes 1 | tf_op jit(solution)/shard_map/far/pallas_call | solution.py:322
  35.7 2.3 %collective-permute-start.10 = (f32[16,128]{1,0:T(8,128)S(1)}, f32[16,128]{1,0:T(8,128)S(1)}, u32[]{:S(2)}, u32[]{:S(2)}) collective-permute-start(f32[16,128]{1,0:T(8,128)S(1)} %get-tuple-element.27), channel_id=1, source_target_pairs={{0,12},{4,8},{8,4},{12,0},{1,13},{5,9},{9,5},{13,1},{2,14},{6,10},... | collective-permute-start | bytes 24584 | tf_op jit(solution)/shard_map/ppermute | solution.py:240
  38.0 0.9 %collective-permute-start.8 = (f32[16,128]{1,0:T(8,128)S(1)}, f32[16,128]{1,0:T(8,128)S(1)}, u32[]{:S(2)}, u32[]{:S(2)}) collective-permute-start(f32[16,128]{1,0:T(8,128)S(1)} %get-tuple-element.27), channel_id=1, source_target_pairs={{0,4},{4,0},{8,12},{12,8},{1,5},{5,1},{9,13},{13,9},{2,6},{6,2},{1... | collective-permute-start | bytes 24584 | tf_op jit(solution)/shard_map/ppermute | solution.py:240
  38.9 1.3 %collective-permute-start.9 = (f32[16,128]{1,0:T(8,128)S(1)}, f32[16,128]{1,0:T(8,128)S(1)}, u32[]{:S(2)}, u32[]{:S(2)}) collective-permute-start(f32[16,128]{1,0:T(8,128)S(1)} %get-tuple-element.27), channel_id=1, source_target_pairs={{0,8},{4,12},{8,0},{12,4},{1,9},{5,13},{9,1},{13,5},{2,10},{6,14},... | collective-permute-start | bytes 24584 | tf_op jit(solution)/shard_map/ppermute | solution.py:240
  40.1 0.7 %collective-permute-start.15 = (f32[256,256]{1,0:T(8,128)S(1)}, f32[256,256]{1,0:T(8,128)S(1)}, u32[]{:S(2)}, u32[]{:S(2)}) collective-permute-start(f32[256,256]{1,0:T(8,128)S(1)} %get-tuple-element.30), channel_id=1, source_target_pairs={{0,2},{1,3},{2,0},{3,1},{4,6},{5,7},{6,4},{7,5},{8,10},{9,11},{10,... | collective-permute-start | bytes 786440 | tf_op jit(solution)/shard_map/ppermute | solution.py:240
  40.8 0.4 collective-permute-done.10
  41.2 0.5 collective-permute-done.8
  41.7 1.8 %collective-permute-done.9 = f32[16,128]{1,0:T(8,128)S(1)} collective-permute-done((f32[16,128]{1,0:T(8,128)S(1)}, f32[16,128]{1,0:T(8,128)S(1)}, u32[]{:S(2)}, u32[]{:S(2)}) %collective-permute-start.9) | collective-permute-done | bytes 8224 | tf_op jit(solution)/shard_map/ppermute | solution.py:240
  43.4 0.0 collective-permute-done.11
  43.4 0.1 collective-permute-start.12
  43.5 1.7 %collective-permute-start.13 = (f32[16,128]{1,0:T(8,128)S(1)}, f32[16,128]{1,0:T(8,128)S(1)}, u32[]{:S(2)}, u32[]{:S(2)}) collective-permute-start(f32[16,128]{1,0:T(8,128)S(1)} %add_add_fusion.1), channel_id=1, source_target_pairs={{0,2},{1,3},{2,0},{3,1},{4,6},{5,7},{6,4},{7,5},{8,10},{9,11},{10,... | collective-permute-start | bytes 24584 | tf_op jit(solution)/shard_map/ppermute | solution.py:240
  45.1 0.2 collective-permute-start.14
  45.4 0.4 collective-permute-start.16
  45.8 0.0 collective-permute-done.12
  45.8 1.4 %collective-permute-done.13 = f32[16,128]{1,0:T(8,128)S(1)} collective-permute-done((f32[16,128]{1,0:T(8,128)S(1)}, f32[16,128]{1,0:T(8,128)S(1)}, u32[]{:S(2)}, u32[]{:S(2)}) %collective-permute-start.13) | collective-permute-done | bytes 8224 | tf_op jit(solution)/shard_map/ppermute | solution.py:240
  47.2 1.0 %collective-permute-done.14 = f32[16,128]{1,0:T(8,128)S(1)} collective-permute-done((f32[16,128]{1,0:T(8,128)S(1)}, f32[16,128]{1,0:T(8,128)S(1)}, u32[]{:S(2)}, u32[]{:S(2)}) %collective-permute-start.14) | collective-permute-done | bytes 8224 | tf_op jit(solution)/shard_map/ppermute | solution.py:240
  48.2 0.0 collective-permute-done.15
  48.3 0.2 collective-permute-start.17
  48.5 0.0 collective-permute-done.16.refs_2_
  48.5 1.4 %collective-permute-done.17.refs_3_ = f32[256,256]{1,0:T(8,128)S(1)} collective-permute-done((f32[256,256]{1,0:T(8,128)S(1)}, f32[256,256]{1,0:T(8,128)S(1)}, u32[]{:S(2)}, u32[]{:S(2)}) %collective-permute-start.17) | collective-permute-done | bytes 262176 | tf_op jit(solution)/shard_map/ppermute | solution.py:240
  49.9 1.4 %residual.1 = (f32[1024,256]{1,0:T(8,128)}, f32[1024,256]{1,0:T(8,128)}) custom-call(f32[16,128]{1,0:T(8,128)S(1)} %add_add_fusion.sums, f32[1024,256]{1,0:T(8,128)S(1)} %broadcast_select_fusion.live.refs_7_, f32[256,256]{1,0:T(8,128)S(1)} %add.30.refs_0_, f32[256,256]{1,0:T(8,128)S(1)} %add.31.refs_1_, f32[256,256]{1,0:T(8,128)S(1)} %collective-permute-done.16.refs_2_, ...), custom_call_target="tpu_custom_call" | custom-call | flops 1 | bytes 1 | tf_op jit(solution)/shard_map/residual/pallas_call | solution.py:361
  (8 shorter events, 0.1 us)
Async XLA Ops:
  0.6 2.9 %collective-permute-start = (s32[8]{0:T(128)}, s32[8]{0:T(128)S(1)}, u32[]{:S(2)}, u32[]{:S(2)}) collective-permute-start(s32[8]{0:T(128)} %refs_0_.5), channel_id=1, source_target_pairs={{0,1},{1,0},{2,3},{3,2},{4,5},{5,4},{6,7},{7,6},{8,9},{9,8},{10,11... | collective-permute-start | bytes 104 | tf_op jit(solution)/shard_map/ppermute | solution.py:240
  1.1 14.7 %collective-permute-start.2 = (f32[8,256,256]{2,1,0:T(8,128)}, f32[8,256,256]{2,1,0:T(8,128)S(1)}, u32[]{:S(2)}, u32[]{:S(2)}) collective-permute-start(f32[8,256,256]{2,1,0:T(8,128)} %refs_4_.5), channel_id=1, source_target_pairs={{0,1},{1,0},{2,3},{3,2},{4,5},{5,4},{6,7},{7,6},{8,9},{9,8},{10,11... | collective-permute-start | bytes 6291464 | tf_op jit(solution)/shard_map/ppermute | solution.py:240
  2.0 11.1 %copy-start.1 = (f32[8,256,256]{2,1,0:T(8,128)S(1)}, f32[8,256,256]{2,1,0:T(8,128)}, u32[]{:S(2)}) copy-start(f32[8,256,256]{2,1,0:T(8,128)} %refs_4_.5) | copy-start | bytes 6291460
  3.5 9.5 %copy-start = (f32[8,8,128,128]{3,2,1,0:T(8,128)S(1)}, f32[8,8,128,128]{3,2,1,0:T(8,128)}, u32[]{:S(2)}) copy-start(f32[8,8,128,128]{3,2,1,0:T(8,128)} %refs_3_.5) | copy-start | bytes 12582916
  3.5 9.5 %copy-start.2 = (s32[8]{0:T(128)S(1)}, s32[8]{0:T(128)}, u32[]{:S(2)}) copy-start(s32[8]{0:T(128)} %refs_0_.5) | copy-start | bytes 100
  5.3 10.5 %collective-permute-start.1 = (f32[4,8,128,128]{3,2,1,0:T(8,128)S(1)}, f32[4,8,128,128]{3,2,1,0:T(8,128)S(1)}, u32[]{:S(2)}, u32[]{:S(2)}) collective-permute-start(f32[4,8,128,128]{3,2,1,0:T(8,128)S(1)} %get-tuple-element.18), channel_id=1, source_target_pairs={{0,1},{1,0},{2,3},{3,2},{4,5},{5,4},{6,7},{7,6},{8,9},{9,8},{10,11... | collective-permute-start | bytes 6291464 | tf_op jit(solution)/shard_map/ppermute | solution.py:240
  5.8 10.0 %collective-permute-start.4 = (f32[128,256]{1,0:T(8,128)S(1)}, f32[128,256]{1,0:T(8,128)S(1)}, u32[]{:S(2)}, u32[]{:S(2)}) collective-permute-start(f32[128,256]{1,0:T(8,128)S(1)} %get-tuple-element.22), channel_id=1, source_target_pairs={{0,4},{4,8},{8,12},{5,1},{9,5},{13,9},{2,6},{6,10},{10,14},{7,3},{... | collective-permute-start | bytes 393224 | tf_op jit(solution)/shard_map/ppermute | solution.py:299
  10.4 13.0 %collective-permute-start.6 = (f32[128,256]{1,0:T(8,128)S(1)}, f32[128,256]{1,0:T(8,128)S(1)}, u32[]{:S(2)}, u32[]{:S(2)}) collective-permute-start(f32[128,256]{1,0:T(8,128)S(1)} %get-tuple-element.24), channel_id=1, source_target_pairs={{8,0},{12,4},{0,8},{4,12},{9,1},{13,5},{1,9},{5,13},{10,2},{14,6},... | collective-permute-start | bytes 393224 | tf_op jit(solution)/shard_map/ppermute | solution.py:274
  15.4 14.0 %copy-start.3 = (s32[8]{0:T(128)S(1)}, s32[8]{0:T(128)}, u32[]{:S(2)}) copy-start(s32[8]{0:T(128)} %refs_2_.5) | copy-start | bytes 100
  15.4 10.1 %collective-permute-start.3 = (f32[128,256]{1,0:T(8,128)S(1)}, f32[128,256]{1,0:T(8,128)S(1)}, u32[]{:S(2)}, u32[]{:S(2)}) collective-permute-start(f32[128,256]{1,0:T(8,128)S(1)} %get-tuple-element.21), channel_id=1, source_target_pairs={{8,0},{12,4},{0,8},{4,12},{9,1},{13,5},{1,9},{5,13},{10,2},{14,6},... | collective-permute-start | bytes 393224 | tf_op jit(solution)/shard_map/ppermute | solution.py:274
  23.4 6.0 %collective-permute-start.7 = (f32[1,128,256]{2,1,0:T(8,128)S(1)}, f32[1,128,256]{2,1,0:T(8,128)S(1)}, u32[]{:S(2)}, u32[]{:S(2)}) collective-permute-start(f32[1,128,256]{2,1,0:T(8,128)S(1)} %bitcast.6), channel_id=1, source_target_pairs={{0,2},{1,3},{2,0},{3,1},{4,6},{5,7},{6,4},{7,5},{8,10},{9,11},{10,... | collective-permute-start | bytes 393224 | tf_op jit(solution)/shard_map/ppermute | solution.py:240
  25.5 8.2 %collective-permute-start.5 = (f32[1,128,256]{2,1,0:T(8,128)S(1)}, f32[1,128,256]{2,1,0:T(8,128)S(1)}, u32[]{:S(2)}, u32[]{:S(2)}) collective-permute-start(f32[1,128,256]{2,1,0:T(8,128)S(1)} %bitcast.4), channel_id=1, source_target_pairs={{0,2},{1,3},{2,0},{3,1},{4,6},{5,7},{6,4},{7,5},{8,10},{9,11},{10,... | collective-permute-start | bytes 393224 | tf_op jit(solution)/shard_map/ppermute | solution.py:240
  31.4 12.0 %collective-permute-start.11 = (f32[256,256]{1,0:T(8,128)S(1)}, f32[256,256]{1,0:T(8,128)S(1)}, u32[]{:S(2)}, u32[]{:S(2)}) collective-permute-start(f32[256,256]{1,0:T(8,128)S(1)} %get-tuple-element.28), channel_id=1, source_target_pairs={{0,2},{1,3},{2,0},{3,1},{4,6},{5,7},{6,4},{7,5},{8,10},{9,11},{10,... | collective-permute-start | bytes 786440 | tf_op jit(solution)/shard_map/ppermute | solution.py:240
  35.7 5.5 %collective-permute-start.10 = (f32[16,128]{1,0:T(8,128)S(1)}, f32[16,128]{1,0:T(8,128)S(1)}, u32[]{:S(2)}, u32[]{:S(2)}) collective-permute-start(f32[16,128]{1,0:T(8,128)S(1)} %get-tuple-element.27), channel_id=1, source_target_pairs={{0,12},{4,8},{8,4},{12,0},{1,13},{5,9},{9,5},{13,1},{2,14},{6,10},... | collective-permute-start | bytes 24584 | tf_op jit(solution)/shard_map/ppermute | solution.py:240
  38.0 3.7 %collective-permute-start.8 = (f32[16,128]{1,0:T(8,128)S(1)}, f32[16,128]{1,0:T(8,128)S(1)}, u32[]{:S(2)}, u32[]{:S(2)}) collective-permute-start(f32[16,128]{1,0:T(8,128)S(1)} %get-tuple-element.27), channel_id=1, source_target_pairs={{0,4},{4,0},{8,12},{12,8},{1,5},{5,1},{9,13},{13,9},{2,6},{6,2},{1... | collective-permute-start | bytes 24584 | tf_op jit(solution)/shard_map/ppermute | solution.py:240
  38.9 4.5 %collective-permute-start.9 = (f32[16,128]{1,0:T(8,128)S(1)}, f32[16,128]{1,0:T(8,128)S(1)}, u32[]{:S(2)}, u32[]{:S(2)}) collective-permute-start(f32[16,128]{1,0:T(8,128)S(1)} %get-tuple-element.27), channel_id=1, source_target_pairs={{0,8},{4,12},{8,0},{12,4},{1,9},{5,13},{9,1},{13,5},{2,10},{6,14},... | collective-permute-start | bytes 24584 | tf_op jit(solution)/shard_map/ppermute | solution.py:240
  40.1 8.1 %collective-permute-start.15 = (f32[256,256]{1,0:T(8,128)S(1)}, f32[256,256]{1,0:T(8,128)S(1)}, u32[]{:S(2)}, u32[]{:S(2)}) collective-permute-start(f32[256,256]{1,0:T(8,128)S(1)} %get-tuple-element.30), channel_id=1, source_target_pairs={{0,2},{1,3},{2,0},{3,1},{4,6},{5,7},{6,4},{7,5},{8,10},{9,11},{10,... | collective-permute-start | bytes 786440 | tf_op jit(solution)/shard_map/ppermute | solution.py:240
  43.4 2.4 %collective-permute-start.12 = (f32[16,128]{1,0:T(8,128)S(1)}, f32[16,128]{1,0:T(8,128)S(1)}, u32[]{:S(2)}, u32[]{:S(2)}) collective-permute-start(f32[16,128]{1,0:T(8,128)S(1)} %add_add_fusion.1), channel_id=1, source_target_pairs={{0,1},{1,0},{2,3},{3,2},{4,5},{5,4},{6,7},{7,6},{8,9},{9,8},{10,11... | collective-permute-start | bytes 24584 | tf_op jit(solution)/shard_map/ppermute | solution.py:240
  43.5 3.7 %collective-permute-start.13 = (f32[16,128]{1,0:T(8,128)S(1)}, f32[16,128]{1,0:T(8,128)S(1)}, u32[]{:S(2)}, u32[]{:S(2)}) collective-permute-start(f32[16,128]{1,0:T(8,128)S(1)} %add_add_fusion.1), channel_id=1, source_target_pairs={{0,2},{1,3},{2,0},{3,1},{4,6},{5,7},{6,4},{7,5},{8,10},{9,11},{10,... | collective-permute-start | bytes 24584 | tf_op jit(solution)/shard_map/ppermute | solution.py:240
  45.1 3.1 %collective-permute-start.14 = (f32[16,128]{1,0:T(8,128)S(1)}, f32[16,128]{1,0:T(8,128)S(1)}, u32[]{:S(2)}, u32[]{:S(2)}) collective-permute-start(f32[16,128]{1,0:T(8,128)S(1)} %add_add_fusion.1), channel_id=1, source_target_pairs={{0,3},{1,2},{2,1},{3,0},{4,7},{5,6},{6,5},{7,4},{8,11},{9,10},{10,... | collective-permute-start | bytes 24584 | tf_op jit(solution)/shard_map/ppermute | solution.py:240
  45.4 3.1 %collective-permute-start.16 = (f32[256,256]{1,0:T(8,128)S(1)}, f32[256,256]{1,0:T(8,128)S(1)}, u32[]{:S(2)}, u32[]{:S(2)}) collective-permute-start(f32[256,256]{1,0:T(8,128)S(1)} %add.30.refs_0_), channel_id=1, source_target_pairs={{0,1},{1,0},{2,3},{3,2},{4,5},{5,4},{6,7},{7,6},{8,9},{9,8},{10,11... | collective-permute-start | bytes 786440 | tf_op jit(solution)/shard_map/ppermute | solution.py:240
  48.3 1.6 %collective-permute-start.17 = (f32[256,256]{1,0:T(8,128)S(1)}, f32[256,256]{1,0:T(8,128)S(1)}, u32[]{:S(2)}, u32[]{:S(2)}) collective-permute-start(f32[256,256]{1,0:T(8,128)S(1)} %add.31.refs_1_), channel_id=1, source_target_pairs={{0,1},{1,0},{2,3},{3,2},{4,5},{5,4},{6,7},{7,6},{8,9},{9,8},{10,11... | collective-permute-start | bytes 786440 | tf_op jit(solution)/shard_map/ppermute | solution.py:240

commit v4 on v3

--- a/solution.py
+++ b/solution.py
@@ -26,7 +26,7 @@
     return jnp.where(index < live, rows, 0.0)
 
 
-PREPARE_VMEM, NEAR_VMEM = 46, 32
+PREPARE_VMEM, OWN_VMEM, NEAR_VMEM = 62, 46, 32
 GROUP = 2
 
 
@@ -39,19 +39,38 @@
     return wave.at[pl.ds(pl.multiple_of(sector * block, block), block), :]
 
 
-def prepare_kernel(half, live, left, mine_a, mine_b, halo, left_send, src, sem):
+def prepare_kernel(half, rows_hbm, wave, left, mine_a, mine_b, halo, left_send, stage, rows_ref, sem, stage_sem):
     core, side, _ = place()
     block = halo.shape[0]
-    send = pltpu.make_async_copy(left.at[pl.ds((1 - core) * half, half)], left_send, sem.at[0])
-    send.start()
-    mine_a[...] = sector_rows(live, core * half + side, block)[...]
-    mine_b[...] = sector_rows(live, core * half + half // 2 + side, block)[...]
-    halo[...] = sector_rows(live, (1 - core) * (2 * half - 1), block)[...]
-    src[pl.ds(pl.multiple_of(core * (half + 1) * block, block), block), :] = jnp.zeros((block, src.shape[1]), BF16)
-    for i in range(half + 1):
-        rows = sector_rows(live, core * (half - 1) + i, block)[...]
-        put(src, pl.multiple_of((i + 1 - core) * block, block), rows)
-    send.wait()
+    rows = pltpu.make_async_copy(rows_hbm, rows_ref, sem.at[0])
+    rows.start()
+    wanted = (
+        (core * half + side, mine_a),
+        (core * half + half // 2 + side, mine_b),
+        ((1 - core) * (2 * half - 1), halo),
+    )
+    reads = [
+        pltpu.make_async_copy(sector_rows(wave, sector, block), ref, sem.at[i + 1])
+        for i, (sector, ref) in enumerate(wanted)
+    ]
+    pieces = [
+        (
+            pltpu.make_async_copy(left.at[(1 - core) * half + s], stage.at[s], stage_sem.at[0, s]),
+            pltpu.make_async_copy(stage.at[s], left_send.at[s], stage_sem.at[1, s]),
+        )
+        for s in range(half)
+    ]
+    for move in reads + [piece[0] for piece in pieces]:
+        move.start()
+    rows.wait()
+    for move, (sector, ref) in zip(reads, wanted):
+        move.wait()
+        ref[...] = masked(ref[...], rows_ref[sector])
+    for read, write in pieces:
+        read.wait()
+        write.start()
+    for _, write in pieces:
+        write.wait()
 
 
 def put(src, at, value):
@@ -77,7 +96,7 @@
     return n
 
 
-def add_terms(n, order, offsets, src, left, right, first, acc, tbuf):
+def add_terms(n, order, offsets, src, left, right, first, acc, tbuf, right_ready=None, left_ready=None):
     rows = acc.shape[0]
     block = left.shape[-1]
     count = rows // block
@@ -89,6 +108,12 @@
             k = jnp.minimum(i * GROUP + j, n - 1)
             real.append(i * GROUP + j < n)
             terms.append(order[k])
+            if right_ready is not None:
+
+                @pl.when(real[j])
+                def _(j=j):
+                    right_ready(terms[j])
+
             at = pl.ds(pl.multiple_of(offsets[k], block), rows)
             high, low = split(right[terms[j]])
             wide = jnp.concatenate([high, high, low], 0)
@@ -97,6 +122,8 @@
                 here = slice(s * block, (s + 1) * block)
                 tbuf[s, j * block : (j + 1) * block, :] = high[here]
                 tbuf[s, (GROUP + j) * block : (GROUP + j + 1) * block, :] = low[here]
+        if left_ready is not None:
+            pl.when(i == 0)(left_ready)
         for s in range(count):
             blocks = [left[first + s, terms[0]]]
             for j in range(1, GROUP):
@@ -111,49 +138,68 @@
 
 def near_kernel(own, *refs):
     if own:
-        cls, left, right, src, acc, *rest = refs
+        cls, left_hbm, right_hbm, rows_hbm, whole, wave, acc, left, right, src, live, rows_ref, load, *rest = refs
     else:
-        cls, left, right, cls_own, left_own, right_own, halo, src_in, acc_in, acc, src, *rest = refs
+        cls, left, right, src, acc_in, acc, *rest = refs
     tbuf, cls_ref, order, offsets, sem = rest
-    block = left.shape[-1]
-    half = acc.shape[0] // block
+    half, terms, block, _ = left.shape
     core, _, _ = place()
 
-    fetch = [pltpu.make_async_copy(cls, cls_ref.at[0], sem.at[0])]
-    if not own:
-        fetch.append(pltpu.make_async_copy(cls_own, cls_ref.at[1], sem.at[1]))
+    fetch = [pltpu.make_async_copy(cls, cls_ref, sem.at[0])]
+    if own:
+        fetch.append(pltpu.make_async_copy(rows_hbm, rows_ref, sem.at[1]))
     for move in fetch:
         move.start()
-    halo_at = pl.multiple_of(core * (half + 1) * block, block)
     if own:
+        left_move = pltpu.make_async_copy(left_hbm.at[pl.ds(core * half, half)], left, load.at[terms])
+        right_moves = lambda t: pltpu.make_async_copy(right_hbm.at[t], right.at[t], load.at[t])
+        for t in range(terms):
+            right_moves(t).start()
+            if t == 1:
+                left_move.start()
         acc[...] = jnp.zeros_like(acc)
+        halo_at = pl.multiple_of(core * (half + 1) * block, block)
+        src[pl.ds(halo_at, block), :] = jnp.zeros((block, src.shape[1]), BF16)
     else:
         acc[...] = acc_in[...]
-        src[...] = src_in[...]
-        put(src, halo_at, halo[...])
     for move in fetch:
         move.wait()
+    if own:
+        for s in range(2 * half):
+            here = pl.ds(s * block, block)
+            live[here, :] = masked(wave[here, :], rows_ref[s])
+        for i in range(half + 1):
+            sector = core * (half - 1) + i
+            rows = masked(sector_rows(whole, sector, block)[...], rows_ref[sector])
+            put(src, pl.multiple_of((i + 1 - core) * block, block), rows)
 
     def near(c):
         at = jnp.where(c == 0, block, jnp.where(c == 3, 2 * block, 0))
         return jnp.logical_or(c == 0, c >= 3), at
 
+    n = pack(cls_ref, near, order, offsets)
     if not own:
-        edge = core * (half - 1)
-        n = pack(cls_ref.at[1], lambda c: (c == 4 - core, halo_at), order, offsets)
-        part = acc.at[pl.ds(pl.multiple_of(edge * block, block), block), :]
-        add_terms(n, order, offsets, src, left_own, right_own, core * half + edge, part, tbuf)
-    n = pack(cls_ref.at[0], near, order, offsets)
-    add_terms(n, order, offsets, src, left, right, core * half if own else 0, acc, tbuf)
+        add_terms(n, order, offsets, src, left, right, 0, acc, tbuf)
+        return
+    add_terms(n, order, offsets, src, left, right, 0, acc, tbuf, lambda t: right_moves(t).wait(), left_move.wait)
+    for t in range(terms):
+
+        @pl.when(jnp.logical_not(near(cls_ref[t])[0]))
+        def _(t=t):
+            right_moves(t).wait()
+
+    @pl.when(n == 0)
+    def _():
+        left_move.wait()
 
 
 def far_kernel(lo, shift, secs, chained, *refs):
     refs = list(refs)
-    cls, cls_pair, rows_hbm, left, right, left_pair, right_pair, live, mine, other, acc_in = refs[:11]
-    sums_in = refs.pop(11) if chained else None
-    acc, sums, src, tbuf, rows_ref, cls_ref, order, offsets, sem = refs[11:]
+    cls, cls_pair, rows_hbm, left, right, left_pair, right_pair, live, mine, other, halo, acc_in = refs[:12]
+    sums_in = refs.pop(12) if chained else None
+    acc, sums, src, tbuf, rows_ref, cls_ref, order, offsets, sem = refs[12:]
     rows, cols = acc.shape
-    half, _, block, _ = left_pair.shape
+    half, _, block, _ = left.shape
     count = rows // block
     core, side, sec = place()
     merged = mine.shape[0] == 1
@@ -170,6 +216,8 @@
         for ref, x in ((mine, side), (other, 1 - side)):
             part = ref.shape[1]
             put(src, pl.multiple_of(k * rows + x * part, part), ref[k])
+    halo_at = mine.shape[0] * rows
+    put(src, halo_at, halo[...])
     for move in moves:
         move.wait()
 
@@ -178,9 +226,14 @@
         below = jnp.logical_and(c == 2, sec >= shift)
         return jnp.logical_or(above, below), jnp.where(c == 1, 0, 0 if merged else rows)
 
-    for g, (l, r, first) in enumerate(((left, right, core * half + lo), (left_pair, right_pair, lo))):
+    for g, (l, r) in enumerate(((left, right), (left_pair, right_pair))):
         n = pack(cls_ref.at[g], far, order, offsets)
-        add_terms(n, order, offsets, src, l, r, first, acc, tbuf)
+        add_terms(n, order, offsets, src, l, r, lo, acc, tbuf)
+        n = pack(cls_ref.at[g], lambda c: (c == 4 - core, halo_at), order, offsets)
+        n = jnp.where(core == (0 if lo == 0 else 1), n, 0)
+        edge = core * (count - 1)
+        part = acc.at[pl.ds(pl.multiple_of(edge * block, block), block), :]
+        add_terms(n, order, offsets, src, l, r, lo + edge, part, tbuf)
 
     cross = jnp.zeros((8, cols), F32)
     square = jnp.zeros((8, cols), F32)
@@ -258,12 +311,9 @@
     part = half // 2
     shift = QD // sector_count
     merged = secs <= 2 * shift
-    row = jnp.arange(block, dtype=jnp.int32)
-    live = jnp.where((row < block_rows[:, None])[:, :, None], wavefunction.reshape(sector_count, block, cols), 0.0)
-    live = live.reshape(sector_count * block, cols)
-    whole = live
+    whole = wavefunction
     if reps > 1:
-        whole = lax.all_gather(live, "rep", axis=1, tiled=True)
+        whole = lax.all_gather(wavefunction, "rep", axis=1, tiled=True)
     wide = whole.shape[1]
 
     up = [(i, i - shift) for i in range(shift, secs)]
@@ -285,34 +335,44 @@
     blocks = shape(half, terms, block, block)
     source_shape = ((half + 2) * block, 3 * wide)
     cls_pair = swap(term_charge, "mpo", 1)
-    mine_a, mine_b, halo, left_send, src = pl.pallas_call(
+    mine_a, mine_b, halo, left_send = pl.pallas_call(
         functools.partial(prepare_kernel, half),
-        out_shape=(shape(block, wide),) * 3 + (blocks, jax.ShapeDtypeStruct(source_shape, BF16)),
-        in_specs=[VMEM, ANY],
-        out_specs=(VMEM,) * 5,
-        scratch_shapes=[pltpu.SemaphoreType.DMA((1,))],
+        out_shape=(shape(block, wide),) * 3 + (blocks,),
+        in_specs=[ANY] * 3,
+        out_specs=(VMEM,) * 3 + (ANY,),
+        scratch_shapes=[
+            pltpu.VMEM(blocks.shape, F32),
+            pltpu.SMEM((sector_count,), jnp.int32),
+            pltpu.SemaphoreType.DMA((4,)),
+            pltpu.SemaphoreType.DMA((2, half)),
+        ],
         compiler_params=params(PREPARE_VMEM),
         cost_estimate=cost(1, 1),
         name="prepare",
-    )(after(whole, cls_pair), left_blocks)
+    )(after(block_rows, cls_pair), whole, left_blocks)
     far_a = far(mine_a)
-    halo = lax.ppermute(halo, ("sec", "mpo"), halo_pairs)
-    right_pair = swap(right_blocks, "mpo", 1)
+    right_pair = swap(after(right_blocks, mine_a), "mpo", 1)
     left_pair = swap(left_send, "mpo", 1)
 
     lists = [pltpu.SMEM((terms,), jnp.int32)] * 2
 
     def near(own, *args):
+        outs = [shape(half * block, cols)]
+        scratch = []
+        if own:
+            outs += [blocks, shape(terms, wide, cols)]
+            outs += [jax.ShapeDtypeStruct(source_shape, BF16), shape(sector_count * block, cols)]
+            scratch = [pltpu.SMEM((sector_count,), jnp.int32), pltpu.SemaphoreType.DMA((terms + 1,))]
         return pl.pallas_call(
             functools.partial(near_kernel, own),
-            out_shape=shape(half * block, cols),
-            in_specs=[ANY] + [VMEM] * 3 if own else [ANY, VMEM, VMEM] * 2 + [VMEM] * 3,
-            out_specs=VMEM,
-            scratch_shapes=([] if own else [pltpu.VMEM(source_shape, BF16)])
-            + [pltpu.VMEM((half, 2 * GROUP * block, cols), BF16), pltpu.SMEM((2, terms), jnp.int32)]
+            out_shape=tuple(outs),
+            in_specs=[ANY] * 4 + [VMEM] * 2 if own else [ANY] + [VMEM] * 4,
+            out_specs=(VMEM,) * len(outs),
+            scratch_shapes=scratch
+            + [pltpu.VMEM((half, 2 * GROUP * block, cols), BF16), pltpu.SMEM((terms,), jnp.int32)]
             + lists
             + [pltpu.SemaphoreType.DMA((2,))],
-            compiler_params=params(NEAR_VMEM),
+            compiler_params=params(OWN_VMEM if own else NEAR_VMEM),
             cost_estimate=cost(1, 1),
             name="own_near" if own else "pair_near",
         )(*args)
@@ -322,10 +382,10 @@
         return pl.pallas_call(
             functools.partial(far_kernel, lo, shift, secs, sums is not None),
             out_shape=(shape(rows, cols), shape(16, 128)),
-            in_specs=[ANY] * 3 + [VMEM] * (8 + len(extra)),
+            in_specs=[ANY] * 3 + [VMEM] * (9 + len(extra)),
             out_specs=(VMEM, VMEM),
             scratch_shapes=[
-                pltpu.VMEM((far[0].shape[0] * rows, 3 * wide), BF16),
+                pltpu.VMEM((far[0].shape[0] * rows + block, 3 * wide), BF16),
                 pltpu.VMEM((part, 2 * GROUP * block, cols), BF16),
                 pltpu.SMEM((sector_count,), jnp.int32),
                 pltpu.SMEM((2, terms), jnp.int32),
@@ -335,11 +395,14 @@
             compiler_params=params(32),
             cost_estimate=cost(1, 1),
             name="far",
-        )(term_charge, cls_pair, block_rows, left_blocks, right_blocks, left_pair, right_pair, live, *far, acc, *extra)
-
-    acc = near(True, term_charge, left_blocks, right_blocks, src)
+        )(term_charge, cls_pair, block_rows, left, right, left_pair, right_pair, live, *far, halo, acc, *extra)
+
+    acc, left, right, src, live = near(
+        True, term_charge, left_blocks, right_blocks, after(block_rows, mine_a), whole, wavefunction
+    )
     far_b = far(after(mine_b, acc))
-    acc = near(False, cls_pair, left_pair, right_pair, term_charge, left_blocks, right_blocks, halo, src, acc)
+    halo = lax.ppermute(after(halo, acc), ("sec", "mpo"), halo_pairs)
+    (acc,) = near(False, cls_pair, left_pair, right_pair, src, acc)
     other_a = swap(after(far_a, acc), "mpo", 2)
     other_b = swap(after(far_b, acc), "mpo", 2)
     part_a, sums = add_far(0, (far_a, other_a), acc, None)

time: 51 us -> 49.5 us (0.971)
  Pallas kernels: 14.1 us -> 19.2 us
  starting transfers between devices: 21.6 us -> 18.8 us
  other arithmetic: 2.38 us -> 0.08 us
  waiting for transfers between devices: 12.4 us -> 10.5 us
    ppermute x15, starting transfers between devices: 14 us -> 11 us  [swap(): return lax.ppermute(array, axis, pairs)]
    pallas_call x2, Pallas kernels: 6.95 us -> 8.96 us  [near(): pl.pallas_call(functools.partial(near_kernel, own), out_shape=tuple(outs)...]
    pallas_call x1, Pallas kernels: 1.77 us -> 3.64 us  [local(): pl.pallas_call(functools.partial(prepare_kernel, half), out_shape=(shape(...]
    select_n x1 -> x0, other arithmetic: 1.57 us -> none  [local(): jnp.where((row < block_rows[:, None])[:, :, None], wavefunction.reshape(s...]
    pallas_call x2, Pallas kernels: 4.01 us -> 5.24 us  [add_far(): pl.pallas_call(functools.partial(far_kernel, lo, shift, secs, sums is not...]
    ppermute x15, waiting for transfers between devices: 8.9 us -> 7.69 us  [swap(): return lax.ppermute(array, axis, pairs)]
    ppermute x2, starting transfers between devices: 3.05 us -> 3.97 us  [far(): return lax.ppermute(array, 'sec', up + down)[None]]
    ppermute x1, starting transfers between devices: 4.55 us -> 3.79 us  [local(): halo = lax.ppermute(after(halo, acc), ('sec', 'mpo'), halo_pairs)]
  transfers between devices with their start and end apart: 18 -> 18, of which waited for: 9 -> 6; matrix products, arithmetic and copies ran while one was open for 5% -> 0% of each run, Pallas kernels for 25% -> 29%
where the time goes in v4:
time: 49.5 us
  Pallas kernels  19.2 us (39%)
  starting transfers between devices  18.8 us (38%)
  waiting for transfers between devices  10.5 us (21%)
  between operations  0.81 us (2%)
    ppermute x15, starting transfers between devices, swap(): return lax.ppermute(array, axis, pairs)  11 us
    pallas_call x2, Pallas kernels, near(): pl.pallas_call(functools.partial(near_kernel, own), out_shape=tuple(outs)...  8.96 us
    ppermute x15, waiting for transfers between devices, swap(): return lax.ppermute(array, axis, pairs)  7.69 us
    pallas_call x2, Pallas kernels, add_far(): pl.pallas_call(functools.partial(far_kernel, lo, shift, secs, sums is not...  5.24 us
    ppermute x2, starting transfers between devices, far(): return lax.ppermute(array, 'sec', up + down)[None]  3.97 us
    ppermute x1, starting transfers between devices, local(): halo = lax.ppermute(after(halo, acc), ('sec', 'mpo'), halo_pairs)  3.79 us
    pallas_call x1, Pallas kernels, local(): pl.pallas_call(functools.partial(prepare_kernel, half), out_shape=(shape(...  3.64 us
    ppermute x2, waiting for transfers between devices, far(): return lax.ppermute(array, 'sec', up + down)[None]  2.85 us
  transfers between devices with their start and end apart: 18, of which 6 were waited for; matrix products, arithmetic and copies ran while one was open for 0% of the time, Pallas kernels for 29%

profile of v4, /device:TPU:0, one launch (start us, length us, event | category | flops | bytes accessed | tf_op | source)
XLA Modules:
  0.0 49.5 jit_solution(14809701551379903849)
XLA Ops:
  0.6 0.0 copy-start.2
  0.6 0.0 copy-start.1
  0.6 0.0 copy-start
  0.7 0.5 %collective-permute-start = (s32[8]{0:T(128)}, s32[8]{0:T(128)S(1)}, u32[]{:S(2)}, u32[]{:S(2)}) collective-permute-start(s32[8]{0:T(128)} %refs_0_.5), channel_id=1, source_target_pairs={{0,1},{1,0},{2,3},{3,2},{4,5},{5,4},{6,7},{7,6},{8,9},{9,8},{10,11... | collective-permute-start | bytes 104 | tf_op jit(solution)/shard_map/ppermute | solution.py:293
  1.2 1.0 %collective-permute-done.refs_0_.refs_1_ = s32[8]{0:T(128)S(1)} collective-permute-done((s32[8]{0:T(128)}, s32[8]{0:T(128)S(1)}, u32[]{:S(2)}, u32[]{:S(2)}) %collective-permute-start) | collective-permute-done | bytes 64 | tf_op jit(solution)/shard_map/ppermute | solution.py:293
  2.1 3.6 %prepare.1 = (f32[128,256]{1,0:T(8,128)}, f32[128,256]{1,0:T(8,128)}, f32[128,256]{1,0:T(8,128)}, f32[4,8,128,128]{3,2,1,0:T(8,128)}) custom-call(s32[8]{0:T(128)} %refs_2_.5, f32[1024,256]{1,0:T(8,128)} %refs_5_.1, f32[8,8,128,128]{3,2,1,0:T(8,128)} %refs_1_.1), custom_call_target="tpu_custom_call" | custom-call | flops 1 | bytes 1 | tf_op jit(solution)/shard_map/prepare/pallas_call | solution.py:338
  5.8 0.4 collective-permute-start.2
  6.2 0.2 collective-permute-start.1
  6.4 3.9 %collective-permute-start.6 = (f32[128,256]{1,0:T(8,128)}, f32[128,256]{1,0:T(8,128)S(1)}, u32[]{:S(2)}, u32[]{:S(2)}) collective-permute-start(f32[128,256]{1,0:T(8,128)} %get-tuple-element.25), channel_id=1, source_target_pairs={{8,0},{12,4},{0,8},{4,12},{9,1},{13,5},{1,9},{5,13},{10,2},{14,6},... | collective-permute-start | bytes 393224 | tf_op jit(solution)/shard_map/ppermute | solution.py:324
  10.3 0.0 copy-done
  10.3 5.7 %own_near.1 = (f32[512,256]{1,0:T(8,128)S(1)}, f32[4,8,128,128]{3,2,1,0:T(8,128)S(1)}, f32[8,256,256]{2,1,0:T(8,128)S(1)}, bf16[768,768]{1,0:T(8,128)(2,1)S(1)}, f32[1024,256]{1,0:T(8,128)S(1)}) custom-call(s32[8]{0:T(128)S(1)} %copy-done.2, f32[8,8,128,128]{3,2,1,0:T(8,128)} %refs_1_.1, f32[8,256,256]{2,1,0:T(8,128)} %refs_2_.3, s32[8]{0:T(128)S(1)} %copy-done.1, ...), custom_call_target="tpu_custom_call" | custom-call | flops 1 | bytes 1 | tf_op jit(solution)/shard_map/own_near/pallas_call | solution.py:366
  16.0 0.0 copy-done.4
  16.0 0.1 collective-permute-start.3
  16.0 0.0 copy-done.3
  16.1 3.8 %collective-permute-start.5 = (f32[128,256]{1,0:T(8,128)S(1)}, f32[128,256]{1,0:T(8,128)S(1)}, u32[]{:S(2)}, u32[]{:S(2)}) collective-permute-start(f32[128,256]{1,0:T(8,128)S(1)} %copy-done.3), channel_id=1, source_target_pairs={{0,4},{4,8},{8,12},{5,1},{9,5},{13,9},{2,6},{6,10},{10,14},{7,3},{... | collective-permute-start | bytes 393224 | tf_op jit(solution)/shard_map/ppermute | solution.py:404
  19.9 0.0 collective-permute-done.2.refs_2_.refs_6_
  19.9 0.0 collective-permute-done.1.refs_1_.refs_5_
  19.9 3.3 %pair_near.1.refs_11_ = f32[512,256]{1,0:T(8,128)S(1)} custom-call(s32[8]{0:T(128)S(1)} %collective-permute-done.refs_0_.refs_1_, f32[4,8,128,128]{3,2,1,0:T(8,128)S(1)} %collective-permute-done.1.refs_1_.refs_5_, f32[8,256,256]{2,1,0:T(8,128)S(1)} %collective-permute-done.2.refs_2_.refs_6_, bf16[768,768]{1,0:T(8,128)(2,1)S(1)} %get-tuple-element.35.refs_3_, ...), custom_call_target="tpu_custom_call" | custom-call | flops 1 | bytes 1 | tf_op jit(solution)/shard_map/pair_near/pallas_call | solution.py:366
  23.1 0.0 collective-permute-done.6
  23.2 0.1 collective-permute-start.7
  23.2 2.8 %collective-permute-done.3 = f32[128,256]{1,0:T(8,128)S(1)} collective-permute-done((f32[128,256]{1,0:T(8,128)S(1)}, f32[128,256]{1,0:T(8,128)S(1)}, u32[]{:S(2)}, u32[]{:S(2)}) %collective-permute-start.3) | collective-permute-done | bytes 131104 | tf_op jit(solution)/shard_map/ppermute | solution.py:324
  26.1 0.2 collective-permute-start.4
  26.3 0.0 collective-permute-done.5.refs_10_
  26.3 2.9 %collective-permute-done.7.refs_9_ = f32[1,128,256]{2,1,0:T(8,128)S(1)} collective-permute-done((f32[1,128,256]{2,1,0:T(8,128)S(1)}, f32[1,128,256]{2,1,0:T(8,128)S(1)}, u32[]{:S(2)}, u32[]{:S(2)}) %collective-permute-start.7) | collective-permute-done | bytes 131104 | tf_op jit(solution)/shard_map/ppermute | solution.py:293
  29.3 3.1 %far.2 = (f32[256,256]{1,0:T(8,128)S(1)}, f32[16,128]{1,0:T(8,128)S(1)}) custom-call(s32[8]{0:T(128)S(1)} %copy-done.2, s32[8]{0:T(128)S(1)} %collective-permute-done.refs_0_.refs_1_, s32[8]{0:T(128)S(1)} %copy-done.1, f32[4,8,128,128]{3,2,1,0:T(8,128)S(1)} %get-tuple-element.27.refs_3_, f32[8,256,256]{2,1,0:T(8,128)S(1)} %get-tuple-element.28.refs_4_, ...), custom_call_target="tpu_custom_call" | custom-call | flops 1 | bytes 1 | tf_op jit(solution)/shard_map/far/pallas_call | solution.py:382
  32.4 0.3 collective-permute-start.11
  32.7 0.0 collective-permute-done.4.refs_9_
  32.7 2.1 %far.3 = (f32[256,256]{1,0:T(8,128)S(1)}, f32[16,128]{1,0:T(8,128)S(1)}) custom-call(s32[8]{0:T(128)S(1)} %copy-done.2, s32[8]{0:T(128)S(1)} %collective-permute-done.refs_0_.refs_1_, s32[8]{0:T(128)S(1)} %copy-done.1, f32[4,8,128,128]{3,2,1,0:T(8,128)S(1)} %get-tuple-element.27.refs_3_, f32[8,256,256]{2,1,0:T(8,128)S(1)} %get-tuple-element.28.refs_4_, ...), custom_call_target="tpu_custom_call" | custom-call | flops 1 | bytes 1 | tf_op jit(solution)/shard_map/far/pallas_call | solution.py:382
  34.8 1.9 %collective-permute-start.10 = (f32[16,128]{1,0:T(8,128)S(1)}, f32[16,128]{1,0:T(8,128)S(1)}, u32[]{:S(2)}, u32[]{:S(2)}) collective-permute-start(f32[16,128]{1,0:T(8,128)S(1)} %get-tuple-element.41), channel_id=1, source_target_pairs={{0,12},{4,8},{8,4},{12,0},{1,13},{5,9},{9,5},{13,1},{2,14},{6,10},... | collective-permute-start | bytes 24584 | tf_op jit(solution)/shard_map/ppermute | solution.py:293
  36.7 1.2 %collective-permute-start.9 = (f32[16,128]{1,0:T(8,128)S(1)}, f32[16,128]{1,0:T(8,128)S(1)}, u32[]{:S(2)}, u32[]{:S(2)}) collective-permute-start(f32[16,128]{1,0:T(8,128)S(1)} %get-tuple-element.41), channel_id=1, source_target_pairs={{0,8},{4,12},{8,0},{12,4},{1,9},{5,13},{9,1},{13,5},{2,10},{6,14},... | collective-permute-start | bytes 24584 | tf_op jit(solution)/shard_map/ppermute | solution.py:293
  38.0 1.3 %collective-permute-start.8 = (f32[16,128]{1,0:T(8,128)S(1)}, f32[16,128]{1,0:T(8,128)S(1)}, u32[]{:S(2)}, u32[]{:S(2)}) collective-permute-start(f32[16,128]{1,0:T(8,128)S(1)} %get-tuple-element.41), channel_id=1, source_target_pairs={{0,4},{4,0},{8,12},{12,8},{1,5},{5,1},{9,13},{13,9},{2,6},{6,2},{1... | collective-permute-start | bytes 24584 | tf_op jit(solution)/shard_map/ppermute | solution.py:293
  39.2 2.5 %collective-permute-start.15 = (f32[256,256]{1,0:T(8,128)S(1)}, f32[256,256]{1,0:T(8,128)S(1)}, u32[]{:S(2)}, u32[]{:S(2)}) collective-permute-start(f32[256,256]{1,0:T(8,128)S(1)} %get-tuple-element.44), channel_id=1, source_target_pairs={{0,2},{1,3},{2,0},{3,1},{4,6},{5,7},{6,4},{7,5},{8,10},{9,11},{10,... | collective-permute-start | bytes 786440 | tf_op jit(solution)/shard_map/ppermute | solution.py:293
  41.7 0.0 collective-permute-done.10
  41.7 0.0 collective-permute-done.9
  41.7 0.0 collective-permute-done.8
  41.7 0.0 collective-permute-done.11
  41.8 0.1 collective-permute-start.14
  41.8 1.7 %collective-permute-start.13 = (f32[16,128]{1,0:T(8,128)S(1)}, f32[16,128]{1,0:T(8,128)S(1)}, u32[]{:S(2)}, u32[]{:S(2)}) collective-permute-start(f32[16,128]{1,0:T(8,128)S(1)} %add_add_fusion.1), channel_id=1, source_target_pairs={{0,2},{1,3},{2,0},{3,1},{4,6},{5,7},{6,4},{7,5},{8,10},{9,11},{10,... | collective-permute-start | bytes 24584 | tf_op jit(solution)/shard_map/ppermute | solution.py:293
  43.5 0.2 collective-permute-start.12
  43.7 0.4 collective-permute-start.16
  44.1 1.8 %collective-permute-done.14 = f32[16,128]{1,0:T(8,128)S(1)} collective-permute-done((f32[16,128]{1,0:T(8,128)S(1)}, f32[16,128]{1,0:T(8,128)S(1)}, u32[]{:S(2)}, u32[]{:S(2)}) %collective-permute-start.14) | collective-permute-done | bytes 8224 | tf_op jit(solution)/shard_map/ppermute | solution.py:293
  45.9 0.5 %collective-permute-done.13 = f32[16,128]{1,0:T(8,128)S(1)} collective-permute-done((f32[16,128]{1,0:T(8,128)S(1)}, f32[16,128]{1,0:T(8,128)S(1)}, u32[]{:S(2)}, u32[]{:S(2)}) %collective-permute-start.13) | collective-permute-done | bytes 8224 | tf_op jit(solution)/shard_map/ppermute | solution.py:293
  46.4 0.0 collective-permute-done.12
  46.4 0.0 collective-permute-done.15
  46.5 0.1 collective-permute-start.17
  46.6 0.0 collective-permute-done.16.refs_2_
  46.6 1.5 %collective-permute-done.17.refs_3_ = f32[256,256]{1,0:T(8,128)S(1)} collective-permute-done((f32[256,256]{1,0:T(8,128)S(1)}, f32[256,256]{1,0:T(8,128)S(1)}, u32[]{:S(2)}, u32[]{:S(2)}) %collective-permute-start.17) | collective-permute-done | bytes 262176 | tf_op jit(solution)/shard_map/ppermute | solution.py:293
  48.1 1.4 %residual.1 = (f32[1024,256]{1,0:T(8,128)}, f32[1024,256]{1,0:T(8,128)}) custom-call(f32[16,128]{1,0:T(8,128)S(1)} %add_add_fusion.sums, f32[1024,256]{1,0:T(8,128)S(1)} %get-tuple-element.31.refs_7_.live, f32[256,256]{1,0:T(8,128)S(1)} %add.30.refs_0_, f32[256,256]{1,0:T(8,128)S(1)} %add.31.refs_1_, f32[256,256]{1,0:T(8,128)S(1)} %collective-permute-done.16.refs_2_, ...), custom_call_target="tpu_custom_call" | custom-call | flops 1 | bytes 1 | tf_op jit(solution)/shard_map/residual/pallas_call | solution.py:424
  (8 shorter events, 0.1 us)
Async XLA Ops:
  0.6 9.6 %copy-start.2 = (s32[8]{0:T(128)S(1)}, s32[8]{0:T(128)}, u32[]{:S(2)}) copy-start(s32[8]{0:T(128)} %refs_0_.5) | copy-start | bytes 100
  0.6 9.6 %copy-start.1 = (s32[8]{0:T(128)S(1)}, s32[8]{0:T(128)}, u32[]{:S(2)}) copy-start(s32[8]{0:T(128)} %refs_2_.5) | copy-start | bytes 100
  0.6 9.6 %copy-start = (f32[1024,256]{1,0:T(8,128)S(1)}, f32[1024,256]{1,0:T(8,128)}, u32[]{:S(2)}) copy-start(f32[1024,256]{1,0:T(8,128)} %refs_5_.1) | copy-start | bytes 3145732
  0.7 1.5 %collective-permute-start = (s32[8]{0:T(128)}, s32[8]{0:T(128)S(1)}, u32[]{:S(2)}, u32[]{:S(2)}) collective-permute-start(s32[8]{0:T(128)} %refs_0_.5), channel_id=1, source_target_pairs={{0,1},{1,0},{2,3},{3,2},{4,5},{5,4},{6,7},{7,6},{8,9},{9,8},{10,11... | collective-permute-start | bytes 104 | tf_op jit(solution)/shard_map/ppermute | solution.py:293
  5.8 14.1 %collective-permute-start.2 = (f32[8,256,256]{2,1,0:T(8,128)}, f32[8,256,256]{2,1,0:T(8,128)S(1)}, u32[]{:S(2)}, u32[]{:S(2)}) collective-permute-start(f32[8,256,256]{2,1,0:T(8,128)} %refs_2_.3), channel_id=1, source_target_pairs={{0,1},{1,0},{2,3},{3,2},{4,5},{5,4},{6,7},{7,6},{8,9},{9,8},{10,11... | collective-permute-start | bytes 6291464 | tf_op jit(solution)/shard_map/ppermute | solution.py:293
  6.1 9.8 %copy-start.4 = (f32[128,256]{1,0:T(8,128)S(1)}, f32[128,256]{1,0:T(8,128)}, u32[]{:S(2)}) copy-start(f32[128,256]{1,0:T(8,128)} %get-tuple-element.34) | copy-start | bytes 393220
  6.2 9.9 %copy-start.3 = (f32[128,256]{1,0:T(8,128)S(1)}, f32[128,256]{1,0:T(8,128)}, u32[]{:S(2)}) copy-start(f32[128,256]{1,0:T(8,128)} %get-tuple-element.38) | copy-start | bytes 393220
  6.2 13.7 %collective-permute-start.1 = (f32[4,8,128,128]{3,2,1,0:T(8,128)}, f32[4,8,128,128]{3,2,1,0:T(8,128)S(1)}, u32[]{:S(2)}, u32[]{:S(2)}) collective-permute-start(f32[4,8,128,128]{3,2,1,0:T(8,128)} %get-tuple-element.29), channel_id=1, source_target_pairs={{0,1},{1,0},{2,3},{3,2},{4,5},{5,4},{6,7},{7,6},{8,9},{9,8},{10,11... | collective-permute-start | bytes 6291464 | tf_op jit(solution)/shard_map/ppermute | solution.py:293
  6.4 16.8 %collective-permute-start.6 = (f32[128,256]{1,0:T(8,128)}, f32[128,256]{1,0:T(8,128)S(1)}, u32[]{:S(2)}, u32[]{:S(2)}) collective-permute-start(f32[128,256]{1,0:T(8,128)} %get-tuple-element.25), channel_id=1, source_target_pairs={{8,0},{12,4},{0,8},{4,12},{9,1},{13,5},{1,9},{5,13},{10,2},{14,6},... | collective-permute-start | bytes 393224 | tf_op jit(solution)/shard_map/ppermute | solution.py:324
  16.0 10.1 %collective-permute-start.3 = (f32[128,256]{1,0:T(8,128)S(1)}, f32[128,256]{1,0:T(8,128)S(1)}, u32[]{:S(2)}, u32[]{:S(2)}) collective-permute-start(f32[128,256]{1,0:T(8,128)S(1)} %copy-done.4), channel_id=1, source_target_pairs={{8,0},{12,4},{0,8},{4,12},{9,1},{13,5},{1,9},{5,13},{10,2},{14,6},... | collective-permute-start | bytes 393224 | tf_op jit(solution)/shard_map/ppermute | solution.py:324
  16.1 10.3 %collective-permute-start.5 = (f32[128,256]{1,0:T(8,128)S(1)}, f32[128,256]{1,0:T(8,128)S(1)}, u32[]{:S(2)}, u32[]{:S(2)}) collective-permute-start(f32[128,256]{1,0:T(8,128)S(1)} %copy-done.3), channel_id=1, source_target_pairs={{0,4},{4,8},{8,12},{5,1},{9,5},{13,9},{2,6},{6,10},{10,14},{7,3},{... | collective-permute-start | bytes 393224 | tf_op jit(solution)/shard_map/ppermute | solution.py:404
  23.2 6.1 %collective-permute-start.7 = (f32[1,128,256]{2,1,0:T(8,128)S(1)}, f32[1,128,256]{2,1,0:T(8,128)S(1)}, u32[]{:S(2)}, u32[]{:S(2)}) collective-permute-start(f32[1,128,256]{2,1,0:T(8,128)S(1)} %bitcast.4), channel_id=1, source_target_pairs={{0,2},{1,3},{2,0},{3,1},{4,6},{5,7},{6,4},{7,5},{8,10},{9,11},{10,... | collective-permute-start | bytes 393224 | tf_op jit(solution)/shard_map/ppermute | solution.py:293
  26.1 6.6 %collective-permute-start.4 = (f32[1,128,256]{2,1,0:T(8,128)S(1)}, f32[1,128,256]{2,1,0:T(8,128)S(1)}, u32[]{:S(2)}, u32[]{:S(2)}) collective-permute-start(f32[1,128,256]{2,1,0:T(8,128)S(1)} %bitcast.2), channel_id=1, source_target_pairs={{0,2},{1,3},{2,0},{3,1},{4,6},{5,7},{6,4},{7,5},{8,10},{9,11},{10,... | collective-permute-start | bytes 393224 | tf_op jit(solution)/shard_map/ppermute | solution.py:293
  32.4 9.3 %collective-permute-start.11 = (f32[256,256]{1,0:T(8,128)S(1)}, f32[256,256]{1,0:T(8,128)S(1)}, u32[]{:S(2)}, u32[]{:S(2)}) collective-permute-start(f32[256,256]{1,0:T(8,128)S(1)} %get-tuple-element.42), channel_id=1, source_target_pairs={{0,2},{1,3},{2,0},{3,1},{4,6},{5,7},{6,4},{7,5},{8,10},{9,11},{10,... | collective-permute-start | bytes 786440 | tf_op jit(solution)/shard_map/ppermute | solution.py:293
  34.8 6.9 %collective-permute-start.10 = (f32[16,128]{1,0:T(8,128)S(1)}, f32[16,128]{1,0:T(8,128)S(1)}, u32[]{:S(2)}, u32[]{:S(2)}) collective-permute-start(f32[16,128]{1,0:T(8,128)S(1)} %get-tuple-element.41), channel_id=1, source_target_pairs={{0,12},{4,8},{8,4},{12,0},{1,13},{5,9},{9,5},{13,1},{2,14},{6,10},... | collective-permute-start | bytes 24584 | tf_op jit(solution)/shard_map/ppermute | solution.py:293
  36.7 5.0 %collective-permute-start.9 = (f32[16,128]{1,0:T(8,128)S(1)}, f32[16,128]{1,0:T(8,128)S(1)}, u32[]{:S(2)}, u32[]{:S(2)}) collective-permute-start(f32[16,128]{1,0:T(8,128)S(1)} %get-tuple-element.41), channel_id=1, source_target_pairs={{0,8},{4,12},{8,0},{12,4},{1,9},{5,13},{9,1},{13,5},{2,10},{6,14},... | collective-permute-start | bytes 24584 | tf_op jit(solution)/shard_map/ppermute | solution.py:293
  38.0 3.8 %collective-permute-start.8 = (f32[16,128]{1,0:T(8,128)S(1)}, f32[16,128]{1,0:T(8,128)S(1)}, u32[]{:S(2)}, u32[]{:S(2)}) collective-permute-start(f32[16,128]{1,0:T(8,128)S(1)} %get-tuple-element.41), channel_id=1, source_target_pairs={{0,4},{4,0},{8,12},{12,8},{1,5},{5,1},{9,13},{13,9},{2,6},{6,2},{1... | collective-permute-start | bytes 24584 | tf_op jit(solution)/shard_map/ppermute | solution.py:293
  39.2 7.2 %collective-permute-start.15 = (f32[256,256]{1,0:T(8,128)S(1)}, f32[256,256]{1,0:T(8,128)S(1)}, u32[]{:S(2)}, u32[]{:S(2)}) collective-permute-start(f32[256,256]{1,0:T(8,128)S(1)} %get-tuple-element.44), channel_id=1, source_target_pairs={{0,2},{1,3},{2,0},{3,1},{4,6},{5,7},{6,4},{7,5},{8,10},{9,11},{10,... | collective-permute-start | bytes 786440 | tf_op jit(solution)/shard_map/ppermute | solution.py:293
  41.8 4.1 %collective-permute-start.14 = (f32[16,128]{1,0:T(8,128)S(1)}, f32[16,128]{1,0:T(8,128)S(1)}, u32[]{:S(2)}, u32[]{:S(2)}) collective-permute-start(f32[16,128]{1,0:T(8,128)S(1)} %add_add_fusion.1), channel_id=1, source_target_pairs={{0,3},{1,2},{2,1},{3,0},{4,7},{5,6},{6,5},{7,4},{8,11},{9,10},{10,... | collective-permute-start | bytes 24584 | tf_op jit(solution)/shard_map/ppermute | solution.py:293
  41.8 4.6 %collective-permute-start.13 = (f32[16,128]{1,0:T(8,128)S(1)}, f32[16,128]{1,0:T(8,128)S(1)}, u32[]{:S(2)}, u32[]{:S(2)}) collective-permute-start(f32[16,128]{1,0:T(8,128)S(1)} %add_add_fusion.1), channel_id=1, source_target_pairs={{0,2},{1,3},{2,0},{3,1},{4,6},{5,7},{6,4},{7,5},{8,10},{9,11},{10,... | collective-permute-start | bytes 24584 | tf_op jit(solution)/shard_map/ppermute | solution.py:293
  43.5 2.9 %collective-permute-start.12 = (f32[16,128]{1,0:T(8,128)S(1)}, f32[16,128]{1,0:T(8,128)S(1)}, u32[]{:S(2)}, u32[]{:S(2)}) collective-permute-start(f32[16,128]{1,0:T(8,128)S(1)} %add_add_fusion.1), channel_id=1, source_target_pairs={{0,1},{1,0},{2,3},{3,2},{4,5},{5,4},{6,7},{7,6},{8,9},{9,8},{10,11... | collective-permute-start | bytes 24584 | tf_op jit(solution)/shard_map/ppermute | solution.py:293
  43.7 2.9 %collective-permute-start.16 = (f32[256,256]{1,0:T(8,128)S(1)}, f32[256,256]{1,0:T(8,128)S(1)}, u32[]{:S(2)}, u32[]{:S(2)}) collective-permute-start(f32[256,256]{1,0:T(8,128)S(1)} %add.30.refs_0_), channel_id=1, source_target_pairs={{0,1},{1,0},{2,3},{3,2},{4,5},{5,4},{6,7},{7,6},{8,9},{9,8},{10,11... | collective-permute-start | bytes 786440 | tf_op jit(solution)/shard_map/ppermute | solution.py:293
  46.5 1.6 %collective-permute-start.17 = (f32[256,256]{1,0:T(8,128)S(1)}, f32[256,256]{1,0:T(8,128)S(1)}, u32[]{:S(2)}, u32[]{:S(2)}) collective-permute-start(f32[256,256]{1,0:T(8,128)S(1)} %add.31.refs_1_), channel_id=1, source_target_pairs={{0,1},{1,0},{2,3},{3,2},{4,5},{5,4},{6,7},{7,6},{8,9},{9,8},{10,11... | collective-permute-start | bytes 786440 | tf_op jit(solution)/shard_map/ppermute | solution.py:293

commit v5 on v4

--- a/solution.py
+++ b/solution.py
@@ -26,7 +26,7 @@
     return jnp.where(index < live, rows, 0.0)
 
 
-PREPARE_VMEM, OWN_VMEM, NEAR_VMEM = 62, 46, 32
+PREPARE_VMEM, CUT_VMEM, OWN_VMEM, NEAR_VMEM = 62, 50, 46, 32
 GROUP = 2
 
 
@@ -39,38 +39,37 @@
     return wave.at[pl.ds(pl.multiple_of(sector * block, block), block), :]
 
 
-def prepare_kernel(half, rows_hbm, wave, left, mine_a, mine_b, halo, left_send, stage, rows_ref, sem, stage_sem):
+def prepare_kernel(half, rows_hbm, wave, *refs):
+    *sends, halo, rows_ref, sem = refs
     core, side, _ = place()
     block = halo.shape[0]
+    piece = block // 2
     rows = pltpu.make_async_copy(rows_hbm, rows_ref, sem.at[0])
     rows.start()
-    wanted = (
-        (core * half + side, mine_a),
-        (core * half + half // 2 + side, mine_b),
-        ((1 - core) * (2 * half - 1), halo),
-    )
-    reads = [
-        pltpu.make_async_copy(sector_rows(wave, sector, block), ref, sem.at[i + 1])
-        for i, (sector, ref) in enumerate(wanted)
-    ]
-    pieces = [
-        (
-            pltpu.make_async_copy(left.at[(1 - core) * half + s], stage.at[s], stage_sem.at[0, s]),
-            pltpu.make_async_copy(stage.at[s], left_send.at[s], stage_sem.at[1, s]),
-        )
-        for s in range(half)
-    ]
-    for move in reads + [piece[0] for piece in pieces]:
-        move.start()
+    wanted = [(halo, (1 - core) * (2 * half - 1) * block)]
+    first = core * half * block
+    for ref in sends:
+        wanted.append((ref, first + side * ref.shape[0]))
+        first += 2 * ref.shape[0]
+    reads = []
+    for i, (ref, first) in enumerate(wanted):
+        source = wave.at[pl.ds(pl.multiple_of(first, piece), ref.shape[0]), :]
+        reads.append(pltpu.make_async_copy(source, ref, sem.at[i + 1]))
+        reads[i].start()
     rows.wait()
-    for move, (sector, ref) in zip(reads, wanted):
-        move.wait()
-        ref[...] = masked(ref[...], rows_ref[sector])
-    for read, write in pieces:
+    for read, (ref, first) in zip(reads, wanted):
         read.wait()
-        write.start()
-    for _, write in pieces:
-        write.wait()
+        for at in range(0, ref.shape[0], piece):
+            here = pl.ds(at, piece)
+            live = rows_ref[lax.div(first + at, block)] - lax.rem(first + at, block)
+            ref[here, :] = masked(ref[here, :], live)
+
+
+def cut_kernel(half, left, left_send, sem):
+    core, _, _ = place()
+    move = pltpu.make_async_copy(left.at[pl.ds((1 - core) * half, half)], left_send, sem.at[0])
+    move.start()
+    move.wait()
 
 
 def put(src, at, value):
@@ -254,23 +253,26 @@
     sums[8:16, :] = square
 
 
-def final_kernel(sides, block, sums, live, *refs):
+def final_kernel(sides, sums, live, *refs):
     totals, (applied, correction, buf, sem) = refs[:-4], refs[-4:]
     core, _, _ = place()
     half = live.shape[0] // 2
     chunks = len(totals) // 2
-    rows = totals[0].shape[0]
     places = []
     moves = []
+    at = 0
     for i, total in enumerate(totals):
-        c = core if i < chunks else 1 - core
-        places.append(pl.ds(pl.multiple_of(c * half + i % chunks * rows, rows), rows))
+        rows = total.shape[0]
+        first = (core if i < chunks else 1 - core) * half + at % half
+        at += rows
+        places.append(pl.ds(pl.multiple_of(first, 8), rows))
         moves.append(pltpu.make_async_copy(total, applied.at[places[i], :], sem.at[0, i]))
         moves[-1].start()
     rayleigh = jnp.sum(sums[0:8, :]) / (jnp.sum(sums[8:16, :]) * (1.0 / sides))
     for i, total in enumerate(totals):
-        buf[i] = total[...] - rayleigh * live[places[i], :]
-        moves.append(pltpu.make_async_copy(buf.at[i], correction.at[places[i], :], sem.at[1, i]))
+        here = places[i]
+        buf[here, :] = total[...] - rayleigh * live[here, :]
+        moves.append(pltpu.make_async_copy(buf.at[here, :], correction.at[here, :], sem.at[1, i]))
         moves[-1].start()
     for move in moves:
         move.wait()
@@ -331,28 +333,33 @@
             if 0 <= to < secs:
                 halo_pairs.append((z * mpos + m, to * mpos + m))
 
-    rows = part * block
     blocks = shape(half, terms, block, block)
     source_shape = ((half + 2) * block, 3 * wide)
+    sizes = (half // 2, half // 2)
     cls_pair = swap(term_charge, "mpo", 1)
-    mine_a, mine_b, halo, left_send = pl.pallas_call(
+    mine_a, mine_b, halo = pl.pallas_call(
         functools.partial(prepare_kernel, half),
-        out_shape=(shape(block, wide),) * 3 + (blocks,),
-        in_specs=[ANY] * 3,
-        out_specs=(VMEM,) * 3 + (ANY,),
-        scratch_shapes=[
-            pltpu.VMEM(blocks.shape, F32),
-            pltpu.SMEM((sector_count,), jnp.int32),
-            pltpu.SemaphoreType.DMA((4,)),
-            pltpu.SemaphoreType.DMA((2, half)),
-        ],
+        out_shape=tuple(shape(size * block // 2, wide) for size in sizes) + (shape(block, wide),),
+        in_specs=[ANY] * 2,
+        out_specs=(VMEM,) * 3,
+        scratch_shapes=[pltpu.SMEM((sector_count,), jnp.int32), pltpu.SemaphoreType.DMA((4,))],
         compiler_params=params(PREPARE_VMEM),
         cost_estimate=cost(1, 1),
         name="prepare",
-    )(after(block_rows, cls_pair), whole, left_blocks)
+    )(block_rows, whole)
+    (left_send,) = pl.pallas_call(
+        functools.partial(cut_kernel, half),
+        out_shape=(blocks,),
+        in_specs=[ANY],
+        out_specs=(VMEM,),
+        scratch_shapes=[pltpu.SemaphoreType.DMA((1,))],
+        compiler_params=params(CUT_VMEM),
+        cost_estimate=cost(1, 1),
+        name="pair_blocks",
+    )(after(left_blocks, mine_a, cls_pair))
+    left_pair = swap(left_send, "mpo", 1)
     far_a = far(mine_a)
     right_pair = swap(after(right_blocks, mine_a), "mpo", 1)
-    left_pair = swap(left_send, "mpo", 1)
 
     lists = [pltpu.SMEM((terms,), jnp.int32)] * 2
 
@@ -377,7 +384,8 @@
             name="own_near" if own else "pair_near",
         )(*args)
 
-    def add_far(lo, far, acc, sums):
+    def add_far(lo, count, far, acc, sums):
+        rows = count * block
         extra = () if sums is None else (sums,)
         return pl.pallas_call(
             functools.partial(far_kernel, lo, shift, secs, sums is not None),
@@ -386,7 +394,7 @@
             out_specs=(VMEM, VMEM),
             scratch_shapes=[
                 pltpu.VMEM((far[0].shape[0] * rows + block, 3 * wide), BF16),
-                pltpu.VMEM((part, 2 * GROUP * block, cols), BF16),
+                pltpu.VMEM((count, 2 * GROUP * block, cols), BF16),
                 pltpu.SMEM((sector_count,), jnp.int32),
                 pltpu.SMEM((2, terms), jnp.int32),
                 *lists,
@@ -400,14 +408,14 @@
     acc, left, right, src, live = near(
         True, term_charge, left_blocks, right_blocks, after(block_rows, mine_a), whole, wavefunction
     )
-    far_b = far(after(mine_b, acc))
+    far_b = far(mine_b)
     halo = lax.ppermute(after(halo, acc), ("sec", "mpo"), halo_pairs)
+    other_a = swap(after(far_a, acc), "mpo", 2)
     (acc,) = near(False, cls_pair, left_pair, right_pair, src, acc)
-    other_a = swap(after(far_a, acc), "mpo", 2)
     other_b = swap(after(far_b, acc), "mpo", 2)
-    part_a, sums = add_far(0, (far_a, other_a), acc, None)
+    part_a, sums = add_far(0, sizes[0], (far_a, other_a), acc, None)
     recv_a = swap(part_a, "mpo", 2)
-    part_b, sums = add_far(part, (far_b, other_b), acc, sums)
+    part_b, sums = add_far(sizes[0], sizes[1], (far_b, other_b), acc, sums)
     recv_b = swap(part_b, "mpo", 2)
 
     if secs == 4:
@@ -417,17 +425,17 @@
     if reps > 1:
         sums = lax.psum(sums, "rep")
     sums = everyone(after(sums, recv_a), "mpo")
-    totals = [part_a + recv_a, part_b + after(recv_b, sums)]
+    totals = [part_a + recv_a, part_b + recv_b]
     totals += [swap(total, "mpo", 1) for total in totals]
 
     out = shape(sector_count * block, cols)
     return pl.pallas_call(
-        functools.partial(final_kernel, mpos // 2, block),
+        functools.partial(final_kernel, mpos // 2),
         out_shape=(out, out),
         in_specs=[VMEM] * (2 + len(totals)),
         out_specs=(ANY, ANY),
         scratch_shapes=[
-            pltpu.VMEM((len(totals), rows, cols), F32),
+            pltpu.VMEM((sector_count * block, cols), F32),
             pltpu.SemaphoreType.DMA((2, len(totals))),
         ],
         compiler_params=params(32),

time: 49.5 us -> 47 us (0.949)
  waiting for transfers between devices: 10.5 us -> 6.93 us
  starting transfers between devices: 18.8 us -> 21.4 us
  Pallas kernels: 19.2 us -> 18 us
    ppermute x15, starting transfers between devices: 11 us -> 13.8 us  [swap(): return lax.ppermute(array, axis, pairs)]
    ppermute x15, waiting for transfers between devices: 7.69 us -> 5.34 us  [swap(): return lax.ppermute(array, axis, pairs)]
    pallas_call x2, Pallas kernels: 8.96 us -> 7.01 us  [near(): pl.pallas_call(functools.partial(near_kernel, own), out_shape=tuple(outs)...]
    ppermute x2, waiting for transfers between devices: 2.85 us -> 1.59 us  [far(): return lax.ppermute(array, 'sec', up + down)[None]]
    pallas_call x2, Pallas kernels: 5.24 us -> 6.02 us  [add_far(): pl.pallas_call(functools.partial(far_kernel, lo, shift, secs, sums is not...]
    pallas_call x2 -> x3, Pallas kernels: 5.02 us -> 4.93 us  [the longest x1 1.8 us: local(): pl.pallas_call(functools.partial(prepare_kernel, half), out_shape=tuple((...]
  transfers between devices with their start and end apart: 18 -> 18, of which waited for: 6 -> 4; matrix products, arithmetic and copies ran while one was open for 0% -> 0% of each run, Pallas kernels for 29% -> 35%
where the time goes in v5:
time: 47 us; the launch traced here: 47.2 us
  starting transfers between devices  21.4 us (46%)
  Pallas kernels  18 us (38%)
  waiting for transfers between devices  6.93 us (15%)
  between operations  0.83 us (2%)
    ppermute x15, starting transfers between devices, swap(): return lax.ppermute(array, axis, pairs)  13.8 us
    pallas_call x2, Pallas kernels, near(): pl.pallas_call(functools.partial(near_kernel, own), out_shape=tuple(outs)...  7.01 us
    pallas_call x2, Pallas kernels, add_far(): pl.pallas_call(functools.partial(far_kernel, lo, shift, secs, sums is not...  6.02 us
    ppermute x15, waiting for transfers between devices, swap(): return lax.ppermute(array, axis, pairs)  5.34 us
    ppermute x2, starting transfers between devices, far(): return lax.ppermute(array, 'sec', up + down)[None]  3.82 us
    ppermute x1, starting transfers between devices, local(): halo = lax.ppermute(after(halo, acc), ('sec', 'mpo'), halo_pairs)  3.73 us
    pallas_call x1, Pallas kernels, local(): pl.pallas_call(functools.partial(prepare_kernel, half), out_shape=tuple((...  1.8 us
    pallas_call x1, Pallas kernels, local(): pl.pallas_call(functools.partial(cut_kernel, half), out_shape=(blocks,),...  1.74 us
  transfers between devices with their start and end apart: 18, of which 4 were waited for; matrix products, arithmetic and copies ran while one was open for 0% of the time, Pallas kernels for 35%

profile of v5, /device:TPU:0, one launch (start us, length us, event | category | flops | bytes accessed | tf_op | source)
XLA Modules:
  0.0 47.2 jit_solution(6005854937545075538)
XLA Ops:
  0.6 0.5 %collective-permute-start = (s32[8]{0:T(128)}, s32[8]{0:T(128)S(1)}, u32[]{:S(2)}, u32[]{:S(2)}) collective-permute-start(s32[8]{0:T(128)} %refs_0_.5), channel_id=1, source_target_pairs={{0,1},{1,0},{2,3},{3,2},{4,5},{5,4},{6,7},{7,6},{8,9},{9,8},{10,11... | collective-permute-start | bytes 104 | tf_op jit(solution)/shard_map/ppermute | solution.py:295
  1.1 1.8 %prepare.1 = (f32[128,256]{1,0:T(8,128)}, f32[128,256]{1,0:T(8,128)}, f32[128,256]{1,0:T(8,128)}) custom-call(s32[8]{0:T(128)} %refs_2_.5, f32[1024,256]{1,0:T(8,128)} %refs_5_.1), custom_call_target="tpu_custom_call" | custom-call | flops 1 | bytes 1 | tf_op jit(solution)/shard_map/prepare/pallas_call | solution.py:340
  3.0 0.0 copy-start.5
  3.0 0.0 copy-start.4
  3.0 0.0 copy-start
  3.0 0.0 copy-start.1
  3.0 0.0 copy-start.2
  3.0 0.1 collective-permute-start.2
  3.1 0.0 collective-permute-done.refs_0_.refs_1_
  3.1 1.7 %pair_blocks.1 = f32[4,8,128,128]{3,2,1,0:T(8,128)S(1)} custom-call(f32[8,8,128,128]{3,2,1,0:T(8,128)} %left), custom_call_target="tpu_custom_call" | custom-call | flops 1 | bytes 1 | tf_op jit(solution)/shard_map/pair_blocks/pallas_call | solution.py:350
  4.9 0.4 collective-permute-start.1
  5.3 3.7 %collective-permute-start.6 = (f32[128,256]{1,0:T(8,128)S(1)}, f32[128,256]{1,0:T(8,128)S(1)}, u32[]{:S(2)}, u32[]{:S(2)}) collective-permute-start(f32[128,256]{1,0:T(8,128)S(1)} %copy-done.5), channel_id=1, source_target_pairs={{8,0},{12,4},{0,8},{4,12},{9,1},{13,5},{1,9},{5,13},{10,2},{14,6},... | collective-permute-start | bytes 393224 | tf_op jit(solution)/shard_map/ppermute | solution.py:326
  9.0 0.1 collective-permute-start.3
  9.1 4.6 %own_near.1 = (f32[512,256]{1,0:T(8,128)S(1)}, f32[4,8,128,128]{3,2,1,0:T(8,128)S(1)}, f32[8,256,256]{2,1,0:T(8,128)S(1)}, bf16[768,768]{1,0:T(8,128)(2,1)S(1)}, f32[1024,256]{1,0:T(8,128)S(1)}) custom-call(s32[8]{0:T(128)S(1)} %copy-done.2, f32[8,8,128,128]{3,2,1,0:T(8,128)} %left, f32[8,256,256]{2,1,0:T(8,128)} %refs_2_.3, s32[8]{0:T(128)S(1)} %copy-done.1, ...), custom_call_target="tpu_custom_call" | custom-call | flops 1 | bytes 1 | tf_op jit(solution)/shard_map/own_near/pallas_call | solution.py:373
  13.8 3.7 %collective-permute-start.5 = (f32[128,256]{1,0:T(8,128)S(1)}, f32[128,256]{1,0:T(8,128)S(1)}, u32[]{:S(2)}, u32[]{:S(2)}) collective-permute-start(f32[128,256]{1,0:T(8,128)S(1)} %copy-done.3), channel_id=1, source_target_pairs={{0,4},{4,8},{8,12},{5,1},{9,5},{13,9},{2,6},{6,10},{10,14},{7,3},{... | collective-permute-start | bytes 393224 | tf_op jit(solution)/shard_map/ppermute | solution.py:412
  17.5 1.6 %collective-permute-done.6 = f32[128,256]{1,0:T(8,128)S(1)} collective-permute-done((f32[128,256]{1,0:T(8,128)S(1)}, f32[128,256]{1,0:T(8,128)S(1)}, u32[]{:S(2)}, u32[]{:S(2)}) %collective-permute-start.6) | collective-permute-done | bytes 131104 | tf_op jit(solution)/shard_map/ppermute | solution.py:326
  19.1 1.7 %collective-permute-start.7 = (f32[1,128,256]{2,1,0:T(8,128)S(1)}, f32[1,128,256]{2,1,0:T(8,128)S(1)}, u32[]{:S(2)}, u32[]{:S(2)}) collective-permute-start(f32[1,128,256]{2,1,0:T(8,128)S(1)} %bitcast.4), channel_id=1, source_target_pairs={{0,2},{1,3},{2,0},{3,1},{4,6},{5,7},{6,4},{7,5},{8,10},{9,11},{10,... | collective-permute-start | bytes 393224 | tf_op jit(solution)/shard_map/ppermute | solution.py:295
  20.7 0.0 collective-permute-done.2.refs_2_.refs_6_
  20.8 0.0 collective-permute-done.1.refs_1_.refs_5_
  20.8 2.4 %pair_near.1.refs_11_ = f32[512,256]{1,0:T(8,128)S(1)} custom-call(s32[8]{0:T(128)S(1)} %collective-permute-done.refs_0_.refs_1_, f32[4,8,128,128]{3,2,1,0:T(8,128)S(1)} %collective-permute-done.1.refs_1_.refs_5_, f32[8,256,256]{2,1,0:T(8,128)S(1)} %collective-permute-done.2.refs_2_.refs_6_, bf16[768,768]{1,0:T(8,128)(2,1)S(1)} %get-tuple-element.29.refs_3_, ...), custom_call_target="tpu_custom_call" | custom-call | flops 1 | bytes 1 | tf_op jit(solution)/shard_map/pair_near/pallas_call | solution.py:373
  23.1 0.0 collective-permute-done.3
  23.2 2.2 %collective-permute-start.4 = (f32[1,128,256]{2,1,0:T(8,128)S(1)}, f32[1,128,256]{2,1,0:T(8,128)S(1)}, u32[]{:S(2)}, u32[]{:S(2)}) collective-permute-start(f32[1,128,256]{2,1,0:T(8,128)S(1)} %bitcast.2), channel_id=1, source_target_pairs={{0,2},{1,3},{2,0},{3,1},{4,6},{5,7},{6,4},{7,5},{8,10},{9,11},{10,... | collective-permute-start | bytes 393224 | tf_op jit(solution)/shard_map/ppermute | solution.py:295
  25.4 0.0 collective-permute-done.5.refs_10_
  25.4 0.0 collective-permute-done.7.refs_9_
  25.4 3.3 %far.2 = (f32[256,256]{1,0:T(8,128)S(1)}, f32[16,128]{1,0:T(8,128)S(1)}) custom-call(s32[8]{0:T(128)S(1)} %copy-done.2, s32[8]{0:T(128)S(1)} %collective-permute-done.refs_0_.refs_1_, s32[8]{0:T(128)S(1)} %copy-done.1, f32[4,8,128,128]{3,2,1,0:T(8,128)S(1)} %get-tuple-element.23.refs_3_, f32[8,256,256]{2,1,0:T(8,128)S(1)} %get-tuple-element.24.refs_4_, ...), custom_call_target="tpu_custom_call" | custom-call | flops 1 | bytes 1 | tf_op jit(solution)/shard_map/far/pallas_call | solution.py:390
  28.6 1.3 %collective-permute-start.11 = (f32[256,256]{1,0:T(8,128)S(1)}, f32[256,256]{1,0:T(8,128)S(1)}, u32[]{:S(2)}, u32[]{:S(2)}) collective-permute-start(f32[256,256]{1,0:T(8,128)S(1)} %get-tuple-element.37), channel_id=1, source_target_pairs={{0,2},{1,3},{2,0},{3,1},{4,6},{5,7},{6,4},{7,5},{8,10},{9,11},{10,... | collective-permute-start | bytes 786440 | tf_op jit(solution)/shard_map/ppermute | solution.py:295
  30.0 0.0 collective-permute-done.4.refs_9_
  30.0 2.7 %far.3 = (f32[256,256]{1,0:T(8,128)S(1)}, f32[16,128]{1,0:T(8,128)S(1)}) custom-call(s32[8]{0:T(128)S(1)} %copy-done.2, s32[8]{0:T(128)S(1)} %collective-permute-done.refs_0_.refs_1_, s32[8]{0:T(128)S(1)} %copy-done.1, f32[4,8,128,128]{3,2,1,0:T(8,128)S(1)} %get-tuple-element.23.refs_3_, f32[8,256,256]{2,1,0:T(8,128)S(1)} %get-tuple-element.24.refs_4_, ...), custom_call_target="tpu_custom_call" | custom-call | flops 1 | bytes 1 | tf_op jit(solution)/shard_map/far/pallas_call | solution.py:390
  32.7 0.9 %collective-permute-start.15 = (f32[256,256]{1,0:T(8,128)S(1)}, f32[256,256]{1,0:T(8,128)S(1)}, u32[]{:S(2)}, u32[]{:S(2)}) collective-permute-start(f32[256,256]{1,0:T(8,128)S(1)} %get-tuple-element.39), channel_id=1, source_target_pairs={{0,2},{1,3},{2,0},{3,1},{4,6},{5,7},{6,4},{7,5},{8,10},{9,11},{10,... | collective-permute-start | bytes 786440 | tf_op jit(solution)/shard_map/ppermute | solution.py:295
  33.6 2.5 %collective-permute-start.10 = (f32[16,128]{1,0:T(8,128)S(1)}, f32[16,128]{1,0:T(8,128)S(1)}, u32[]{:S(2)}, u32[]{:S(2)}) collective-permute-start(f32[16,128]{1,0:T(8,128)S(1)} %get-tuple-element.36), channel_id=1, source_target_pairs={{0,12},{4,8},{8,4},{12,0},{1,13},{5,9},{9,5},{13,1},{2,14},{6,10},... | collective-permute-start | bytes 24584 | tf_op jit(solution)/shard_map/ppermute | solution.py:295
  36.1 0.0 collective-permute-start.9
  36.1 1.9 %collective-permute-start.8 = (f32[16,128]{1,0:T(8,128)S(1)}, f32[16,128]{1,0:T(8,128)S(1)}, u32[]{:S(2)}, u32[]{:S(2)}) collective-permute-start(f32[16,128]{1,0:T(8,128)S(1)} %get-tuple-element.36), channel_id=1, source_target_pairs={{0,4},{4,0},{8,12},{12,8},{1,5},{5,1},{9,13},{13,9},{2,6},{6,2},{1... | collective-permute-start | bytes 24584 | tf_op jit(solution)/shard_map/ppermute | solution.py:295
  38.0 0.0 collective-permute-done.11
  38.1 0.1 collective-permute-start.16
  38.1 2.6 %collective-permute-done.15 = f32[256,256]{1,0:T(8,128)S(1)} collective-permute-done((f32[256,256]{1,0:T(8,128)S(1)}, f32[256,256]{1,0:T(8,128)S(1)}, u32[]{:S(2)}, u32[]{:S(2)}) %collective-permute-start.15) | collective-permute-done | bytes 262176 | tf_op jit(solution)/shard_map/ppermute | solution.py:295
  40.7 0.1 collective-permute-start.17
  40.8 0.0 collective-permute-done.10
  40.8 0.0 collective-permute-done.9
  40.8 0.0 collective-permute-done.8
  40.9 1.3 %collective-permute-start.14 = (f32[16,128]{1,0:T(8,128)S(1)}, f32[16,128]{1,0:T(8,128)S(1)}, u32[]{:S(2)}, u32[]{:S(2)}) collective-permute-start(f32[16,128]{1,0:T(8,128)S(1)} %add_add_fusion.1), channel_id=1, source_target_pairs={{0,3},{1,2},{2,1},{3,0},{4,7},{5,6},{6,5},{7,4},{8,11},{9,10},{10,... | collective-permute-start | bytes 24584 | tf_op jit(solution)/shard_map/ppermute | solution.py:295
  42.1 0.9 %collective-permute-start.13 = (f32[16,128]{1,0:T(8,128)S(1)}, f32[16,128]{1,0:T(8,128)S(1)}, u32[]{:S(2)}, u32[]{:S(2)}) collective-permute-start(f32[16,128]{1,0:T(8,128)S(1)} %add_add_fusion.1), channel_id=1, source_target_pairs={{0,2},{1,3},{2,0},{3,1},{4,6},{5,7},{6,4},{7,5},{8,10},{9,11},{10,... | collective-permute-start | bytes 24584 | tf_op jit(solution)/shard_map/ppermute | solution.py:295
  43.0 0.0 collective-permute-start.12
  43.0 1.0 %collective-permute-done.14 = f32[16,128]{1,0:T(8,128)S(1)} collective-permute-done((f32[16,128]{1,0:T(8,128)S(1)}, f32[16,128]{1,0:T(8,128)S(1)}, u32[]{:S(2)}, u32[]{:S(2)}) %collective-permute-start.14) | collective-permute-done | bytes 8224 | tf_op jit(solution)/shard_map/ppermute | solution.py:295
  44.0 1.8 %collective-permute-done.13 = f32[16,128]{1,0:T(8,128)S(1)} collective-permute-done((f32[16,128]{1,0:T(8,128)S(1)}, f32[16,128]{1,0:T(8,128)S(1)}, u32[]{:S(2)}, u32[]{:S(2)}) %collective-permute-start.13) | collective-permute-done | bytes 8224 | tf_op jit(solution)/shard_map/ppermute | solution.py:295
  45.8 0.0 collective-permute-done.12
  45.8 0.0 collective-permute-done.16.refs_2_
  45.8 0.0 collective-permute-done.17.refs_3_
  45.8 1.4 %residual.1 = (f32[1024,256]{1,0:T(8,128)}, f32[1024,256]{1,0:T(8,128)}) custom-call(f32[16,128]{1,0:T(8,128)S(1)} %add_add_fusion.sums, f32[1024,256]{1,0:T(8,128)S(1)} %get-tuple-element.27.refs_7_.live, f32[256,256]{1,0:T(8,128)S(1)} %add.30.refs_0_, f32[256,256]{1,0:T(8,128)S(1)} %add.31.refs_1_, f32[256,256]{1,0:T(8,128)S(1)} %collective-permute-done.16.refs_2_, ...), custom_call_target="tpu_custom_call" | custom-call | flops 1 | bytes 1 | tf_op jit(solution)/shard_map/residual/pallas_call | solution.py:432
  (11 shorter events, 0.1 us)
Async XLA Ops:
  0.6 2.5 %collective-permute-start = (s32[8]{0:T(128)}, s32[8]{0:T(128)S(1)}, u32[]{:S(2)}, u32[]{:S(2)}) collective-permute-start(s32[8]{0:T(128)} %refs_0_.5), channel_id=1, source_target_pairs={{0,1},{1,0},{2,3},{3,2},{4,5},{5,4},{6,7},{7,6},{8,9},{9,8},{10,11... | collective-permute-start | bytes 104 | tf_op jit(solution)/shard_map/ppermute | solution.py:295
  3.0 2.3 %copy-start.5 = (f32[128,256]{1,0:T(8,128)S(1)}, f32[128,256]{1,0:T(8,128)}, u32[]{:S(2)}) copy-start(f32[128,256]{1,0:T(8,128)} %get-tuple-element.21) | copy-start | bytes 393220
  3.0 6.0 %copy-start.4 = (f32[128,256]{1,0:T(8,128)S(1)}, f32[128,256]{1,0:T(8,128)}, u32[]{:S(2)}) copy-start(f32[128,256]{1,0:T(8,128)} %get-tuple-element.28) | copy-start | bytes 393220
  3.0 6.1 %copy-start = (f32[1024,256]{1,0:T(8,128)S(1)}, f32[1024,256]{1,0:T(8,128)}, u32[]{:S(2)}) copy-start(f32[1024,256]{1,0:T(8,128)} %refs_5_.1) | copy-start | bytes 3145732
  3.0 6.1 %copy-start.1 = (s32[8]{0:T(128)S(1)}, s32[8]{0:T(128)}, u32[]{:S(2)}) copy-start(s32[8]{0:T(128)} %refs_2_.5) | copy-start | bytes 100
  3.0 6.1 %copy-start.2 = (s32[8]{0:T(128)S(1)}, s32[8]{0:T(128)}, u32[]{:S(2)}) copy-start(s32[8]{0:T(128)} %refs_0_.5) | copy-start | bytes 100
  3.0 17.7 %collective-permute-start.2 = (f32[8,256,256]{2,1,0:T(8,128)}, f32[8,256,256]{2,1,0:T(8,128)S(1)}, u32[]{:S(2)}, u32[]{:S(2)}) collective-permute-start(f32[8,256,256]{2,1,0:T(8,128)} %refs_2_.3), channel_id=1, source_target_pairs={{0,1},{1,0},{2,3},{3,2},{4,5},{5,4},{6,7},{7,6},{8,9},{9,8},{10,11... | collective-permute-start | bytes 6291464 | tf_op jit(solution)/shard_map/ppermute | solution.py:295
  4.9 15.9 %collective-permute-start.1 = (f32[4,8,128,128]{3,2,1,0:T(8,128)S(1)}, f32[4,8,128,128]{3,2,1,0:T(8,128)S(1)}, u32[]{:S(2)}, u32[]{:S(2)}) collective-permute-start(f32[4,8,128,128]{3,2,1,0:T(8,128)S(1)} %pair_blocks.1), channel_id=1, source_target_pairs={{0,1},{1,0},{2,3},{3,2},{4,5},{5,4},{6,7},{7,6},{8,9},{9,8},{10,11... | collective-permute-start | bytes 6291464 | tf_op jit(solution)/shard_map/ppermute | solution.py:295
  5.3 13.8 %collective-permute-start.6 = (f32[128,256]{1,0:T(8,128)S(1)}, f32[128,256]{1,0:T(8,128)S(1)}, u32[]{:S(2)}, u32[]{:S(2)}) collective-permute-start(f32[128,256]{1,0:T(8,128)S(1)} %copy-done.5), channel_id=1, source_target_pairs={{8,0},{12,4},{0,8},{4,12},{9,1},{13,5},{1,9},{5,13},{10,2},{14,6},... | collective-permute-start | bytes 393224 | tf_op jit(solution)/shard_map/ppermute | solution.py:326
  9.0 4.7 %copy-start.3 = (f32[128,256]{1,0:T(8,128)S(1)}, f32[128,256]{1,0:T(8,128)}, u32[]{:S(2)}) copy-start(f32[128,256]{1,0:T(8,128)} %get-tuple-element.33) | copy-start | bytes 393220
  9.0 14.1 %collective-permute-start.3 = (f32[128,256]{1,0:T(8,128)S(1)}, f32[128,256]{1,0:T(8,128)S(1)}, u32[]{:S(2)}, u32[]{:S(2)}) collective-permute-start(f32[128,256]{1,0:T(8,128)S(1)} %copy-done.4), channel_id=1, source_target_pairs={{8,0},{12,4},{0,8},{4,12},{9,1},{13,5},{1,9},{5,13},{10,2},{14,6},... | collective-permute-start | bytes 393224 | tf_op jit(solution)/shard_map/ppermute | solution.py:326
  13.8 11.6 %collective-permute-start.5 = (f32[128,256]{1,0:T(8,128)S(1)}, f32[128,256]{1,0:T(8,128)S(1)}, u32[]{:S(2)}, u32[]{:S(2)}) collective-permute-start(f32[128,256]{1,0:T(8,128)S(1)} %copy-done.3), channel_id=1, source_target_pairs={{0,4},{4,8},{8,12},{5,1},{9,5},{13,9},{2,6},{6,10},{10,14},{7,3},{... | collective-permute-start | bytes 393224 | tf_op jit(solution)/shard_map/ppermute | solution.py:412
  19.1 6.3 %collective-permute-start.7 = (f32[1,128,256]{2,1,0:T(8,128)S(1)}, f32[1,128,256]{2,1,0:T(8,128)S(1)}, u32[]{:S(2)}, u32[]{:S(2)}) collective-permute-start(f32[1,128,256]{2,1,0:T(8,128)S(1)} %bitcast.4), channel_id=1, source_target_pairs={{0,2},{1,3},{2,0},{3,1},{4,6},{5,7},{6,4},{7,5},{8,10},{9,11},{10,... | collective-permute-start | bytes 393224 | tf_op jit(solution)/shard_map/ppermute | solution.py:295
  23.2 6.8 %collective-permute-start.4 = (f32[1,128,256]{2,1,0:T(8,128)S(1)}, f32[1,128,256]{2,1,0:T(8,128)S(1)}, u32[]{:S(2)}, u32[]{:S(2)}) collective-permute-start(f32[1,128,256]{2,1,0:T(8,128)S(1)} %bitcast.2), channel_id=1, source_target_pairs={{0,2},{1,3},{2,0},{3,1},{4,6},{5,7},{6,4},{7,5},{8,10},{9,11},{10,... | collective-permute-start | bytes 393224 | tf_op jit(solution)/shard_map/ppermute | solution.py:295
  28.6 9.4 %collective-permute-start.11 = (f32[256,256]{1,0:T(8,128)S(1)}, f32[256,256]{1,0:T(8,128)S(1)}, u32[]{:S(2)}, u32[]{:S(2)}) collective-permute-start(f32[256,256]{1,0:T(8,128)S(1)} %get-tuple-element.37), channel_id=1, source_target_pairs={{0,2},{1,3},{2,0},{3,1},{4,6},{5,7},{6,4},{7,5},{8,10},{9,11},{10,... | collective-permute-start | bytes 786440 | tf_op jit(solution)/shard_map/ppermute | solution.py:295
  32.7 8.0 %collective-permute-start.15 = (f32[256,256]{1,0:T(8,128)S(1)}, f32[256,256]{1,0:T(8,128)S(1)}, u32[]{:S(2)}, u32[]{:S(2)}) collective-permute-start(f32[256,256]{1,0:T(8,128)S(1)} %get-tuple-element.39), channel_id=1, source_target_pairs={{0,2},{1,3},{2,0},{3,1},{4,6},{5,7},{6,4},{7,5},{8,10},{9,11},{10,... | collective-permute-start | bytes 786440 | tf_op jit(solution)/shard_map/ppermute | solution.py:295
  33.6 7.2 %collective-permute-start.10 = (f32[16,128]{1,0:T(8,128)S(1)}, f32[16,128]{1,0:T(8,128)S(1)}, u32[]{:S(2)}, u32[]{:S(2)}) collective-permute-start(f32[16,128]{1,0:T(8,128)S(1)} %get-tuple-element.36), channel_id=1, source_target_pairs={{0,12},{4,8},{8,4},{12,0},{1,13},{5,9},{9,5},{13,1},{2,14},{6,10},... | collective-permute-start | bytes 24584 | tf_op jit(solution)/shard_map/ppermute | solution.py:295
  36.1 4.7 %collective-permute-start.9 = (f32[16,128]{1,0:T(8,128)S(1)}, f32[16,128]{1,0:T(8,128)S(1)}, u32[]{:S(2)}, u32[]{:S(2)}) collective-permute-start(f32[16,128]{1,0:T(8,128)S(1)} %get-tuple-element.36), channel_id=1, source_target_pairs={{0,8},{4,12},{8,0},{12,4},{1,9},{5,13},{9,1},{13,5},{2,10},{6,14},... | collective-permute-start | bytes 24584 | tf_op jit(solution)/shard_map/ppermute | solution.py:295
  36.1 4.7 %collective-permute-start.8 = (f32[16,128]{1,0:T(8,128)S(1)}, f32[16,128]{1,0:T(8,128)S(1)}, u32[]{:S(2)}, u32[]{:S(2)}) collective-permute-start(f32[16,128]{1,0:T(8,128)S(1)} %get-tuple-element.36), channel_id=1, source_target_pairs={{0,4},{4,0},{8,12},{12,8},{1,5},{5,1},{9,13},{13,9},{2,6},{6,2},{1... | collective-permute-start | bytes 24584 | tf_op jit(solution)/shard_map/ppermute | solution.py:295
  38.1 7.7 %collective-permute-start.16 = (f32[256,256]{1,0:T(8,128)S(1)}, f32[256,256]{1,0:T(8,128)S(1)}, u32[]{:S(2)}, u32[]{:S(2)}) collective-permute-start(f32[256,256]{1,0:T(8,128)S(1)} %add.30.refs_0_), channel_id=1, source_target_pairs={{0,1},{1,0},{2,3},{3,2},{4,5},{5,4},{6,7},{7,6},{8,9},{9,8},{10,11... | collective-permute-start | bytes 786440 | tf_op jit(solution)/shard_map/ppermute | solution.py:295
  40.7 5.1 %collective-permute-start.17 = (f32[256,256]{1,0:T(8,128)S(1)}, f32[256,256]{1,0:T(8,128)S(1)}, u32[]{:S(2)}, u32[]{:S(2)}) collective-permute-start(f32[256,256]{1,0:T(8,128)S(1)} %add.31.refs_1_), channel_id=1, source_target_pairs={{0,1},{1,0},{2,3},{3,2},{4,5},{5,4},{6,7},{7,6},{8,9},{9,8},{10,11... | collective-permute-start | bytes 786440 | tf_op jit(solution)/shard_map/ppermute | solution.py:295
  40.9 3.1 %collective-permute-start.14 = (f32[16,128]{1,0:T(8,128)S(1)}, f32[16,128]{1,0:T(8,128)S(1)}, u32[]{:S(2)}, u32[]{:S(2)}) collective-permute-start(f32[16,128]{1,0:T(8,128)S(1)} %add_add_fusion.1), channel_id=1, source_target_pairs={{0,3},{1,2},{2,1},{3,0},{4,7},{5,6},{6,5},{7,4},{8,11},{9,10},{10,... | collective-permute-start | bytes 24584 | tf_op jit(solution)/shard_map/ppermute | solution.py:295
  42.1 3.7 %collective-permute-start.13 = (f32[16,128]{1,0:T(8,128)S(1)}, f32[16,128]{1,0:T(8,128)S(1)}, u32[]{:S(2)}, u32[]{:S(2)}) collective-permute-start(f32[16,128]{1,0:T(8,128)S(1)} %add_add_fusion.1), channel_id=1, source_target_pairs={{0,2},{1,3},{2,0},{3,1},{4,6},{5,7},{6,4},{7,5},{8,10},{9,11},{10,... | collective-permute-start | bytes 24584 | tf_op jit(solution)/shard_map/ppermute | solution.py:295
  43.0 2.7 %collective-permute-start.12 = (f32[16,128]{1,0:T(8,128)S(1)}, f32[16,128]{1,0:T(8,128)S(1)}, u32[]{:S(2)}, u32[]{:S(2)}) collective-permute-start(f32[16,128]{1,0:T(8,128)S(1)} %add_add_fusion.1), channel_id=1, source_target_pairs={{0,1},{1,0},{2,3},{3,2},{4,5},{5,4},{6,7},{7,6},{8,9},{9,8},{10,11... | collective-permute-start | bytes 24584 | tf_op jit(solution)/shard_map/ppermute | solution.py:295

commit v6 on v5

--- a/solution.py
+++ b/solution.py
@@ -27,7 +27,7 @@
 
 
 PREPARE_VMEM, CUT_VMEM, OWN_VMEM, NEAR_VMEM = 62, 50, 46, 32
-GROUP = 2
+GROUPS = (4, 2)
 
 
 def place():
@@ -81,10 +81,10 @@
     src[here, 2 * wide : 3 * wide] = high
 
 
-def pack(cls_ref, choose, order, offsets):
+def pack(classes, choose, order, offsets):
     n = jnp.int32(0)
-    for t in range(cls_ref.shape[0]):
-        chosen, at = choose(cls_ref[t])
+    for t, c in enumerate(classes):
+        chosen, at = choose(c)
 
         @pl.when(chosen)
         def _(n=n, t=t, at=at):
@@ -95,101 +95,87 @@
     return n
 
 
-def add_terms(n, order, offsets, src, left, right, first, acc, tbuf, right_ready=None, left_ready=None):
+def add_terms(n, order, offsets, src, right_of, left_of, acc, tbuf):
     rows = acc.shape[0]
-    block = left.shape[-1]
+    block = tbuf.shape[1] // (2 * max(GROUPS))
     count = rows // block
 
-    @pl.loop(0, lax.div(n + GROUP - 1, GROUP))
-    def _(i):
+    def add(begin, group):
         terms, real = [], []
-        for j in range(GROUP):
-            k = jnp.minimum(i * GROUP + j, n - 1)
-            real.append(i * GROUP + j < n)
+        for j in range(group):
+            k = jnp.minimum(begin + j, n - 1)
+            real.append(begin + j < n)
             terms.append(order[k])
-            if right_ready is not None:
-
-                @pl.when(real[j])
-                def _(j=j):
-                    right_ready(terms[j])
-
             at = pl.ds(pl.multiple_of(offsets[k], block), rows)
-            high, low = split(right[terms[j]])
+            high, low = split(right_of(terms[j]))
             wide = jnp.concatenate([high, high, low], 0)
             high, low = split(jnp.dot(src[at, :], wide, preferred_element_type=F32))
             for s in range(count):
                 here = slice(s * block, (s + 1) * block)
                 tbuf[s, j * block : (j + 1) * block, :] = high[here]
-                tbuf[s, (GROUP + j) * block : (GROUP + j + 1) * block, :] = low[here]
-        if left_ready is not None:
-            pl.when(i == 0)(left_ready)
+                tbuf[s, (group + j) * block : (group + j + 1) * block, :] = low[here]
         for s in range(count):
-            blocks = [left[first + s, terms[0]]]
-            for j in range(1, GROUP):
-                blocks.append(jnp.where(real[j], left[first + s, terms[j]], 0.0))
+            blocks = [left_of(s, terms[0])]
+            for j in range(1, group):
+                blocks.append(jnp.where(real[j], left_of(s, terms[j]), 0.0))
             high, low = split(jnp.concatenate(blocks, 1))
             acc[s * block : (s + 1) * block, :] += jnp.dot(
                 jnp.concatenate([high, high, low], 1),
-                jnp.concatenate([tbuf[s], tbuf[s, 0 : GROUP * block]], 0),
+                jnp.concatenate([tbuf[s, 0 : 2 * group * block], tbuf[s, 0 : group * block]], 0),
                 preferred_element_type=F32,
             )
 
-
-def near_kernel(own, *refs):
-    if own:
-        cls, left_hbm, right_hbm, rows_hbm, whole, wave, acc, left, right, src, live, rows_ref, load, *rest = refs
-    else:
-        cls, left, right, src, acc_in, acc, *rest = refs
-    tbuf, cls_ref, order, offsets, sem = rest
+    large, small = GROUPS
+    full = lax.div(n + large - small - 1, large)
+
+    @pl.loop(0, full)
+    def _(i):
+        add(i * large, large)
+
+    @pl.when(n > full * large)
+    def _():
+        add(full * large, small)
+
+
+def load_kernel(left_hbm, right_hbm, rows_hbm, whole, wave, left, right, src, live, rows_ref, sem):
     half, terms, block, _ = left.shape
     core, _, _ = place()
-
-    fetch = [pltpu.make_async_copy(cls, cls_ref, sem.at[0])]
-    if own:
-        fetch.append(pltpu.make_async_copy(rows_hbm, rows_ref, sem.at[1]))
-    for move in fetch:
+    rows = pltpu.make_async_copy(rows_hbm, rows_ref, sem.at[0])
+    moves = [
+        pltpu.make_async_copy(left_hbm.at[pl.ds(core * half, half)], left, sem.at[1]),
+        pltpu.make_async_copy(right_hbm, right, sem.at[2]),
+    ]
+    for move in [rows] + moves:
         move.start()
-    if own:
-        left_move = pltpu.make_async_copy(left_hbm.at[pl.ds(core * half, half)], left, load.at[terms])
-        right_moves = lambda t: pltpu.make_async_copy(right_hbm.at[t], right.at[t], load.at[t])
-        for t in range(terms):
-            right_moves(t).start()
-            if t == 1:
-                left_move.start()
-        acc[...] = jnp.zeros_like(acc)
-        halo_at = pl.multiple_of(core * (half + 1) * block, block)
-        src[pl.ds(halo_at, block), :] = jnp.zeros((block, src.shape[1]), BF16)
-    else:
-        acc[...] = acc_in[...]
-    for move in fetch:
+    halo_at = pl.multiple_of(core * (half + 1) * block, block)
+    src[pl.ds(halo_at, block), :] = jnp.zeros((block, src.shape[1]), BF16)
+    rows.wait()
+    for s in range(2 * half):
+        here = pl.ds(s * block, block)
+        live[here, :] = masked(wave[here, :], rows_ref[s])
+    for i in range(half + 1):
+        sector = core * (half - 1) + i
+        value = masked(sector_rows(whole, sector, block)[...], rows_ref[sector])
+        put(src, pl.multiple_of((i + 1 - core) * block, block), value)
+    for move in moves:
         move.wait()
-    if own:
-        for s in range(2 * half):
-            here = pl.ds(s * block, block)
-            live[here, :] = masked(wave[here, :], rows_ref[s])
-        for i in range(half + 1):
-            sector = core * (half - 1) + i
-            rows = masked(sector_rows(whole, sector, block)[...], rows_ref[sector])
-            put(src, pl.multiple_of((i + 1 - core) * block, block), rows)
+
+
+def near_kernel(chained, cls, left, right, src, *refs):
+    acc_in, refs = (refs[0], refs[1:]) if chained else (None, refs)
+    acc, tbuf, cls_ref, order, offsets, sem = refs
+    block = left.shape[-1]
+    fetch = pltpu.make_async_copy(cls, cls_ref, sem.at[0])
+    fetch.start()
+    acc[...] = acc_in[...] if chained else jnp.zeros_like(acc)
+    fetch.wait()
 
     def near(c):
         at = jnp.where(c == 0, block, jnp.where(c == 3, 2 * block, 0))
         return jnp.logical_or(c == 0, c >= 3), at
 
-    n = pack(cls_ref, near, order, offsets)
-    if not own:
-        add_terms(n, order, offsets, src, left, right, 0, acc, tbuf)
-        return
-    add_terms(n, order, offsets, src, left, right, 0, acc, tbuf, lambda t: right_moves(t).wait(), left_move.wait)
-    for t in range(terms):
-
-        @pl.when(jnp.logical_not(near(cls_ref[t])[0]))
-        def _(t=t):
-            right_moves(t).wait()
-
-    @pl.when(n == 0)
-    def _():
-        left_move.wait()
+    n = pack([cls_ref[t] for t in range(right.shape[0])], near, order, offsets)
+    add_terms(n, order, offsets, src, lambda t: right[t], lambda s, t: left[s, t], acc, tbuf)
 
 
 def far_kernel(lo, shift, secs, chained, *refs):
@@ -198,7 +184,7 @@
     sums_in = refs.pop(12) if chained else None
     acc, sums, src, tbuf, rows_ref, cls_ref, order, offsets, sem = refs[12:]
     rows, cols = acc.shape
-    half, _, block, _ = left.shape
+    half, terms, block, _ = left.shape
     count = rows // block
     core, side, sec = place()
     merged = mine.shape[0] == 1
@@ -225,14 +211,20 @@
         below = jnp.logical_and(c == 2, sec >= shift)
         return jnp.logical_or(above, below), jnp.where(c == 1, 0, 0 if merged else rows)
 
-    for g, (l, r) in enumerate(((left, right), (left_pair, right_pair))):
-        n = pack(cls_ref.at[g], far, order, offsets)
-        add_terms(n, order, offsets, src, l, r, lo, acc, tbuf)
-        n = pack(cls_ref.at[g], lambda c: (c == 4 - core, halo_at), order, offsets)
-        n = jnp.where(core == (0 if lo == 0 else 1), n, 0)
-        edge = core * (count - 1)
-        part = acc.at[pl.ds(pl.multiple_of(edge * block, block), block), :]
-        add_terms(n, order, offsets, src, l, r, lo + edge, part, tbuf)
+    def either(own, pair, t, *index):
+        here = index + (lax.rem(t, terms),)
+        return jnp.where(t < terms, own[here], pair[here])
+
+    classes = [cls_ref[g, t] for g in range(2) for t in range(terms)]
+    right_of = functools.partial(either, right, right_pair)
+    n = pack(classes, far, order, offsets)
+    left_of = lambda s, t: either(left, left_pair, t, lo + s)
+    add_terms(n, order, offsets, src, right_of, left_of, acc, tbuf)
+    n = pack(classes, lambda c: (c == 4 - core, halo_at), order, offsets)
+    n = jnp.where(core == (0 if lo == 0 else 1), n, 0)
+    edge = core * (count - 1)
+    left_of = lambda s, t: either(left, left_pair, t, lo + edge)
+    add_terms(n, order, offsets, src, right_of, left_of, acc.at[pl.ds(pl.multiple_of(edge * block, block), block), :], tbuf)
 
     cross = jnp.zeros((8, cols), F32)
     square = jnp.zeros((8, cols), F32)
@@ -253,27 +245,27 @@
     sums[8:16, :] = square
 
 
-def final_kernel(sides, sums, live, *refs):
-    totals, (applied, correction, buf, sem) = refs[:-4], refs[-4:]
+def final_kernel(sides, live, total, total_pair, applied, correction, buf, sem):
     core, _, _ = place()
-    half = live.shape[0] // 2
-    chunks = len(totals) // 2
-    places = []
+    rows = live.shape[0] // 2
+    pieces = sem.shape[1] // 2
+    piece = rows // pieces
     moves = []
-    at = 0
-    for i, total in enumerate(totals):
-        rows = total.shape[0]
-        first = (core if i < chunks else 1 - core) * half + at % half
-        at += rows
-        places.append(pl.ds(pl.multiple_of(first, 8), rows))
-        moves.append(pltpu.make_async_copy(total, applied.at[places[i], :], sem.at[0, i]))
+
+    def send(source, target, kind, i):
+        moves.append(pltpu.make_async_copy(source, target, sem.at[kind, i]))
         moves[-1].start()
+
+    for i, (ref, c) in enumerate(((total, core), (total_pair, 1 - core))):
+        here = pl.ds(pl.multiple_of(c * rows, rows), rows)
+        send(ref.at[pl.ds(0, rows), :], applied.at[here, :], 0, i)
+    sums = total[rows : rows + 16, 0:128] + total_pair[rows : rows + 16, 0:128]
     rayleigh = jnp.sum(sums[0:8, :]) / (jnp.sum(sums[8:16, :]) * (1.0 / sides))
-    for i, total in enumerate(totals):
-        here = places[i]
-        buf[here, :] = total[...] - rayleigh * live[here, :]
-        moves.append(pltpu.make_async_copy(buf.at[here, :], correction.at[here, :], sem.at[1, i]))
-        moves[-1].start()
+    for i, (ref, c) in enumerate(((total, core), (total_pair, 1 - core))):
+        for p in range(pieces):
+            here = pl.ds(pl.multiple_of(c * rows + p * piece, piece), piece)
+            buf[here, :] = ref[pl.ds(p * piece, piece), :] - rayleigh * live[here, :]
+            send(buf.at[here, :], correction.at[here, :], 1, i * pieces + p)
     for move in moves:
         move.wait()
 
@@ -295,8 +287,14 @@
     return lax.ppermute(array, axis, pairs)
 
 
-def everyone(array, axis):
-    return (array + swap(array, axis, 1)) + (swap(array, axis, 2) + swap(array, axis, 3))
+def spread_sum(sums):
+    sums = sums + swap(sums, "mpo", 1)
+    parts = []
+    for bit in range(4):
+        pairs = [(4 * z + m, 4 * (z ^ bit) + (m ^ 2 if m % 2 else m)) for z in range(4) for m in range(4)]
+        parts.append(lax.ppermute(sums, ("sec", "mpo"), [p for p in pairs if p[0] != p[1]]))
+    parts[0] = jnp.where(lax.axis_index("mpo") % 2 == 0, sums, parts[0])
+    return (parts[0] + parts[1]) + (parts[2] + parts[3])
 
 
 def after(array, *others):
@@ -361,27 +359,21 @@
     far_a = far(mine_a)
     right_pair = swap(after(right_blocks, mine_a), "mpo", 1)
 
-    lists = [pltpu.SMEM((terms,), jnp.int32)] * 2
-
-    def near(own, *args):
-        outs = [shape(half * block, cols)]
-        scratch = []
-        if own:
-            outs += [blocks, shape(terms, wide, cols)]
-            outs += [jax.ShapeDtypeStruct(source_shape, BF16), shape(sector_count * block, cols)]
-            scratch = [pltpu.SMEM((sector_count,), jnp.int32), pltpu.SemaphoreType.DMA((terms + 1,))]
+    lists = [pltpu.SMEM((2 * terms,), jnp.int32)] * 2
+
+    def near(name, *args):
+        chained = len(args) == 5
         return pl.pallas_call(
-            functools.partial(near_kernel, own),
-            out_shape=tuple(outs),
-            in_specs=[ANY] * 4 + [VMEM] * 2 if own else [ANY] + [VMEM] * 4,
-            out_specs=(VMEM,) * len(outs),
-            scratch_shapes=scratch
-            + [pltpu.VMEM((half, 2 * GROUP * block, cols), BF16), pltpu.SMEM((terms,), jnp.int32)]
+            functools.partial(near_kernel, chained),
+            out_shape=shape(half * block, cols),
+            in_specs=[ANY] + [VMEM] * (len(args) - 1),
+            out_specs=VMEM,
+            scratch_shapes=[pltpu.VMEM((half, 2 * GROUPS[0] * block, cols), BF16), pltpu.SMEM((terms,), jnp.int32)]
             + lists
-            + [pltpu.SemaphoreType.DMA((2,))],
-            compiler_params=params(OWN_VMEM if own else NEAR_VMEM),
+            + [pltpu.SemaphoreType.DMA((1,))],
+            compiler_params=params(NEAR_VMEM),
             cost_estimate=cost(1, 1),
-            name="own_near" if own else "pair_near",
+            name=name,
         )(*args)
 
     def add_far(lo, count, far, acc, sums):
@@ -394,7 +386,7 @@
             out_specs=(VMEM, VMEM),
             scratch_shapes=[
                 pltpu.VMEM((far[0].shape[0] * rows + block, 3 * wide), BF16),
-                pltpu.VMEM((count, 2 * GROUP * block, cols), BF16),
+                pltpu.VMEM((count, 2 * GROUPS[0] * block, cols), BF16),
                 pltpu.SMEM((sector_count,), jnp.int32),
                 pltpu.SMEM((2, terms), jnp.int32),
                 *lists,
@@ -405,43 +397,52 @@
             name="far",
         )(term_charge, cls_pair, block_rows, left, right, left_pair, right_pair, live, *far, halo, acc, *extra)
 
-    acc, left, right, src, live = near(
-        True, term_charge, left_blocks, right_blocks, after(block_rows, mine_a), whole, wavefunction
-    )
-    far_b = far(mine_b)
+    left, right, src, live = pl.pallas_call(
+        load_kernel,
+        out_shape=(
+            blocks,
+            shape(terms, wide, cols),
+            jax.ShapeDtypeStruct(source_shape, BF16),
+            shape(sector_count * block, cols),
+        ),
+        in_specs=[ANY] * 3 + [VMEM] * 2,
+        out_specs=(VMEM,) * 4,
+        scratch_shapes=[pltpu.SMEM((sector_count,), jnp.int32), pltpu.SemaphoreType.DMA((3,))],
+        compiler_params=params(OWN_VMEM),
+        cost_estimate=cost(1, 1),
+        name="own_terms",
+    )(left_blocks, right_blocks, after(block_rows, mine_a), whole, wavefunction)
+    far_b = far(after(mine_b, src))
+    acc = near("own_near", term_charge, left, right, src)
     halo = lax.ppermute(after(halo, acc), ("sec", "mpo"), halo_pairs)
     other_a = swap(after(far_a, acc), "mpo", 2)
-    (acc,) = near(False, cls_pair, left_pair, right_pair, src, acc)
+    acc = near("pair_near", cls_pair, left_pair, right_pair, src, acc)
     other_b = swap(after(far_b, acc), "mpo", 2)
     part_a, sums = add_far(0, sizes[0], (far_a, other_a), acc, None)
     recv_a = swap(part_a, "mpo", 2)
     part_b, sums = add_far(sizes[0], sizes[1], (far_b, other_b), acc, sums)
     recv_b = swap(part_b, "mpo", 2)
 
-    if secs == 4:
-        sums = everyone(sums, "sec")
+    if secs == 4 and mpos == 4 and reps == 1:
+        sums = spread_sum(sums)
     else:
-        sums = lax.psum(sums, "sec")
-    if reps > 1:
-        sums = lax.psum(sums, "rep")
-    sums = everyone(after(sums, recv_a), "mpo")
-    totals = [part_a + recv_a, part_b + recv_b]
-    totals += [swap(total, "mpo", 1) for total in totals]
+        sums = lax.psum(sums, ("sec", "rep"))
+        sums = sums + swap(sums, "mpo", 2)
+    sums = jnp.pad(sums, ((0, 0), (0, cols - sums.shape[1])))
+    total = jnp.concatenate([part_a + recv_a, part_b + after(recv_b, sums), sums])
+    total_pair = swap(total, "mpo", 1)
 
     out = shape(sector_count * block, cols)
     return pl.pallas_call(
         functools.partial(final_kernel, mpos // 2),
         out_shape=(out, out),
-        in_specs=[VMEM] * (2 + len(totals)),
+        in_specs=[VMEM] * 3,
         out_specs=(ANY, ANY),
-        scratch_shapes=[
-            pltpu.VMEM((sector_count * block, cols), F32),
-            pltpu.SemaphoreType.DMA((2, len(totals))),
-        ],
+        scratch_shapes=[pltpu.VMEM((sector_count * block, cols), F32), pltpu.SemaphoreType.DMA((2, 4))],
         compiler_params=params(32),
         cost_estimate=cost(1, 1),
         name="residual",
-    )(sums, live, *totals)
+    )(live, total, total_pair)
 
 
 def solution(mesh):

time: 47 us -> 45.9 us (0.977)
  starting transfers between devices: 21.4 us -> 19.4 us
  waiting for transfers between devices: 6.93 us -> 7.8 us
    ppermute x15 -> x9, starting transfers between devices: 13.8 us -> 7.68 us  [swap(): return lax.ppermute(array, axis, pairs)]
    ppermute x0 -> x4, starting transfers between devices: none -> 4.14 us  [spread_sum(): lax.ppermute(sums, ('sec', 'mpo'), [p for p in pairs if p[0] != p[1]])]
    ppermute x0 -> x4, waiting for transfers between devices: none -> 2.66 us  [spread_sum(): lax.ppermute(sums, ('sec', 'mpo'), [p for p in pairs if p[0] != p[1]])]
    pallas_call x2, Pallas kernels: 6.02 us -> 4.73 us  [add_far(): pl.pallas_call(functools.partial(far_kernel, lo, shift, secs, sums is not...]
    ppermute x15 -> x9, waiting for transfers between devices: 5.34 us -> 4.27 us  [swap(): return lax.ppermute(array, axis, pairs)]
    pallas_call x2 -> x3, Pallas kernels: 7.01 us -> 8.04 us  [the longest x2 5.79 us: near(): pl.pallas_call(functools.partial(near_kernel, chained), out_shape=shape(h...]
    ppermute x2, waiting for transfers between devices: 1.59 us -> 0.87 us  [far(): return lax.ppermute(array, 'sec', up + down)[None]]
  transfers between devices with their start and end apart: 18 -> 16, of which waited for: 4 -> 7; matrix products, arithmetic and copies ran while one was open for 0% -> 0% of each run, Pallas kernels for 35% -> 35%
where the time goes in v6:
time: 45.9 us
  starting transfers between devices  19.4 us (42%)
  Pallas kernels  17.6 us (38%)
  waiting for transfers between devices  7.8 us (17%)
  between operations  0.87 us (2%)
    ppermute x9, starting transfers between devices, swap(): return lax.ppermute(array, axis, pairs)  7.68 us
    pallas_call x2, Pallas kernels, near(): pl.pallas_call(functools.partial(near_kernel, chained), out_shape=shape(h...  5.79 us
    pallas_call x2, Pallas kernels, add_far(): pl.pallas_call(functools.partial(far_kernel, lo, shift, secs, sums is not...  4.73 us
    ppermute x9, waiting for transfers between devices, swap(): return lax.ppermute(array, axis, pairs)  4.27 us
    ppermute x4, starting transfers between devices, spread_sum(): lax.ppermute(sums, ('sec', 'mpo'), [p for p in pairs if p[0] != p[1]])  4.14 us
    ppermute x2, starting transfers between devices, far(): return lax.ppermute(array, 'sec', up + down)[None]  3.82 us
    ppermute x1, starting transfers between devices, local(): halo = lax.ppermute(after(halo, acc), ('sec', 'mpo'), halo_pairs)  3.8 us
    ppermute x4, waiting for transfers between devices, spread_sum(): lax.ppermute(sums, ('sec', 'mpo'), [p for p in pairs if p[0] != p[1]])  2.66 us
  transfers between devices with their start and end apart: 16, of which 7 were waited for; matrix products, arithmetic and copies ran while one was open for 0% of the time, Pallas kernels for 35%

profile of v6, /device:TPU:0, one launch (start us, length us, event | category | flops | bytes accessed | tf_op | source)
XLA Modules:
  0.0 45.9 jit_solution(17331025031374084520)
XLA Ops:
  0.6 0.5 %collective-permute-start = (s32[8]{0:T(128)}, s32[8]{0:T(128)S(1)}, u32[]{:S(2)}, u32[]{:S(2)}) collective-permute-start(s32[8]{0:T(128)} %refs_0_.3), channel_id=1, source_target_pairs={{0,1},{1,0},{2,3},{3,2},{4,5},{5,4},{6,7},{7,6},{8,9},{9,8},{10,11... | collective-permute-start | bytes 104 | tf_op jit(solution)/shard_map/ppermute | solution.py:287
  1.1 1.8 %prepare.1 = (f32[128,256]{1,0:T(8,128)}, f32[128,256]{1,0:T(8,128)}, f32[128,256]{1,0:T(8,128)}) custom-call(s32[8]{0:T(128)} %refs_2_.3, f32[1024,256]{1,0:T(8,128)} %wave.3), custom_call_target="tpu_custom_call" | custom-call | flops 1 | bytes 1 | tf_op jit(solution)/shard_map/prepare/pallas_call | solution.py:338
  2.9 0.0 copy-start.5
  3.0 0.0 copy-start
  3.0 0.0 copy-start.1
  3.0 0.1 collective-permute-start.2
  3.1 0.0 collective-permute-done.cls.refs_1_
  3.1 1.7 %pair_blocks.1 = f32[4,8,128,128]{3,2,1,0:T(8,128)S(1)} custom-call(f32[8,8,128,128]{3,2,1,0:T(8,128)} %left), custom_call_target="tpu_custom_call" | custom-call | flops 1 | bytes 1 | tf_op jit(solution)/shard_map/pair_blocks/pallas_call | solution.py:348
  4.8 0.0 copy-start.4
  4.8 0.0 copy-start.2
  4.8 0.4 collective-permute-start.1
  5.3 0.0 copy-done.5
  5.3 3.7 %collective-permute-start.3 = (f32[128,256]{1,0:T(8,128)S(1)}, f32[128,256]{1,0:T(8,128)S(1)}, u32[]{:S(2)}, u32[]{:S(2)}) collective-permute-start(f32[128,256]{1,0:T(8,128)S(1)} %copy-done.5), channel_id=1, source_target_pairs={{8,0},{12,4},{0,8},{4,12},{9,1},{13,5},{1,9},{5,13},{10,2},{14,6},... | collective-permute-start | bytes 393224 | tf_op jit(solution)/shard_map/ppermute | solution.py:324
  9.0 2.2 %own_terms.1 = (f32[4,8,128,128]{3,2,1,0:T(8,128)S(1)}, f32[8,256,256]{2,1,0:T(8,128)S(1)}, bf16[768,768]{1,0:T(8,128)(2,1)S(1)}, f32[1024,256]{1,0:T(8,128)S(1)}) custom-call(f32[8,8,128,128]{3,2,1,0:T(8,128)} %left, f32[8,256,256]{2,1,0:T(8,128)} %right_hbm.1, s32[8]{0:T(128)S(1)} %copy-done.1, f32[1024,256]{1,0:T(8,128)S(1)} %copy-done, ...), custom_call_target="tpu_custom_call" | custom-call | flops 1 | bytes 1 | tf_op jit(solution)/shard_map/own_terms/pallas_call | solution.py:400
  11.3 0.0 copy-done.4
  11.3 0.1 collective-permute-start.7
  11.4 0.0 copy-done.2
  11.4 2.9 %own_near.1.refs_0_ = f32[512,256]{1,0:T(8,128)S(1)} custom-call(s32[8]{0:T(128)S(1)} %copy-done.2, f32[4,8,128,128]{3,2,1,0:T(8,128)S(1)} %get-tuple-element.24.left.refs_3_, f32[8,256,256]{2,1,0:T(8,128)S(1)} %get-tuple-element.25.right.refs_4_, bf16[768,768]{1,0:T(8,128)(2,1)S(1)} %get-tuple-element.28.src), custom_call_target="tpu_custom_call" | custom-call | flops 1 | bytes 1 | tf_op jit(solution)/shard_map/own_near/pallas_call | solution.py:366
  14.3 3.8 %collective-permute-start.5 = (f32[128,256]{1,0:T(8,128)S(1)}, f32[128,256]{1,0:T(8,128)S(1)}, u32[]{:S(2)}, u32[]{:S(2)}) collective-permute-start(f32[128,256]{1,0:T(8,128)S(1)} %copy-done.3), channel_id=1, source_target_pairs={{0,4},{4,8},{8,12},{5,1},{9,5},{13,9},{2,6},{6,10},{10,14},{7,3},{... | collective-permute-start | bytes 393224 | tf_op jit(solution)/shard_map/ppermute | solution.py:417
  18.1 0.9 %collective-permute-done.3 = f32[128,256]{1,0:T(8,128)S(1)} collective-permute-done((f32[128,256]{1,0:T(8,128)S(1)}, f32[128,256]{1,0:T(8,128)S(1)}, u32[]{:S(2)}, u32[]{:S(2)}) %collective-permute-start.3) | collective-permute-done | bytes 131104 | tf_op jit(solution)/shard_map/ppermute | solution.py:324
  18.9 1.9 %collective-permute-start.4 = (f32[1,128,256]{2,1,0:T(8,128)S(1)}, f32[1,128,256]{2,1,0:T(8,128)S(1)}, u32[]{:S(2)}, u32[]{:S(2)}) collective-permute-start(f32[1,128,256]{2,1,0:T(8,128)S(1)} %bitcast.4), channel_id=1, source_target_pairs={{0,2},{1,3},{2,0},{3,1},{4,6},{5,7},{6,4},{7,5},{8,10},{9,11},{10,... | collective-permute-start | bytes 393224 | tf_op jit(solution)/shard_map/ppermute | solution.py:287
  20.8 0.0 collective-permute-done.2.right.refs_6_
  20.8 0.0 collective-permute-done.1.left.refs_5_
  20.8 2.9 %pair_near.1.refs_11_ = f32[512,256]{1,0:T(8,128)S(1)} custom-call(s32[8]{0:T(128)S(1)} %collective-permute-done.cls.refs_1_, f32[4,8,128,128]{3,2,1,0:T(8,128)S(1)} %collective-permute-done.1.left.refs_5_, f32[8,256,256]{2,1,0:T(8,128)S(1)} %collective-permute-done.2.right.refs_6_, bf16[768,768]{1,0:T(8,128)(2,1)S(1)} %get-tuple-element.28.src, ...), custom_call_target="tpu_custom_call" | custom-call | flops 1 | bytes 1 | tf_op jit(solution)/shard_map/pair_near/pallas_call | solution.py:366
  23.7 0.0 collective-permute-done.7
  23.8 0.1 collective-permute-start.8
  23.8 0.0 collective-permute-done.5.refs_10_
  23.8 0.1 collective-permute-done.4.refs_9_
  24.0 3.0 %far.2 = (f32[256,256]{1,0:T(8,128)S(1)}, f32[16,128]{1,0:T(8,128)S(1)}) custom-call(s32[8]{0:T(128)S(1)} %copy-done.2, s32[8]{0:T(128)S(1)} %collective-permute-done.cls.refs_1_, s32[8]{0:T(128)S(1)} %copy-done.1, f32[4,8,128,128]{3,2,1,0:T(8,128)S(1)} %get-tuple-element.24.left.refs_3_, f32[8,256,256]{2,1,0:T(8,128)S(1)} %get-tuple-element.25.right.refs_4_, ...), custom_call_target="tpu_custom_call" | custom-call | flops 1 | bytes 1 | tf_op jit(solution)/shard_map/far/pallas_call | solution.py:382
  27.0 1.8 %collective-permute-start.6 = (f32[256,256]{1,0:T(8,128)S(1)}, f32[256,256]{1,0:T(8,128)S(1)}, u32[]{:S(2)}, u32[]{:S(2)}) collective-permute-start(f32[256,256]{1,0:T(8,128)S(1)} %get-tuple-element.32), channel_id=1, source_target_pairs={{0,2},{1,3},{2,0},{3,1},{4,6},{5,7},{6,4},{7,5},{8,10},{9,11},{10,... | collective-permute-start | bytes 786440 | tf_op jit(solution)/shard_map/ppermute | solution.py:287
  28.8 1.4 %collective-permute-done.8.refs_9_ = f32[1,128,256]{2,1,0:T(8,128)S(1)} collective-permute-done((f32[1,128,256]{2,1,0:T(8,128)S(1)}, f32[1,128,256]{2,1,0:T(8,128)S(1)}, u32[]{:S(2)}, u32[]{:S(2)}) %collective-permute-start.8) | collective-permute-done | bytes 131104 | tf_op jit(solution)/shard_map/ppermute | solution.py:287
  30.2 1.7 %far.3 = (f32[256,256]{1,0:T(8,128)S(1)}, f32[16,128]{1,0:T(8,128)S(1)}) custom-call(s32[8]{0:T(128)S(1)} %copy-done.2, s32[8]{0:T(128)S(1)} %collective-permute-done.cls.refs_1_, s32[8]{0:T(128)S(1)} %copy-done.1, f32[4,8,128,128]{3,2,1,0:T(8,128)S(1)} %get-tuple-element.24.left.refs_3_, f32[8,256,256]{2,1,0:T(8,128)S(1)} %get-tuple-element.25.right.refs_4_, ...), custom_call_target="tpu_custom_call" | custom-call | flops 1 | bytes 1 | tf_op jit(solution)/shard_map/far/pallas_call | solution.py:382
  31.9 0.1 collective-permute-start.9
  32.0 0.1 collective-permute-start.10
  32.1 1.2 %collective-permute-done.10 = f32[16,128]{1,0:T(8,128)S(1)} collective-permute-done((f32[16,128]{1,0:T(8,128)S(1)}, f32[16,128]{1,0:T(8,128)S(1)}, u32[]{:S(2)}, u32[]{:S(2)}) %collective-permute-start.10) | collective-permute-done | bytes 8224 | tf_op jit(solution)/shard_map/ppermute | solution.py:287
  33.2 1.4 %collective-permute-start.13 = (f32[16,128]{1,0:T(8,128)S(1)}, f32[16,128]{1,0:T(8,128)S(1)}, u32[]{:S(2)}, u32[]{:S(2)}) collective-permute-start(f32[16,128]{1,0:T(8,128)S(1)} %add.26), channel_id=1, source_target_pairs={{0,8},{1,11},{2,10},{3,9},{4,12},{5,15},{6,14},{7,13},{8,0},{9,3},... | collective-permute-start | bytes 24584 | tf_op jit(solution)/shard_map/ppermute | solution.py:295
  34.6 1.1 %collective-permute-start.14 = (f32[16,128]{1,0:T(8,128)S(1)}, f32[16,128]{1,0:T(8,128)S(1)}, u32[]{:S(2)}, u32[]{:S(2)}) collective-permute-start(f32[16,128]{1,0:T(8,128)S(1)} %add.26), channel_id=1, source_target_pairs={{0,12},{1,15},{2,14},{3,13},{4,8},{5,11},{6,10},{7,9},{8,4},{9,7},... | collective-permute-start | bytes 24584 | tf_op jit(solution)/shard_map/ppermute | solution.py:295
  35.7 1.0 %collective-permute-start.12 = (f32[16,128]{1,0:T(8,128)S(1)}, f32[16,128]{1,0:T(8,128)S(1)}, u32[]{:S(2)}, u32[]{:S(2)}) collective-permute-start(f32[16,128]{1,0:T(8,128)S(1)} %add.26), channel_id=1, source_target_pairs={{0,4},{1,7},{2,6},{3,5},{4,0},{5,3},{6,2},{7,1},{8,12},{9,15},{10,... | collective-permute-start | bytes 24584 | tf_op jit(solution)/shard_map/ppermute | solution.py:295
  36.7 1.1 %collective-permute-done.13 = f32[16,128]{1,0:T(8,128)S(1)} collective-permute-done((f32[16,128]{1,0:T(8,128)S(1)}, f32[16,128]{1,0:T(8,128)S(1)}, u32[]{:S(2)}, u32[]{:S(2)}) %collective-permute-start.13) | collective-permute-done | bytes 8224 | tf_op jit(solution)/shard_map/ppermute | solution.py:295
  37.9 0.7 %collective-permute-start.11 = (f32[16,128]{1,0:T(8,128)S(1)}, f32[16,128]{1,0:T(8,128)S(1)}, u32[]{:S(2)}, u32[]{:S(2)}) collective-permute-start(f32[16,128]{1,0:T(8,128)S(1)} %add.26), channel_id=1, source_target_pairs={{1,3},{3,1},{5,7},{7,5},{9,11},{11,9},{13,15},{15,13},{17,19},{19,... | collective-permute-start | bytes 24584 | tf_op jit(solution)/shard_map/ppermute | solution.py:295
  38.5 1.5 %collective-permute-done.14 = f32[16,128]{1,0:T(8,128)S(1)} collective-permute-done((f32[16,128]{1,0:T(8,128)S(1)}, f32[16,128]{1,0:T(8,128)S(1)}, u32[]{:S(2)}, u32[]{:S(2)}) %collective-permute-start.14) | collective-permute-done | bytes 8224 | tf_op jit(solution)/shard_map/ppermute | solution.py:295
  40.1 0.0 collective-permute-done.12
  40.1 0.0 collective-permute-done.11
  40.1 0.0 collective-permute-done.6
  40.1 0.0 collective-permute-done.9
  40.2 2.7 %collective-permute-start.15 = (f32[528,256]{1,0:T(8,128)S(1)}, f32[528,256]{1,0:T(8,128)S(1)}, u32[]{:S(2)}, u32[]{:S(2)}) collective-permute-start(f32[528,256]{1,0:T(8,128)S(1)} %pad_maximum_fusion.total), channel_id=1, source_target_pairs={{0,1},{1,0},{2,3},{3,2},{4,5},{5,4},{6,7},{7,6},{8,9},{9,8},{10,11... | collective-permute-start | bytes 1622024 | tf_op jit(solution)/shard_map/ppermute | solution.py:287
  43.0 1.6 %collective-permute-done.15.total_pair = f32[528,256]{1,0:T(8,128)S(1)} collective-permute-done((f32[528,256]{1,0:T(8,128)S(1)}, f32[528,256]{1,0:T(8,128)S(1)}, u32[]{:S(2)}, u32[]{:S(2)}) %collective-permute-start.15) | collective-permute-done | bytes 540704 | tf_op jit(solution)/shard_map/ppermute | solution.py:287
  44.5 1.4 %residual.1 = (f32[1024,256]{1,0:T(8,128)}, f32[1024,256]{1,0:T(8,128)}) custom-call(f32[1024,256]{1,0:T(8,128)S(1)} %get-tuple-element.23.refs_7_.live, f32[528,256]{1,0:T(8,128)S(1)} %pad_maximum_fusion.total, f32[528,256]{1,0:T(8,128)S(1)} %collective-permute-done.15.total_pair), custom_call_target="tpu_custom_call" | custom-call | flops 1 | bytes 1 | tf_op jit(solution)/shard_map/residual/pallas_call | solution.py:436
  (10 shorter events, 0.1 us)
Async XLA Ops:
  0.6 2.5 %collective-permute-start = (s32[8]{0:T(128)}, s32[8]{0:T(128)S(1)}, u32[]{:S(2)}, u32[]{:S(2)}) collective-permute-start(s32[8]{0:T(128)} %refs_0_.3), channel_id=1, source_target_pairs={{0,1},{1,0},{2,3},{3,2},{4,5},{5,4},{6,7},{7,6},{8,9},{9,8},{10,11... | collective-permute-start | bytes 104 | tf_op jit(solution)/shard_map/ppermute | solution.py:287
  2.9 2.3 %copy-start.5 = (f32[128,256]{1,0:T(8,128)S(1)}, f32[128,256]{1,0:T(8,128)}, u32[]{:S(2)}) copy-start(f32[128,256]{1,0:T(8,128)} %get-tuple-element.21) | copy-start | bytes 393220
  3.0 6.0 %copy-start = (f32[1024,256]{1,0:T(8,128)S(1)}, f32[1024,256]{1,0:T(8,128)}, u32[]{:S(2)}) copy-start(f32[1024,256]{1,0:T(8,128)} %wave.3) | copy-start | bytes 3145732
  3.0 6.0 %copy-start.1 = (s32[8]{0:T(128)S(1)}, s32[8]{0:T(128)}, u32[]{:S(2)}) copy-start(s32[8]{0:T(128)} %refs_2_.3) | copy-start | bytes 100
  3.0 17.8 %collective-permute-start.2 = (f32[8,256,256]{2,1,0:T(8,128)}, f32[8,256,256]{2,1,0:T(8,128)S(1)}, u32[]{:S(2)}, u32[]{:S(2)}) collective-permute-start(f32[8,256,256]{2,1,0:T(8,128)} %right_hbm.1), channel_id=1, source_target_pairs={{0,1},{1,0},{2,3},{3,2},{4,5},{5,4},{6,7},{7,6},{8,9},{9,8},{10,11... | collective-permute-start | bytes 6291464 | tf_op jit(solution)/shard_map/ppermute | solution.py:287
  4.8 6.4 %copy-start.4 = (f32[128,256]{1,0:T(8,128)S(1)}, f32[128,256]{1,0:T(8,128)}, u32[]{:S(2)}) copy-start(f32[128,256]{1,0:T(8,128)} %get-tuple-element.34) | copy-start | bytes 393220
  4.8 6.5 %copy-start.2 = (s32[8]{0:T(128)S(1)}, s32[8]{0:T(128)}, u32[]{:S(2)}) copy-start(s32[8]{0:T(128)} %refs_0_.3) | copy-start | bytes 100
  4.8 16.0 %collective-permute-start.1 = (f32[4,8,128,128]{3,2,1,0:T(8,128)S(1)}, f32[4,8,128,128]{3,2,1,0:T(8,128)S(1)}, u32[]{:S(2)}, u32[]{:S(2)}) collective-permute-start(f32[4,8,128,128]{3,2,1,0:T(8,128)S(1)} %pair_blocks.1), channel_id=1, source_target_pairs={{0,1},{1,0},{2,3},{3,2},{4,5},{5,4},{6,7},{7,6},{8,9},{9,8},{10,11... | collective-permute-start | bytes 6291464 | tf_op jit(solution)/shard_map/ppermute | solution.py:287
  5.3 13.7 %collective-permute-start.3 = (f32[128,256]{1,0:T(8,128)S(1)}, f32[128,256]{1,0:T(8,128)S(1)}, u32[]{:S(2)}, u32[]{:S(2)}) collective-permute-start(f32[128,256]{1,0:T(8,128)S(1)} %copy-done.5), channel_id=1, source_target_pairs={{8,0},{12,4},{0,8},{4,12},{9,1},{13,5},{1,9},{5,13},{10,2},{14,6},... | collective-permute-start | bytes 393224 | tf_op jit(solution)/shard_map/ppermute | solution.py:324
  11.3 12.5 %collective-permute-start.7 = (f32[128,256]{1,0:T(8,128)S(1)}, f32[128,256]{1,0:T(8,128)S(1)}, u32[]{:S(2)}, u32[]{:S(2)}) collective-permute-start(f32[128,256]{1,0:T(8,128)S(1)} %copy-done.4), channel_id=1, source_target_pairs={{8,0},{12,4},{0,8},{4,12},{9,1},{13,5},{1,9},{5,13},{10,2},{14,6},... | collective-permute-start | bytes 393224 | tf_op jit(solution)/shard_map/ppermute | solution.py:324
  11.4 2.9 %copy-start.3 = (f32[128,256]{1,0:T(8,128)S(1)}, f32[128,256]{1,0:T(8,128)}, u32[]{:S(2)}) copy-start(f32[128,256]{1,0:T(8,128)} %get-tuple-element.31) | copy-start | bytes 393220
  14.3 9.6 %collective-permute-start.5 = (f32[128,256]{1,0:T(8,128)S(1)}, f32[128,256]{1,0:T(8,128)S(1)}, u32[]{:S(2)}, u32[]{:S(2)}) collective-permute-start(f32[128,256]{1,0:T(8,128)S(1)} %copy-done.3), channel_id=1, source_target_pairs={{0,4},{4,8},{8,12},{5,1},{9,5},{13,9},{2,6},{6,10},{10,14},{7,3},{... | collective-permute-start | bytes 393224 | tf_op jit(solution)/shard_map/ppermute | solution.py:417
  18.9 5.0 %collective-permute-start.4 = (f32[1,128,256]{2,1,0:T(8,128)S(1)}, f32[1,128,256]{2,1,0:T(8,128)S(1)}, u32[]{:S(2)}, u32[]{:S(2)}) collective-permute-start(f32[1,128,256]{2,1,0:T(8,128)S(1)} %bitcast.4), channel_id=1, source_target_pairs={{0,2},{1,3},{2,0},{3,1},{4,6},{5,7},{6,4},{7,5},{8,10},{9,11},{10,... | collective-permute-start | bytes 393224 | tf_op jit(solution)/shard_map/ppermute | solution.py:287
  23.8 6.4 %collective-permute-start.8 = (f32[1,128,256]{2,1,0:T(8,128)S(1)}, f32[1,128,256]{2,1,0:T(8,128)S(1)}, u32[]{:S(2)}, u32[]{:S(2)}) collective-permute-start(f32[1,128,256]{2,1,0:T(8,128)S(1)} %bitcast.2), channel_id=1, source_target_pairs={{0,2},{1,3},{2,0},{3,1},{4,6},{5,7},{6,4},{7,5},{8,10},{9,11},{10,... | collective-permute-start | bytes 393224 | tf_op jit(solution)/shard_map/ppermute | solution.py:287
  27.0 13.1 %collective-permute-start.6 = (f32[256,256]{1,0:T(8,128)S(1)}, f32[256,256]{1,0:T(8,128)S(1)}, u32[]{:S(2)}, u32[]{:S(2)}) collective-permute-start(f32[256,256]{1,0:T(8,128)S(1)} %get-tuple-element.32), channel_id=1, source_target_pairs={{0,2},{1,3},{2,0},{3,1},{4,6},{5,7},{6,4},{7,5},{8,10},{9,11},{10,... | collective-permute-start | bytes 786440 | tf_op jit(solution)/shard_map/ppermute | solution.py:287
  31.9 8.2 %collective-permute-start.9 = (f32[256,256]{1,0:T(8,128)S(1)}, f32[256,256]{1,0:T(8,128)S(1)}, u32[]{:S(2)}, u32[]{:S(2)}) collective-permute-start(f32[256,256]{1,0:T(8,128)S(1)} %get-tuple-element.37), channel_id=1, source_target_pairs={{0,2},{1,3},{2,0},{3,1},{4,6},{5,7},{6,4},{7,5},{8,10},{9,11},{10,... | collective-permute-start | bytes 786440 | tf_op jit(solution)/shard_map/ppermute | solution.py:287
  32.0 1.2 %collective-permute-start.10 = (f32[16,128]{1,0:T(8,128)S(1)}, f32[16,128]{1,0:T(8,128)S(1)}, u32[]{:S(2)}, u32[]{:S(2)}) collective-permute-start(f32[16,128]{1,0:T(8,128)S(1)} %get-tuple-element.38), channel_id=1, source_target_pairs={{0,1},{1,0},{2,3},{3,2},{4,5},{5,4},{6,7},{7,6},{8,9},{9,8},{10,11... | collective-permute-start | bytes 24584 | tf_op jit(solution)/shard_map/ppermute | solution.py:287
  33.2 4.6 %collective-permute-start.13 = (f32[16,128]{1,0:T(8,128)S(1)}, f32[16,128]{1,0:T(8,128)S(1)}, u32[]{:S(2)}, u32[]{:S(2)}) collective-permute-start(f32[16,128]{1,0:T(8,128)S(1)} %add.26), channel_id=1, source_target_pairs={{0,8},{1,11},{2,10},{3,9},{4,12},{5,15},{6,14},{7,13},{8,0},{9,3},... | collective-permute-start | bytes 24584 | tf_op jit(solution)/shard_map/ppermute | solution.py:295
  34.6 5.4 %collective-permute-start.14 = (f32[16,128]{1,0:T(8,128)S(1)}, f32[16,128]{1,0:T(8,128)S(1)}, u32[]{:S(2)}, u32[]{:S(2)}) collective-permute-start(f32[16,128]{1,0:T(8,128)S(1)} %add.26), channel_id=1, source_target_pairs={{0,12},{1,15},{2,14},{3,13},{4,8},{5,11},{6,10},{7,9},{8,4},{9,7},... | collective-permute-start | bytes 24584 | tf_op jit(solution)/shard_map/ppermute | solution.py:295
  35.7 4.3 %collective-permute-start.12 = (f32[16,128]{1,0:T(8,128)S(1)}, f32[16,128]{1,0:T(8,128)S(1)}, u32[]{:S(2)}, u32[]{:S(2)}) collective-permute-start(f32[16,128]{1,0:T(8,128)S(1)} %add.26), channel_id=1, source_target_pairs={{0,4},{1,7},{2,6},{3,5},{4,0},{5,3},{6,2},{7,1},{8,12},{9,15},{10,... | collective-permute-start | bytes 24584 | tf_op jit(solution)/shard_map/ppermute | solution.py:295
  37.9 2.2 %collective-permute-start.11 = (f32[16,128]{1,0:T(8,128)S(1)}, f32[16,128]{1,0:T(8,128)S(1)}, u32[]{:S(2)}, u32[]{:S(2)}) collective-permute-start(f32[16,128]{1,0:T(8,128)S(1)} %add.26), channel_id=1, source_target_pairs={{1,3},{3,1},{5,7},{7,5},{9,11},{11,9},{13,15},{15,13},{17,19},{19,... | collective-permute-start | bytes 24584 | tf_op jit(solution)/shard_map/ppermute | solution.py:295
  40.2 4.3 %collective-permute-start.15 = (f32[528,256]{1,0:T(8,128)S(1)}, f32[528,256]{1,0:T(8,128)S(1)}, u32[]{:S(2)}, u32[]{:S(2)}) collective-permute-start(f32[528,256]{1,0:T(8,128)S(1)} %pad_maximum_fusion.total), channel_id=1, source_target_pairs={{0,1},{1,0},{2,3},{3,2},{4,5},{5,4},{6,7},{7,6},{8,9},{9,8},{10,11... | collective-permute-start | bytes 1622024 | tf_op jit(solution)/shard_map/ppermute | solution.py:287

commit v7 on v6

--- a/solution.py
+++ b/solution.py
@@ -33,6 +33,10 @@
 def place():
     mpo = lax.axis_index("mpo")
     return lax.rem(mpo, 2), lax.rem(lax.div(mpo, 2), 2), lax.axis_index("sec")
+
+
+def chunk_start(chunk, core, half):
+    return (1 - core if chunk else core) * (half // 2)
 
 
 def sector_rows(wave, sector, block):
@@ -47,10 +51,8 @@
     rows = pltpu.make_async_copy(rows_hbm, rows_ref, sem.at[0])
     rows.start()
     wanted = [(halo, (1 - core) * (2 * half - 1) * block)]
-    first = core * half * block
-    for ref in sends:
-        wanted.append((ref, first + side * ref.shape[0]))
-        first += 2 * ref.shape[0]
+    for i, ref in enumerate(sends):
+        wanted.append((ref, (core * half + chunk_start(i, core, half)) * block + side * ref.shape[0]))
     reads = []
     for i, (ref, first) in enumerate(wanted):
         source = wave.at[pl.ds(pl.multiple_of(first, piece), ref.shape[0]), :]
@@ -178,15 +180,16 @@
     add_terms(n, order, offsets, src, lambda t: right[t], lambda s, t: left[s, t], acc, tbuf)
 
 
-def far_kernel(lo, shift, secs, chained, *refs):
+def far_kernel(chunk, shift, secs, *refs):
     refs = list(refs)
-    cls, cls_pair, rows_hbm, left, right, left_pair, right_pair, live, mine, other, halo, acc_in = refs[:12]
-    sums_in = refs.pop(12) if chained else None
-    acc, sums, src, tbuf, rows_ref, cls_ref, order, offsets, sem = refs[12:]
+    cls, cls_pair, rows_hbm, left, right, left_pair, right_pair, live, mine, other, acc_in = refs[:11]
+    halo, sums_in = (None, refs.pop(11)) if chunk else (refs.pop(11), None)
+    acc, sums, src, tbuf, rows_ref, cls_ref, order, offsets, sem = refs[11:]
     rows, cols = acc.shape
     half, terms, block, _ = left.shape
     count = rows // block
     core, side, sec = place()
+    lo = chunk_start(chunk, core, half)
     merged = mine.shape[0] == 1
 
     moves = [
@@ -196,13 +199,14 @@
     ]
     for move in moves:
         move.start()
-    acc[...] = acc_in[pl.ds(lo * block, rows), :]
+    acc[...] = acc_in[pl.ds(pl.multiple_of(lo * block, block), rows), :]
     for k in range(mine.shape[0]):
         for ref, x in ((mine, side), (other, 1 - side)):
             part = ref.shape[1]
             put(src, pl.multiple_of(k * rows + x * part, part), ref[k])
     halo_at = mine.shape[0] * rows
-    put(src, halo_at, halo[...])
+    if not chunk:
+        put(src, halo_at, halo[...])
     for move in moves:
         move.wait()
 
@@ -220,11 +224,12 @@
     n = pack(classes, far, order, offsets)
     left_of = lambda s, t: either(left, left_pair, t, lo + s)
     add_terms(n, order, offsets, src, right_of, left_of, acc, tbuf)
-    n = pack(classes, lambda c: (c == 4 - core, halo_at), order, offsets)
-    n = jnp.where(core == (0 if lo == 0 else 1), n, 0)
-    edge = core * (count - 1)
-    left_of = lambda s, t: either(left, left_pair, t, lo + edge)
-    add_terms(n, order, offsets, src, right_of, left_of, acc.at[pl.ds(pl.multiple_of(edge * block, block), block), :], tbuf)
+    if not chunk:
+        n = pack(classes, lambda c: (c == 4 - core, halo_at), order, offsets)
+        edge = core * (count - 1)
+        left_of = lambda s, t: either(left, left_pair, t, lo + edge)
+        edge_rows = acc.at[pl.ds(pl.multiple_of(edge * block, block), block), :]
+        add_terms(n, order, offsets, src, right_of, left_of, edge_rows, tbuf)
 
     cross = jnp.zeros((8, cols), F32)
     square = jnp.zeros((8, cols), F32)
@@ -239,33 +244,36 @@
         square += fold(value * value)
     fold = lambda v: sum(v[:, i : i + 128] for i in range(0, cols, 128))
     cross, square = fold(cross), fold(square)
-    if chained:
+    if chunk:
         cross, square = cross + sums_in[0:8, :], square + sums_in[8:16, :]
     sums[0:8, :] = cross
     sums[8:16, :] = square
 
 
-def final_kernel(sides, live, total, total_pair, applied, correction, buf, sem):
+def final_kernel(sides, half, live, total, total_pair, applied, correction, buf, sem):
     core, _, _ = place()
     rows = live.shape[0] // 2
-    pieces = sem.shape[1] // 2
-    piece = rows // pieces
+    block = rows // half
+    part = rows // 2
     moves = []
+    places = []
 
     def send(source, target, kind, i):
         moves.append(pltpu.make_async_copy(source, target, sem.at[kind, i]))
         moves[-1].start()
 
-    for i, (ref, c) in enumerate(((total, core), (total_pair, 1 - core))):
-        here = pl.ds(pl.multiple_of(c * rows, rows), rows)
-        send(ref.at[pl.ds(0, rows), :], applied.at[here, :], 0, i)
+    for ref, c in ((total, core), (total_pair, 1 - core)):
+        for chunk in range(2):
+            first = (c * half + chunk_start(chunk, c, half)) * block
+            here = pl.ds(pl.multiple_of(first, block), part)
+            source = ref.at[pl.ds(chunk * part, part), :]
+            places.append((source, here))
+            send(source, applied.at[here, :], 0, len(places) - 1)
     sums = total[rows : rows + 16, 0:128] + total_pair[rows : rows + 16, 0:128]
     rayleigh = jnp.sum(sums[0:8, :]) / (jnp.sum(sums[8:16, :]) * (1.0 / sides))
-    for i, (ref, c) in enumerate(((total, core), (total_pair, 1 - core))):
-        for p in range(pieces):
-            here = pl.ds(pl.multiple_of(c * rows + p * piece, piece), piece)
-            buf[here, :] = ref[pl.ds(p * piece, piece), :] - rayleigh * live[here, :]
-            send(buf.at[here, :], correction.at[here, :], 1, i * pieces + p)
+    for i, (source, here) in enumerate(places):
+        buf[here, :] = source[...] - rayleigh * live[here, :]
+        send(buf.at[here, :], correction.at[here, :], 1, i)
     for move in moves:
         move.wait()
 
@@ -333,11 +341,10 @@
 
     blocks = shape(half, terms, block, block)
     source_shape = ((half + 2) * block, 3 * wide)
-    sizes = (half // 2, half // 2)
     cls_pair = swap(term_charge, "mpo", 1)
     mine_a, mine_b, halo = pl.pallas_call(
         functools.partial(prepare_kernel, half),
-        out_shape=tuple(shape(size * block // 2, wide) for size in sizes) + (shape(block, wide),),
+        out_shape=(shape(part * block // 2, wide),) * 2 + (shape(block, wide),),
         in_specs=[ANY] * 2,
         out_specs=(VMEM,) * 3,
         scratch_shapes=[pltpu.SMEM((sector_count,), jnp.int32), pltpu.SemaphoreType.DMA((4,))],
@@ -357,7 +364,7 @@
     )(after(left_blocks, mine_a, cls_pair))
     left_pair = swap(left_send, "mpo", 1)
     far_a = far(mine_a)
-    right_pair = swap(after(right_blocks, mine_a), "mpo", 1)
+    right_pair = swap(after(right_blocks, left_send), "mpo", 1)
 
     lists = [pltpu.SMEM((2 * terms,), jnp.int32)] * 2
 
@@ -376,26 +383,25 @@
             name=name,
         )(*args)
 
-    def add_far(lo, count, far, acc, sums):
-        rows = count * block
-        extra = () if sums is None else (sums,)
+    def add_far(chunk, *args):
+        rows = part * block
         return pl.pallas_call(
-            functools.partial(far_kernel, lo, shift, secs, sums is not None),
+            functools.partial(far_kernel, chunk, shift, secs),
             out_shape=(shape(rows, cols), shape(16, 128)),
-            in_specs=[ANY] * 3 + [VMEM] * (9 + len(extra)),
+            in_specs=[ANY] * 3 + [VMEM] * (5 + len(args)),
             out_specs=(VMEM, VMEM),
             scratch_shapes=[
-                pltpu.VMEM((far[0].shape[0] * rows + block, 3 * wide), BF16),
-                pltpu.VMEM((count, 2 * GROUPS[0] * block, cols), BF16),
+                pltpu.VMEM(((1 if merged else 2) * rows + block, 3 * wide), BF16),
+                pltpu.VMEM((part, 2 * GROUPS[0] * block, cols), BF16),
                 pltpu.SMEM((sector_count,), jnp.int32),
                 pltpu.SMEM((2, terms), jnp.int32),
                 *lists,
                 pltpu.SemaphoreType.DMA((3,)),
             ],
-            compiler_params=params(32),
+            compiler_params=params(NEAR_VMEM),
             cost_estimate=cost(1, 1),
             name="far",
-        )(term_charge, cls_pair, block_rows, left, right, left_pair, right_pair, live, *far, halo, acc, *extra)
+        )(term_charge, cls_pair, block_rows, left, right, left_pair, right_pair, live, *args)
 
     left, right, src, live = pl.pallas_call(
         load_kernel,
@@ -418,9 +424,9 @@
     other_a = swap(after(far_a, acc), "mpo", 2)
     acc = near("pair_near", cls_pair, left_pair, right_pair, src, acc)
     other_b = swap(after(far_b, acc), "mpo", 2)
-    part_a, sums = add_far(0, sizes[0], (far_a, other_a), acc, None)
+    part_a, sums = add_far(0, far_a, other_a, acc, halo)
     recv_a = swap(part_a, "mpo", 2)
-    part_b, sums = add_far(sizes[0], sizes[1], (far_b, other_b), acc, sums)
+    part_b, sums = add_far(1, far_b, other_b, acc, sums)
     recv_b = swap(part_b, "mpo", 2)
 
     if secs == 4 and mpos == 4 and reps == 1:
@@ -434,7 +440,7 @@
 
     out = shape(sector_count * block, cols)
     return pl.pallas_call(
-        functools.partial(final_kernel, mpos // 2),
+        functools.partial(final_kernel, mpos // 2, half),
         out_shape=(out, out),
         in_specs=[VMEM] * 3,
         out_specs=(ANY, ANY),

time: 45.9 us -> 45.5 us (level); the launches traced: 45.9 us -> 46.1 us
  waiting for transfers between devices: 7.8 us -> 9.56 us
  Pallas kernels: 17.6 us -> 16.4 us
    ppermute x2, waiting for transfers between devices: 0.87 us -> 2.3 us  [far(): return lax.ppermute(array, 'sec', up + down)[None]]
    pallas_call x2, Pallas kernels: 5.79 us -> 5.06 us  [near(): pl.pallas_call(functools.partial(near_kernel, chained), out_shape=shape(h...]
    pallas_call x4, Pallas kernels: 7.9 us -> 7.39 us  [the longest x2 4.21 us: add_far(): pl.pallas_call(functools.partial(far_kernel, chunk, shift, secs), out_sha...]
  transfers between devices with their start and end apart: 16 -> 16, of which waited for: 7 -> 6; matrix products, arithmetic and copies ran while one was open for 0% -> 0% of each run, Pallas kernels for 35% -> 29%
where the time goes in v7:
time: 45.5 us; the launch traced here: 46.1 us
  starting transfers between devices  19.1 us (42%)
  Pallas kernels  16.4 us (36%)
  waiting for transfers between devices  9.56 us (21%)
  between operations  0.89 us (2%)
    ppermute x9, starting transfers between devices, swap(): return lax.ppermute(array, axis, pairs)  7.47 us
    pallas_call x2, Pallas kernels, near(): pl.pallas_call(functools.partial(near_kernel, chained), out_shape=shape(h...  5.06 us
    pallas_call x2, Pallas kernels, add_far(): pl.pallas_call(functools.partial(far_kernel, chunk, shift, secs), out_sha...  4.21 us
    ppermute x9, waiting for transfers between devices, swap(): return lax.ppermute(array, axis, pairs)  4.21 us
    ppermute x4, starting transfers between devices, spread_sum(): lax.ppermute(sums, ('sec', 'mpo'), [p for p in pairs if p[0] != p[1]])  4.14 us
    ppermute x1, starting transfers between devices, local(): halo = lax.ppermute(after(halo, acc), ('sec', 'mpo'), halo_pairs)  3.79 us
    ppermute x2, starting transfers between devices, far(): return lax.ppermute(array, 'sec', up + down)[None]  3.75 us
    ppermute x4, waiting for transfers between devices, spread_sum(): lax.ppermute(sums, ('sec', 'mpo'), [p for p in pairs if p[0] != p[1]])  3.04 us
  transfers between devices with their start and end apart: 16, of which 6 were waited for; matrix products, arithmetic and copies ran while one was open for 0% of the time, Pallas kernels for 29%

profile of v7, /device:TPU:0, one launch (start us, length us, event | category | flops | bytes accessed | tf_op | source)
XLA Modules:
  0.0 46.1 jit_solution(14184931137641697314)
XLA Ops:
  0.6 0.5 %collective-permute-start = (s32[8]{0:T(128)}, s32[8]{0:T(128)S(1)}, u32[]{:S(2)}, u32[]{:S(2)}) collective-permute-start(s32[8]{0:T(128)} %refs_0_.3), channel_id=1, source_target_pairs={{0,1},{1,0},{2,3},{3,2},{4,5},{5,4},{6,7},{7,6},{8,9},{9,8},{10,11... | collective-permute-start | bytes 104 | tf_op jit(solution)/shard_map/ppermute | solution.py:295
  1.1 1.8 %prepare.1 = (f32[128,256]{1,0:T(8,128)}, f32[128,256]{1,0:T(8,128)}, f32[128,256]{1,0:T(8,128)}) custom-call(s32[8]{0:T(128)} %refs_2_.3, f32[1024,256]{1,0:T(8,128)} %wave.3), custom_call_target="tpu_custom_call" | custom-call | flops 1 | bytes 1 | tf_op jit(solution)/shard_map/prepare/pallas_call | solution.py:345
  2.9 0.0 collective-permute-done.cls.refs_1_
  3.0 0.0 copy-start.5
  3.0 0.0 copy-start
  3.0 0.0 copy-start.1
  3.0 1.7 %pair_blocks.1 = f32[4,8,128,128]{3,2,1,0:T(8,128)S(1)} custom-call(f32[8,8,128,128]{3,2,1,0:T(8,128)} %left), custom_call_target="tpu_custom_call" | custom-call | flops 1 | bytes 1 | tf_op jit(solution)/shard_map/pair_blocks/pallas_call | solution.py:355
  4.7 0.0 copy-start.4
  4.7 0.0 copy-start.2
  4.7 0.1 collective-permute-start.1
  4.9 0.5 collective-permute-start.2
  5.3 0.0 copy-done.5
  5.3 3.7 %collective-permute-start.3 = (f32[128,256]{1,0:T(8,128)S(1)}, f32[128,256]{1,0:T(8,128)S(1)}, u32[]{:S(2)}, u32[]{:S(2)}) collective-permute-start(f32[128,256]{1,0:T(8,128)S(1)} %copy-done.5), channel_id=1, source_target_pairs={{8,0},{12,4},{0,8},{4,12},{9,1},{13,5},{1,9},{5,13},{10,2},{14,6},... | collective-permute-start | bytes 393224 | tf_op jit(solution)/shard_map/ppermute | solution.py:332
  9.0 0.0 copy-done
  9.0 2.2 %own_terms.1 = (f32[4,8,128,128]{3,2,1,0:T(8,128)S(1)}, f32[8,256,256]{2,1,0:T(8,128)S(1)}, bf16[768,768]{1,0:T(8,128)(2,1)S(1)}, f32[1024,256]{1,0:T(8,128)S(1)}) custom-call(f32[8,8,128,128]{3,2,1,0:T(8,128)} %left, f32[8,256,256]{2,1,0:T(8,128)} %right_hbm.1, s32[8]{0:T(128)S(1)} %copy-done.1, f32[1024,256]{1,0:T(8,128)S(1)} %copy-done, ...), custom_call_target="tpu_custom_call" | custom-call | flops 1 | bytes 1 | tf_op jit(solution)/shard_map/own_terms/pallas_call | solution.py:406
  11.2 0.1 collective-permute-start.7
  11.3 0.0 copy-done.2
  11.3 1.5 %own_near.1.refs_0_ = f32[512,256]{1,0:T(8,128)S(1)} custom-call(s32[8]{0:T(128)S(1)} %copy-done.2, f32[4,8,128,128]{3,2,1,0:T(8,128)S(1)} %get-tuple-element.24.left.refs_3_, f32[8,256,256]{2,1,0:T(8,128)S(1)} %get-tuple-element.25.right.refs_4_, bf16[768,768]{1,0:T(8,128)(2,1)S(1)} %get-tuple-element.28.src), custom_call_target="tpu_custom_call" | custom-call | flops 1 | bytes 1 | tf_op jit(solution)/shard_map/own_near/pallas_call | solution.py:373
  12.8 3.8 %collective-permute-start.5 = (f32[128,256]{1,0:T(8,128)S(1)}, f32[128,256]{1,0:T(8,128)S(1)}, u32[]{:S(2)}, u32[]{:S(2)}) collective-permute-start(f32[128,256]{1,0:T(8,128)S(1)} %copy-done.3), channel_id=1, source_target_pairs={{0,4},{4,8},{8,12},{5,1},{9,5},{13,9},{2,6},{6,10},{10,14},{7,3},{... | collective-permute-start | bytes 393224 | tf_op jit(solution)/shard_map/ppermute | solution.py:423
  16.6 2.3 %collective-permute-done.3 = f32[128,256]{1,0:T(8,128)S(1)} collective-permute-done((f32[128,256]{1,0:T(8,128)S(1)}, f32[128,256]{1,0:T(8,128)S(1)}, u32[]{:S(2)}, u32[]{:S(2)}) %collective-permute-start.3) | collective-permute-done | bytes 131104 | tf_op jit(solution)/shard_map/ppermute | solution.py:332
  18.9 1.8 %collective-permute-start.4 = (f32[1,128,256]{2,1,0:T(8,128)S(1)}, f32[1,128,256]{2,1,0:T(8,128)S(1)}, u32[]{:S(2)}, u32[]{:S(2)}) collective-permute-start(f32[1,128,256]{2,1,0:T(8,128)S(1)} %bitcast.4), channel_id=1, source_target_pairs={{0,2},{1,3},{2,0},{3,1},{4,6},{5,7},{6,4},{7,5},{8,10},{9,11},{10,... | collective-permute-start | bytes 393224 | tf_op jit(solution)/shard_map/ppermute | solution.py:295
  20.7 0.0 collective-permute-done.1.left.refs_5_
  20.7 0.0 collective-permute-done.2.right.refs_6_
  20.7 3.6 %pair_near.1.refs_10_ = f32[512,256]{1,0:T(8,128)S(1)} custom-call(s32[8]{0:T(128)S(1)} %collective-permute-done.cls.refs_1_, f32[4,8,128,128]{3,2,1,0:T(8,128)S(1)} %collective-permute-done.1.left.refs_5_, f32[8,256,256]{2,1,0:T(8,128)S(1)} %collective-permute-done.2.right.refs_6_, bf16[768,768]{1,0:T(8,128)(2,1)S(1)} %get-tuple-element.28.src, ...), custom_call_target="tpu_custom_call" | custom-call | flops 1 | bytes 1 | tf_op jit(solution)/shard_map/pair_near/pallas_call | solution.py:373
  24.3 0.0 collective-permute-done.7
  24.3 0.1 collective-permute-start.8
  24.4 0.0 collective-permute-done.5.refs_11_
  24.4 0.0 collective-permute-done.4.refs_9_
  24.4 2.5 %far.2 = (f32[256,256]{1,0:T(8,128)S(1)}, f32[16,128]{1,0:T(8,128)S(1)}) custom-call(s32[8]{0:T(128)S(1)} %copy-done.2, s32[8]{0:T(128)S(1)} %collective-permute-done.cls.refs_1_, s32[8]{0:T(128)S(1)} %copy-done.1, f32[4,8,128,128]{3,2,1,0:T(8,128)S(1)} %get-tuple-element.24.left.refs_3_, f32[8,256,256]{2,1,0:T(8,128)S(1)} %get-tuple-element.25.right.refs_4_, ...), custom_call_target="tpu_custom_call" | custom-call | flops 1 | bytes 1 | tf_op jit(solution)/shard_map/far/pallas_call | solution.py:388
  26.9 2.1 %collective-permute-start.6 = (f32[256,256]{1,0:T(8,128)S(1)}, f32[256,256]{1,0:T(8,128)S(1)}, u32[]{:S(2)}, u32[]{:S(2)}) collective-permute-start(f32[256,256]{1,0:T(8,128)S(1)} %get-tuple-element.32), channel_id=1, source_target_pairs={{0,2},{1,3},{2,0},{3,1},{4,6},{5,7},{6,4},{7,5},{8,10},{9,11},{10,... | collective-permute-start | bytes 786440 | tf_op jit(solution)/shard_map/ppermute | solution.py:295
  29.0 1.5 %collective-permute-done.8.refs_9_ = f32[1,128,256]{2,1,0:T(8,128)S(1)} collective-permute-done((f32[1,128,256]{2,1,0:T(8,128)S(1)}, f32[1,128,256]{2,1,0:T(8,128)S(1)}, u32[]{:S(2)}, u32[]{:S(2)}) %collective-permute-start.8) | collective-permute-done | bytes 131104 | tf_op jit(solution)/shard_map/ppermute | solution.py:295
  30.5 1.7 %far.3 = (f32[256,256]{1,0:T(8,128)S(1)}, f32[16,128]{1,0:T(8,128)S(1)}) custom-call(s32[8]{0:T(128)S(1)} %copy-done.2, s32[8]{0:T(128)S(1)} %collective-permute-done.cls.refs_1_, s32[8]{0:T(128)S(1)} %copy-done.1, f32[4,8,128,128]{3,2,1,0:T(8,128)S(1)} %get-tuple-element.24.left.refs_3_, f32[8,256,256]{2,1,0:T(8,128)S(1)} %get-tuple-element.25.right.refs_4_, ...), custom_call_target="tpu_custom_call" | custom-call | flops 1 | bytes 1 | tf_op jit(solution)/shard_map/far/pallas_call | solution.py:388
  32.2 0.1 collective-permute-start.9
  32.2 0.1 collective-permute-start.10
  32.3 1.2 %collective-permute-done.10 = f32[16,128]{1,0:T(8,128)S(1)} collective-permute-done((f32[16,128]{1,0:T(8,128)S(1)}, f32[16,128]{1,0:T(8,128)S(1)}, u32[]{:S(2)}, u32[]{:S(2)}) %collective-permute-start.10) | collective-permute-done | bytes 8224 | tf_op jit(solution)/shard_map/ppermute | solution.py:295
  33.5 1.7 %collective-permute-start.13 = (f32[16,128]{1,0:T(8,128)S(1)}, f32[16,128]{1,0:T(8,128)S(1)}, u32[]{:S(2)}, u32[]{:S(2)}) collective-permute-start(f32[16,128]{1,0:T(8,128)S(1)} %add.26), channel_id=1, source_target_pairs={{0,8},{1,11},{2,10},{3,9},{4,12},{5,15},{6,14},{7,13},{8,0},{9,3},... | collective-permute-start | bytes 24584 | tf_op jit(solution)/shard_map/ppermute | solution.py:303
  35.2 0.7 %collective-permute-start.14 = (f32[16,128]{1,0:T(8,128)S(1)}, f32[16,128]{1,0:T(8,128)S(1)}, u32[]{:S(2)}, u32[]{:S(2)}) collective-permute-start(f32[16,128]{1,0:T(8,128)S(1)} %add.26), channel_id=1, source_target_pairs={{0,12},{1,15},{2,14},{3,13},{4,8},{5,11},{6,10},{7,9},{8,4},{9,7},... | collective-permute-start | bytes 24584 | tf_op jit(solution)/shard_map/ppermute | solution.py:303
  36.0 1.0 %collective-permute-start.12 = (f32[16,128]{1,0:T(8,128)S(1)}, f32[16,128]{1,0:T(8,128)S(1)}, u32[]{:S(2)}, u32[]{:S(2)}) collective-permute-start(f32[16,128]{1,0:T(8,128)S(1)} %add.26), channel_id=1, source_target_pairs={{0,4},{1,7},{2,6},{3,5},{4,0},{5,3},{6,2},{7,1},{8,12},{9,15},{10,... | collective-permute-start | bytes 24584 | tf_op jit(solution)/shard_map/ppermute | solution.py:303
  37.0 1.1 %collective-permute-done.13 = f32[16,128]{1,0:T(8,128)S(1)} collective-permute-done((f32[16,128]{1,0:T(8,128)S(1)}, f32[16,128]{1,0:T(8,128)S(1)}, u32[]{:S(2)}, u32[]{:S(2)}) %collective-permute-start.13) | collective-permute-done | bytes 8224 | tf_op jit(solution)/shard_map/ppermute | solution.py:303
  38.0 0.7 %collective-permute-start.11 = (f32[16,128]{1,0:T(8,128)S(1)}, f32[16,128]{1,0:T(8,128)S(1)}, u32[]{:S(2)}, u32[]{:S(2)}) collective-permute-start(f32[16,128]{1,0:T(8,128)S(1)} %add.26), channel_id=1, source_target_pairs={{1,3},{3,1},{5,7},{7,5},{9,11},{11,9},{13,15},{15,13},{17,19},{19,... | collective-permute-start | bytes 24584 | tf_op jit(solution)/shard_map/ppermute | solution.py:303
  38.7 2.0 %collective-permute-done.14 = f32[16,128]{1,0:T(8,128)S(1)} collective-permute-done((f32[16,128]{1,0:T(8,128)S(1)}, f32[16,128]{1,0:T(8,128)S(1)}, u32[]{:S(2)}, u32[]{:S(2)}) %collective-permute-start.14) | collective-permute-done | bytes 8224 | tf_op jit(solution)/shard_map/ppermute | solution.py:303
  40.7 0.0 collective-permute-done.12
  40.7 0.0 collective-permute-done.11
  40.7 0.0 collective-permute-done.6
  40.8 0.0 collective-permute-done.9
  40.9 2.3 %collective-permute-start.15 = (f32[528,256]{1,0:T(8,128)S(1)}, f32[528,256]{1,0:T(8,128)S(1)}, u32[]{:S(2)}, u32[]{:S(2)}) collective-permute-start(f32[528,256]{1,0:T(8,128)S(1)} %pad_maximum_fusion.total), channel_id=1, source_target_pairs={{0,1},{1,0},{2,3},{3,2},{4,5},{5,4},{6,7},{7,6},{8,9},{9,8},{10,11... | collective-permute-start | bytes 1622024 | tf_op jit(solution)/shard_map/ppermute | solution.py:295
  43.2 1.6 %collective-permute-done.15.total_pair = f32[528,256]{1,0:T(8,128)S(1)} collective-permute-done((f32[528,256]{1,0:T(8,128)S(1)}, f32[528,256]{1,0:T(8,128)S(1)}, u32[]{:S(2)}, u32[]{:S(2)}) %collective-permute-start.15) | collective-permute-done | bytes 540704 | tf_op jit(solution)/shard_map/ppermute | solution.py:295
  44.8 1.4 %residual.1 = (f32[1024,256]{1,0:T(8,128)}, f32[1024,256]{1,0:T(8,128)}) custom-call(f32[1024,256]{1,0:T(8,128)S(1)} %get-tuple-element.23.refs_7_.live, f32[528,256]{1,0:T(8,128)S(1)} %pad_maximum_fusion.total, f32[528,256]{1,0:T(8,128)S(1)} %collective-permute-done.15.total_pair), custom_call_target="tpu_custom_call" | custom-call | flops 1 | bytes 1 | tf_op jit(solution)/shard_map/residual/pallas_call | solution.py:442
  (10 shorter events, 0.1 us)
Async XLA Ops:
  0.6 2.3 %collective-permute-start = (s32[8]{0:T(128)}, s32[8]{0:T(128)S(1)}, u32[]{:S(2)}, u32[]{:S(2)}) collective-permute-start(s32[8]{0:T(128)} %refs_0_.3), channel_id=1, source_target_pairs={{0,1},{1,0},{2,3},{3,2},{4,5},{5,4},{6,7},{7,6},{8,9},{9,8},{10,11... | collective-permute-start | bytes 104 | tf_op jit(solution)/shard_map/ppermute | solution.py:295
  3.0 2.3 %copy-start.5 = (f32[128,256]{1,0:T(8,128)S(1)}, f32[128,256]{1,0:T(8,128)}, u32[]{:S(2)}) copy-start(f32[128,256]{1,0:T(8,128)} %get-tuple-element.21) | copy-start | bytes 393220
  3.0 6.0 %copy-start = (f32[1024,256]{1,0:T(8,128)S(1)}, f32[1024,256]{1,0:T(8,128)}, u32[]{:S(2)}) copy-start(f32[1024,256]{1,0:T(8,128)} %wave.3) | copy-start | bytes 3145732
  3.0 6.0 %copy-start.1 = (s32[8]{0:T(128)S(1)}, s32[8]{0:T(128)}, u32[]{:S(2)}) copy-start(s32[8]{0:T(128)} %refs_2_.3) | copy-start | bytes 100
  4.7 6.5 %copy-start.4 = (f32[128,256]{1,0:T(8,128)S(1)}, f32[128,256]{1,0:T(8,128)}, u32[]{:S(2)}) copy-start(f32[128,256]{1,0:T(8,128)} %get-tuple-element.34) | copy-start | bytes 393220
  4.7 6.6 %copy-start.2 = (s32[8]{0:T(128)S(1)}, s32[8]{0:T(128)}, u32[]{:S(2)}) copy-start(s32[8]{0:T(128)} %refs_0_.3) | copy-start | bytes 100
  4.7 16.0 %collective-permute-start.1 = (f32[4,8,128,128]{3,2,1,0:T(8,128)S(1)}, f32[4,8,128,128]{3,2,1,0:T(8,128)S(1)}, u32[]{:S(2)}, u32[]{:S(2)}) collective-permute-start(f32[4,8,128,128]{3,2,1,0:T(8,128)S(1)} %pair_blocks.1), channel_id=1, source_target_pairs={{0,1},{1,0},{2,3},{3,2},{4,5},{5,4},{6,7},{7,6},{8,9},{9,8},{10,11... | collective-permute-start | bytes 6291464 | tf_op jit(solution)/shard_map/ppermute | solution.py:295
  4.9 15.9 %collective-permute-start.2 = (f32[8,256,256]{2,1,0:T(8,128)}, f32[8,256,256]{2,1,0:T(8,128)S(1)}, u32[]{:S(2)}, u32[]{:S(2)}) collective-permute-start(f32[8,256,256]{2,1,0:T(8,128)} %right_hbm.1), channel_id=1, source_target_pairs={{0,1},{1,0},{2,3},{3,2},{4,5},{5,4},{6,7},{7,6},{8,9},{9,8},{10,11... | collective-permute-start | bytes 6291464 | tf_op jit(solution)/shard_map/ppermute | solution.py:295
  5.3 13.6 %collective-permute-start.3 = (f32[128,256]{1,0:T(8,128)S(1)}, f32[128,256]{1,0:T(8,128)S(1)}, u32[]{:S(2)}, u32[]{:S(2)}) collective-permute-start(f32[128,256]{1,0:T(8,128)S(1)} %copy-done.5), channel_id=1, source_target_pairs={{8,0},{12,4},{0,8},{4,12},{9,1},{13,5},{1,9},{5,13},{10,2},{14,6},... | collective-permute-start | bytes 393224 | tf_op jit(solution)/shard_map/ppermute | solution.py:332
  11.2 13.1 %collective-permute-start.7 = (f32[128,256]{1,0:T(8,128)S(1)}, f32[128,256]{1,0:T(8,128)S(1)}, u32[]{:S(2)}, u32[]{:S(2)}) collective-permute-start(f32[128,256]{1,0:T(8,128)S(1)} %copy-done.4), channel_id=1, source_target_pairs={{8,0},{12,4},{0,8},{4,12},{9,1},{13,5},{1,9},{5,13},{10,2},{14,6},... | collective-permute-start | bytes 393224 | tf_op jit(solution)/shard_map/ppermute | solution.py:332
  11.3 1.5 %copy-start.3 = (f32[128,256]{1,0:T(8,128)S(1)}, f32[128,256]{1,0:T(8,128)}, u32[]{:S(2)}) copy-start(f32[128,256]{1,0:T(8,128)} %get-tuple-element.31) | copy-start | bytes 393220
  12.8 11.5 %collective-permute-start.5 = (f32[128,256]{1,0:T(8,128)S(1)}, f32[128,256]{1,0:T(8,128)S(1)}, u32[]{:S(2)}, u32[]{:S(2)}) collective-permute-start(f32[128,256]{1,0:T(8,128)S(1)} %copy-done.3), channel_id=1, source_target_pairs={{0,4},{4,8},{8,12},{5,1},{9,5},{13,9},{2,6},{6,10},{10,14},{7,3},{... | collective-permute-start | bytes 393224 | tf_op jit(solution)/shard_map/ppermute | solution.py:423
  18.9 5.5 %collective-permute-start.4 = (f32[1,128,256]{2,1,0:T(8,128)S(1)}, f32[1,128,256]{2,1,0:T(8,128)S(1)}, u32[]{:S(2)}, u32[]{:S(2)}) collective-permute-start(f32[1,128,256]{2,1,0:T(8,128)S(1)} %bitcast.4), channel_id=1, source_target_pairs={{0,2},{1,3},{2,0},{3,1},{4,6},{5,7},{6,4},{7,5},{8,10},{9,11},{10,... | collective-permute-start | bytes 393224 | tf_op jit(solution)/shard_map/ppermute | solution.py:295
  24.3 6.2 %collective-permute-start.8 = (f32[1,128,256]{2,1,0:T(8,128)S(1)}, f32[1,128,256]{2,1,0:T(8,128)S(1)}, u32[]{:S(2)}, u32[]{:S(2)}) collective-permute-start(f32[1,128,256]{2,1,0:T(8,128)S(1)} %bitcast.2), channel_id=1, source_target_pairs={{0,2},{1,3},{2,0},{3,1},{4,6},{5,7},{6,4},{7,5},{8,10},{9,11},{10,... | collective-permute-start | bytes 393224 | tf_op jit(solution)/shard_map/ppermute | solution.py:295
  26.9 13.8 %collective-permute-start.6 = (f32[256,256]{1,0:T(8,128)S(1)}, f32[256,256]{1,0:T(8,128)S(1)}, u32[]{:S(2)}, u32[]{:S(2)}) collective-permute-start(f32[256,256]{1,0:T(8,128)S(1)} %get-tuple-element.32), channel_id=1, source_target_pairs={{0,2},{1,3},{2,0},{3,1},{4,6},{5,7},{6,4},{7,5},{8,10},{9,11},{10,... | collective-permute-start | bytes 786440 | tf_op jit(solution)/shard_map/ppermute | solution.py:295
  32.2 8.6 %collective-permute-start.9 = (f32[256,256]{1,0:T(8,128)S(1)}, f32[256,256]{1,0:T(8,128)S(1)}, u32[]{:S(2)}, u32[]{:S(2)}) collective-permute-start(f32[256,256]{1,0:T(8,128)S(1)} %get-tuple-element.37), channel_id=1, source_target_pairs={{0,2},{1,3},{2,0},{3,1},{4,6},{5,7},{6,4},{7,5},{8,10},{9,11},{10,... | collective-permute-start | bytes 786440 | tf_op jit(solution)/shard_map/ppermute | solution.py:295
  32.2 1.2 %collective-permute-start.10 = (f32[16,128]{1,0:T(8,128)S(1)}, f32[16,128]{1,0:T(8,128)S(1)}, u32[]{:S(2)}, u32[]{:S(2)}) collective-permute-start(f32[16,128]{1,0:T(8,128)S(1)} %get-tuple-element.38), channel_id=1, source_target_pairs={{0,1},{1,0},{2,3},{3,2},{4,5},{5,4},{6,7},{7,6},{8,9},{9,8},{10,11... | collective-permute-start | bytes 24584 | tf_op jit(solution)/shard_map/ppermute | solution.py:295
  33.5 4.5 %collective-permute-start.13 = (f32[16,128]{1,0:T(8,128)S(1)}, f32[16,128]{1,0:T(8,128)S(1)}, u32[]{:S(2)}, u32[]{:S(2)}) collective-permute-start(f32[16,128]{1,0:T(8,128)S(1)} %add.26), channel_id=1, source_target_pairs={{0,8},{1,11},{2,10},{3,9},{4,12},{5,15},{6,14},{7,13},{8,0},{9,3},... | collective-permute-start | bytes 24584 | tf_op jit(solution)/shard_map/ppermute | solution.py:303
  35.2 5.4 %collective-permute-start.14 = (f32[16,128]{1,0:T(8,128)S(1)}, f32[16,128]{1,0:T(8,128)S(1)}, u32[]{:S(2)}, u32[]{:S(2)}) collective-permute-start(f32[16,128]{1,0:T(8,128)S(1)} %add.26), channel_id=1, source_target_pairs={{0,12},{1,15},{2,14},{3,13},{4,8},{5,11},{6,10},{7,9},{8,4},{9,7},... | collective-permute-start | bytes 24584 | tf_op jit(solution)/shard_map/ppermute | solution.py:303
  36.0 4.7 %collective-permute-start.12 = (f32[16,128]{1,0:T(8,128)S(1)}, f32[16,128]{1,0:T(8,128)S(1)}, u32[]{:S(2)}, u32[]{:S(2)}) collective-permute-start(f32[16,128]{1,0:T(8,128)S(1)} %add.26), channel_id=1, source_target_pairs={{0,4},{1,7},{2,6},{3,5},{4,0},{5,3},{6,2},{7,1},{8,12},{9,15},{10,... | collective-permute-start | bytes 24584 | tf_op jit(solution)/shard_map/ppermute | solution.py:303
  38.0 2.7 %collective-permute-start.11 = (f32[16,128]{1,0:T(8,128)S(1)}, f32[16,128]{1,0:T(8,128)S(1)}, u32[]{:S(2)}, u32[]{:S(2)}) collective-permute-start(f32[16,128]{1,0:T(8,128)S(1)} %add.26), channel_id=1, source_target_pairs={{1,3},{3,1},{5,7},{7,5},{9,11},{11,9},{13,15},{15,13},{17,19},{19,... | collective-permute-start | bytes 24584 | tf_op jit(solution)/shard_map/ppermute | solution.py:303
  40.9 3.9 %collective-permute-start.15 = (f32[528,256]{1,0:T(8,128)S(1)}, f32[528,256]{1,0:T(8,128)S(1)}, u32[]{:S(2)}, u32[]{:S(2)}) collective-permute-start(f32[528,256]{1,0:T(8,128)S(1)} %pad_maximum_fusion.total), channel_id=1, source_target_pairs={{0,1},{1,0},{2,3},{3,2},{4,5},{5,4},{6,7},{7,6},{8,9},{9,8},{10,11... | collective-permute-start | bytes 1622024 | tf_op jit(solution)/shard_map/ppermute | solution.py:295

commit v8 on v7

--- a/solution.py
+++ b/solution.py
@@ -185,8 +185,10 @@
     cls, cls_pair, rows_hbm, left, right, left_pair, right_pair, live, mine, other, acc_in = refs[:11]
     halo, sums_in = (None, refs.pop(11)) if chunk else (refs.pop(11), None)
     acc, sums, src, tbuf, rows_ref, cls_ref, order, offsets, sem = refs[11:]
-    rows, cols = acc.shape
+    cols = acc.shape[1]
     half, terms, block, _ = left.shape
+    rows = half // 2 * block
+    whole, acc = acc, acc.at[pl.ds(0, rows), :]
     count = rows // block
     core, side, sec = place()
     lo = chunk_start(chunk, core, half)
@@ -248,6 +250,26 @@
         cross, square = cross + sums_in[0:8, :], square + sums_in[8:16, :]
     sums[0:8, :] = cross
     sums[8:16, :] = square
+    if chunk:
+        whole[rows:, :] = jnp.zeros((whole.shape[0] - rows, cols), F32)
+        whole[rows : rows + 16, 0:128] = sums[...]
+
+
+def add_kernel(part, recv, total):
+    total[...] = part[...] + recv[...]
+
+
+def combine_kernel(total_a, part_b, recv_b, sums, first, second, third, total):
+    at = total_a.shape[0]
+    rows = 2 * at
+    even = place()[0] == 0
+    total[0:at, :] = total_a[...]
+    total[at:rows, :] = part_b[0:at, :] + recv_b[0:at, :]
+    total[rows:, :] = jnp.zeros((total.shape[0] - rows, total.shape[1]), F32)
+    rest = second[...] + third[...]
+    total[rows : rows + 16, 0:128] = jnp.where(even, (sums[...] + first[...]) + rest, first[...])
+    total[rows + 16 : rows + 32, 0:128] = jnp.where(even, 0.0, rest)
+    total[rows + 32 : rows + 48, 0:128] = recv_b[at : at + 16, 0:128]
 
 
 def final_kernel(sides, half, live, total, total_pair, applied, correction, buf, sem):
@@ -269,7 +291,9 @@
             source = ref.at[pl.ds(chunk * part, part), :]
             places.append((source, here))
             send(source, applied.at[here, :], 0, len(places) - 1)
-    sums = total[rows : rows + 16, 0:128] + total_pair[rows : rows + 16, 0:128]
+    either = lambda c, at: jnp.where(core == c, total[at : at + 16, 0:128], total_pair[at : at + 16, 0:128])
+    nearest = total[rows + 32 : rows + 48, 0:128] + total_pair[rows + 32 : rows + 48, 0:128]
+    sums = either(0, rows) + ((nearest + either(1, rows)) + either(1, rows + 16))
     rayleigh = jnp.sum(sums[0:8, :]) / (jnp.sum(sums[8:16, :]) * (1.0 / sides))
     for i, (source, here) in enumerate(places):
         buf[here, :] = source[...] - rayleigh * live[here, :]
@@ -295,14 +319,12 @@
     return lax.ppermute(array, axis, pairs)
 
 
-def spread_sum(sums):
-    sums = sums + swap(sums, "mpo", 1)
+def far_parts(sums):
     parts = []
-    for bit in range(4):
+    for bit in range(1, 4):
         pairs = [(4 * z + m, 4 * (z ^ bit) + (m ^ 2 if m % 2 else m)) for z in range(4) for m in range(4)]
-        parts.append(lax.ppermute(sums, ("sec", "mpo"), [p for p in pairs if p[0] != p[1]]))
-    parts[0] = jnp.where(lax.axis_index("mpo") % 2 == 0, sums, parts[0])
-    return (parts[0] + parts[1]) + (parts[2] + parts[3])
+        parts.append(lax.ppermute(sums, ("sec", "mpo"), pairs))
+    return parts
 
 
 def after(array, *others):
@@ -387,7 +409,7 @@
         rows = part * block
         return pl.pallas_call(
             functools.partial(far_kernel, chunk, shift, secs),
-            out_shape=(shape(rows, cols), shape(16, 128)),
+            out_shape=(shape(rows + 16 * chunk, cols), shape(16, 128)),
             in_specs=[ANY] * 3 + [VMEM] * (5 + len(args)),
             out_specs=(VMEM, VMEM),
             scratch_shapes=[
@@ -428,14 +450,32 @@
     recv_a = swap(part_a, "mpo", 2)
     part_b, sums = add_far(1, far_b, other_b, acc, sums)
     recv_b = swap(part_b, "mpo", 2)
-
     if secs == 4 and mpos == 4 and reps == 1:
-        sums = spread_sum(sums)
+        sums = sums + swap(sums, "mpo", 1)
+        parts = far_parts(sums)
     else:
-        sums = lax.psum(sums, ("sec", "rep"))
-        sums = sums + swap(sums, "mpo", 2)
-    sums = jnp.pad(sums, ((0, 0), (0, cols - sums.shape[1])))
-    total = jnp.concatenate([part_a + recv_a, part_b + after(recv_b, sums), sums])
+        own = sums
+        sums = lax.psum(sums, ("sec", "rep", "mpo"))
+        parts = [jnp.zeros_like(sums)] * 2 + [-swap(own, "mpo", 2)]
+        parts[2] = parts[2] + swap(parts[2], "mpo", 1)
+    total_a = pl.pallas_call(
+        add_kernel,
+        out_shape=shape(part * block, cols),
+        in_specs=[VMEM] * 2,
+        out_specs=VMEM,
+        compiler_params=params(NEAR_VMEM),
+        cost_estimate=cost(1e9, 1),
+        name="first_total",
+    )(part_a, recv_a)
+    total = pl.pallas_call(
+        combine_kernel,
+        out_shape=shape(half * block + 48, cols),
+        in_specs=[VMEM] * 7,
+        out_specs=VMEM,
+        compiler_params=params(NEAR_VMEM),
+        cost_estimate=cost(1, 1),
+        name="totals",
+    )(total_a, part_b, recv_b, sums, *parts)
     total_pair = swap(total, "mpo", 1)
 
     out = shape(sector_count * block, cols)

time: 45.5 us -> 44.1 us (0.969); the launches traced: 46.1 us -> 43.8 us
  waiting for transfers between devices: 9.56 us -> 7.45 us
    ppermute x2, waiting for transfers between devices: 2.3 us -> 0.91 us  [far(): return lax.ppermute(array, 'sec', up + down)[None]]
    ppermute x9, waiting for transfers between devices: 4.21 us -> 3.24 us  [swap(): return lax.ppermute(array, axis, pairs)]
    ppermute x4 -> x3, starting transfers between devices: 4.14 us -> 4.39 us  [far_parts(): parts.append(lax.ppermute(sums, ('sec', 'mpo'), pairs))]
    ppermute x4 -> x3, waiting for transfers between devices: 3.04 us -> 3.29 us  [far_parts(): parts.append(lax.ppermute(sums, ('sec', 'mpo'), pairs))]
  transfers between devices with their start and end apart: 16 -> 15, of which waited for: 6 -> 6; matrix products, arithmetic and copies ran while one was open for 0% -> 0% of each run, Pallas kernels for 29% -> 30%
where the time goes in v8:
time: 44.1 us; the launch traced here: 43.8 us
  starting transfers between devices  19.2 us (44%)
  Pallas kernels  16.2 us (37%)
  waiting for transfers between devices  7.45 us (17%)
  between operations  0.8 us (2%)
    ppermute x9, starting transfers between devices, swap(): return lax.ppermute(array, axis, pairs)  7.3 us
    pallas_call x2, Pallas kernels, near(): pl.pallas_call(functools.partial(near_kernel, chained), out_shape=shape(h...  5.05 us
    ppermute x3, starting transfers between devices, far_parts(): parts.append(lax.ppermute(sums, ('sec', 'mpo'), pairs))  4.39 us
    pallas_call x2, Pallas kernels, add_far(): pl.pallas_call(functools.partial(far_kernel, chunk, shift, secs), out_sha...  3.97 us
    ppermute x1, starting transfers between devices, local(): halo = lax.ppermute(after(halo, acc), ('sec', 'mpo'), halo_pairs)  3.79 us
    ppermute x2, starting transfers between devices, far(): return lax.ppermute(array, 'sec', up + down)[None]  3.75 us
    ppermute x3, waiting for transfers between devices, far_parts(): parts.append(lax.ppermute(sums, ('sec', 'mpo'), pairs))  3.29 us
    ppermute x9, waiting for transfers between devices, swap(): return lax.ppermute(array, axis, pairs)  3.24 us
  transfers between devices with their start and end apart: 15, of which 6 were waited for; matrix products, arithmetic and copies ran while one was open for 0% of the time, Pallas kernels for 30%

profile of v8, /device:TPU:0, one launch (start us, length us, event | category | flops | bytes accessed | tf_op | source)
XLA Modules:
  0.0 43.8 jit_solution(4028570888751818259)
XLA Ops:
  0.6 0.5 %collective-permute-start = (s32[8]{0:T(128)}, s32[8]{0:T(128)S(1)}, u32[]{:S(2)}, u32[]{:S(2)}) collective-permute-start(s32[8]{0:T(128)} %refs_0_.3), channel_id=1, source_target_pairs={{0,1},{1,0},{2,3},{3,2},{4,5},{5,4},{6,7},{7,6},{8,9},{9,8},{10,11... | collective-permute-start | bytes 104 | tf_op jit(solution)/shard_map/ppermute | solution.py:319
  1.1 1.8 %prepare.1 = (f32[128,256]{1,0:T(8,128)}, f32[128,256]{1,0:T(8,128)}, f32[128,256]{1,0:T(8,128)}) custom-call(s32[8]{0:T(128)} %refs_2_.3, f32[1024,256]{1,0:T(8,128)} %wave.3), custom_call_target="tpu_custom_call" | custom-call | flops 1 | bytes 1 | tf_op jit(solution)/shard_map/prepare/pallas_call | solution.py:367
  3.0 0.0 collective-permute-done.cls.refs_1_
  3.0 0.0 copy-start.5
  3.0 0.0 copy-start
  3.0 0.0 copy-start.1
  3.0 1.7 %pair_blocks.1 = f32[4,8,128,128]{3,2,1,0:T(8,128)S(1)} custom-call(f32[8,8,128,128]{3,2,1,0:T(8,128)} %left), custom_call_target="tpu_custom_call" | custom-call | flops 1 | bytes 1 | tf_op jit(solution)/shard_map/pair_blocks/pallas_call | solution.py:377
  4.7 0.0 copy-start.4
  4.7 0.0 copy-start.2
  4.7 0.1 collective-permute-start.2
  4.9 0.5 %collective-permute-start.1 = (f32[4,8,128,128]{3,2,1,0:T(8,128)S(1)}, f32[4,8,128,128]{3,2,1,0:T(8,128)S(1)}, u32[]{:S(2)}, u32[]{:S(2)}) collective-permute-start(f32[4,8,128,128]{3,2,1,0:T(8,128)S(1)} %pair_blocks.1), channel_id=1, source_target_pairs={{0,1},{1,0},{2,3},{3,2},{4,5},{5,4},{6,7},{7,6},{8,9},{9,8},{10,11... | collective-permute-start | bytes 6291464 | tf_op jit(solution)/shard_map/ppermute | solution.py:319
  5.3 0.0 copy-done.5
  5.3 3.7 %collective-permute-start.3 = (f32[128,256]{1,0:T(8,128)S(1)}, f32[128,256]{1,0:T(8,128)S(1)}, u32[]{:S(2)}, u32[]{:S(2)}) collective-permute-start(f32[128,256]{1,0:T(8,128)S(1)} %copy-done.5), channel_id=1, source_target_pairs={{8,0},{12,4},{0,8},{4,12},{9,1},{13,5},{1,9},{5,13},{10,2},{14,6},... | collective-permute-start | bytes 393224 | tf_op jit(solution)/shard_map/ppermute | solution.py:354
  9.0 0.0 copy-done
  9.0 2.2 %own_terms.1 = (f32[4,8,128,128]{3,2,1,0:T(8,128)S(1)}, f32[8,256,256]{2,1,0:T(8,128)S(1)}, bf16[768,768]{1,0:T(8,128)(2,1)S(1)}, f32[1024,256]{1,0:T(8,128)S(1)}) custom-call(f32[8,8,128,128]{3,2,1,0:T(8,128)} %left, f32[8,256,256]{2,1,0:T(8,128)} %right_hbm.1, s32[8]{0:T(128)S(1)} %copy-done.1, f32[1024,256]{1,0:T(8,128)S(1)} %copy-done, ...), custom_call_target="tpu_custom_call" | custom-call | flops 1 | bytes 1 | tf_op jit(solution)/shard_map/own_terms/pallas_call | solution.py:428
  11.2 0.0 copy-done.4
  11.2 0.1 collective-permute-start.7
  11.3 3.0 %own_near.1.refs_0_ = f32[512,256]{1,0:T(8,128)S(1)} custom-call(s32[8]{0:T(128)S(1)} %copy-done.2, f32[4,8,128,128]{3,2,1,0:T(8,128)S(1)} %get-tuple-element.23.left.refs_3_, f32[8,256,256]{2,1,0:T(8,128)S(1)} %get-tuple-element.24.right.refs_4_, bf16[768,768]{1,0:T(8,128)(2,1)S(1)} %get-tuple-element.27.src), custom_call_target="tpu_custom_call" | custom-call | flops 1 | bytes 1 | tf_op jit(solution)/shard_map/own_near/pallas_call | solution.py:395
  14.3 0.0 copy-done.3
  14.3 3.8 %collective-permute-start.5 = (f32[128,256]{1,0:T(8,128)S(1)}, f32[128,256]{1,0:T(8,128)S(1)}, u32[]{:S(2)}, u32[]{:S(2)}) collective-permute-start(f32[128,256]{1,0:T(8,128)S(1)} %copy-done.3), channel_id=1, source_target_pairs={{0,4},{4,8},{8,12},{5,1},{9,5},{13,9},{2,6},{6,10},{10,14},{7,3},{... | collective-permute-start | bytes 393224 | tf_op jit(solution)/shard_map/ppermute | solution.py:445
  18.1 0.9 %collective-permute-done.3 = f32[128,256]{1,0:T(8,128)S(1)} collective-permute-done((f32[128,256]{1,0:T(8,128)S(1)}, f32[128,256]{1,0:T(8,128)S(1)}, u32[]{:S(2)}, u32[]{:S(2)}) %collective-permute-start.3) | collective-permute-done | bytes 131104 | tf_op jit(solution)/shard_map/ppermute | solution.py:354
  19.0 1.8 %collective-permute-start.4 = (f32[1,128,256]{2,1,0:T(8,128)S(1)}, f32[1,128,256]{2,1,0:T(8,128)S(1)}, u32[]{:S(2)}, u32[]{:S(2)}) collective-permute-start(f32[1,128,256]{2,1,0:T(8,128)S(1)} %bitcast.4), channel_id=1, source_target_pairs={{0,2},{1,3},{2,0},{3,1},{4,6},{5,7},{6,4},{7,5},{8,10},{9,11},{10,... | collective-permute-start | bytes 393224 | tf_op jit(solution)/shard_map/ppermute | solution.py:319
  20.8 0.0 collective-permute-done.2.right.refs_6_
  20.8 0.0 collective-permute-done.1.left.refs_5_
  20.8 2.1 %pair_near.1.refs_10_ = f32[512,256]{1,0:T(8,128)S(1)} custom-call(s32[8]{0:T(128)S(1)} %collective-permute-done.cls.refs_1_, f32[4,8,128,128]{3,2,1,0:T(8,128)S(1)} %collective-permute-done.1.left.refs_5_, f32[8,256,256]{2,1,0:T(8,128)S(1)} %collective-permute-done.2.right.refs_6_, bf16[768,768]{1,0:T(8,128)(2,1)S(1)} %get-tuple-element.27.src, ...), custom_call_target="tpu_custom_call" | custom-call | flops 1 | bytes 1 | tf_op jit(solution)/shard_map/pair_near/pallas_call | solution.py:395
  22.9 0.0 collective-permute-done.7
  22.9 0.6 %collective-permute-start.8 = (f32[1,128,256]{2,1,0:T(8,128)S(1)}, f32[1,128,256]{2,1,0:T(8,128)S(1)}, u32[]{:S(2)}, u32[]{:S(2)}) collective-permute-start(f32[1,128,256]{2,1,0:T(8,128)S(1)} %bitcast.2), channel_id=1, source_target_pairs={{0,2},{1,3},{2,0},{3,1},{4,6},{5,7},{6,4},{7,5},{8,10},{9,11},{10,... | collective-permute-start | bytes 393224 | tf_op jit(solution)/shard_map/ppermute | solution.py:319
  23.5 0.0 collective-permute-done.5.refs_11_
  23.5 0.5 %collective-permute-done.4.refs_9_ = f32[1,128,256]{2,1,0:T(8,128)S(1)} collective-permute-done((f32[1,128,256]{2,1,0:T(8,128)S(1)}, f32[1,128,256]{2,1,0:T(8,128)S(1)}, u32[]{:S(2)}, u32[]{:S(2)}) %collective-permute-start.4) | collective-permute-done | bytes 131104 | tf_op jit(solution)/shard_map/ppermute | solution.py:319
  24.0 2.3 %far.2 = (f32[256,256]{1,0:T(8,128)S(1)}, f32[16,128]{1,0:T(8,128)S(1)}) custom-call(s32[8]{0:T(128)S(1)} %copy-done.2, s32[8]{0:T(128)S(1)} %collective-permute-done.cls.refs_1_, s32[8]{0:T(128)S(1)} %copy-done.1, f32[4,8,128,128]{3,2,1,0:T(8,128)S(1)} %get-tuple-element.23.left.refs_3_, f32[8,256,256]{2,1,0:T(8,128)S(1)} %get-tuple-element.24.right.refs_4_, ...), custom_call_target="tpu_custom_call" | custom-call | flops 1 | bytes 1 | tf_op jit(solution)/shard_map/far/pallas_call | solution.py:410
  26.3 3.0 %collective-permute-start.6 = (f32[256,256]{1,0:T(8,128)S(1)}, f32[256,256]{1,0:T(8,128)S(1)}, u32[]{:S(2)}, u32[]{:S(2)}) collective-permute-start(f32[256,256]{1,0:T(8,128)S(1)} %get-tuple-element.31.part), channel_id=1, source_target_pairs={{0,2},{1,3},{2,0},{3,1},{4,6},{5,7},{6,4},{7,5},{8,10},{9,11},{10,... | collective-permute-start | bytes 786440 | tf_op jit(solution)/shard_map/ppermute | solution.py:319
  29.3 0.0 collective-permute-done.8.refs_9_
  29.3 1.7 %far.3 = (f32[272,256]{1,0:T(8,128)S(1)}, f32[16,128]{1,0:T(8,128)S(1)}) custom-call(s32[8]{0:T(128)S(1)} %copy-done.2, s32[8]{0:T(128)S(1)} %collective-permute-done.cls.refs_1_, s32[8]{0:T(128)S(1)} %copy-done.1, f32[4,8,128,128]{3,2,1,0:T(8,128)S(1)} %get-tuple-element.23.left.refs_3_, f32[8,256,256]{2,1,0:T(8,128)S(1)} %get-tuple-element.24.right.refs_4_, ...), custom_call_target="tpu_custom_call" | custom-call | flops 1 | bytes 1 | tf_op jit(solution)/shard_map/far/pallas_call | solution.py:410
  31.0 0.1 collective-permute-start.9
  31.1 0.1 collective-permute-start.10
  31.2 1.2 %collective-permute-done.10 = f32[16,128]{1,0:T(8,128)S(1)} collective-permute-done((f32[16,128]{1,0:T(8,128)S(1)}, f32[16,128]{1,0:T(8,128)S(1)}, u32[]{:S(2)}, u32[]{:S(2)}) %collective-permute-start.10) | collective-permute-done | bytes 8224 | tf_op jit(solution)/shard_map/ppermute | solution.py:319
  32.3 3.2 %collective-permute-start.13 = (f32[16,128]{1,0:T(8,128)S(1)}, f32[16,128]{1,0:T(8,128)S(1)}, u32[]{:S(2)}, u32[]{:S(2)}) collective-permute-start(f32[16,128]{1,0:T(8,128)S(1)} %add.3.sums), channel_id=1, source_target_pairs={{0,12},{1,15},{2,14},{3,13},{4,8},{5,11},{6,10},{7,9},{8,4},{9,7},... | collective-permute-start | bytes 24584 | tf_op jit(solution)/shard_map/ppermute | solution.py:326
  35.5 0.0 collective-permute-start.12
  35.5 1.2 %collective-permute-start.11 = (f32[16,128]{1,0:T(8,128)S(1)}, f32[16,128]{1,0:T(8,128)S(1)}, u32[]{:S(2)}, u32[]{:S(2)}) collective-permute-start(f32[16,128]{1,0:T(8,128)S(1)} %add.3.sums), channel_id=1, source_target_pairs={{0,4},{1,7},{2,6},{3,5},{4,0},{5,3},{6,2},{7,1},{8,12},{9,15},{10,... | collective-permute-start | bytes 24584 | tf_op jit(solution)/shard_map/ppermute | solution.py:326
  36.7 0.0 collective-permute-done.6.recv
  36.8 1.0 %collective-permute-done.13.third = f32[16,128]{1,0:T(8,128)S(1)} collective-permute-done((f32[16,128]{1,0:T(8,128)S(1)}, f32[16,128]{1,0:T(8,128)S(1)}, u32[]{:S(2)}, u32[]{:S(2)}) %collective-permute-start.13) | collective-permute-done | bytes 8224 | tf_op jit(solution)/shard_map/ppermute | solution.py:326
  37.8 2.3 %collective-permute-done.12.second = f32[16,128]{1,0:T(8,128)S(1)} collective-permute-done((f32[16,128]{1,0:T(8,128)S(1)}, f32[16,128]{1,0:T(8,128)S(1)}, u32[]{:S(2)}, u32[]{:S(2)}) %collective-permute-start.12) | collective-permute-done | bytes 8224 | tf_op jit(solution)/shard_map/ppermute | solution.py:326
  40.0 0.0 collective-permute-done.11.first
  40.0 0.0 collective-permute-done.9.recv_b
  40.0 0.1 totals.1.total
  40.1 0.7 %collective-permute-start.14 = (f32[560,256]{1,0:T(8,128)S(1)}, f32[560,256]{1,0:T(8,128)S(1)}, u32[]{:S(2)}, u32[]{:S(2)}) collective-permute-start(f32[560,256]{1,0:T(8,128)S(1)} %totals.1.total), channel_id=1, source_target_pairs={{0,1},{1,0},{2,3},{3,2},{4,5},{5,4},{6,7},{7,6},{8,9},{9,8},{10,11... | collective-permute-start | bytes 1720328 | tf_op jit(solution)/shard_map/ppermute | solution.py:319
  40.8 1.6 %collective-permute-done.14.total_pair = f32[560,256]{1,0:T(8,128)S(1)} collective-permute-done((f32[560,256]{1,0:T(8,128)S(1)}, f32[560,256]{1,0:T(8,128)S(1)}, u32[]{:S(2)}, u32[]{:S(2)}) %collective-permute-start.14) | collective-permute-done | bytes 573472 | tf_op jit(solution)/shard_map/ppermute | solution.py:319
  42.4 1.4 %residual.1 = (f32[1024,256]{1,0:T(8,128)}, f32[1024,256]{1,0:T(8,128)}) custom-call(f32[1024,256]{1,0:T(8,128)S(1)} %get-tuple-element.22.refs_7_.live, f32[560,256]{1,0:T(8,128)S(1)} %totals.1.total, f32[560,256]{1,0:T(8,128)S(1)} %collective-permute-done.14.total_pair), custom_call_target="tpu_custom_call" | custom-call | flops 1 | bytes 1 | tf_op jit(solution)/shard_map/residual/pallas_call | solution.py:482
  (5 shorter events, 0.0 us)
Async XLA Ops:
  0.6 2.3 %collective-permute-start = (s32[8]{0:T(128)}, s32[8]{0:T(128)S(1)}, u32[]{:S(2)}, u32[]{:S(2)}) collective-permute-start(s32[8]{0:T(128)} %refs_0_.3), channel_id=1, source_target_pairs={{0,1},{1,0},{2,3},{3,2},{4,5},{5,4},{6,7},{7,6},{8,9},{9,8},{10,11... | collective-permute-start | bytes 104 | tf_op jit(solution)/shard_map/ppermute | solution.py:319
  3.0 2.3 %copy-start.5 = (f32[128,256]{1,0:T(8,128)S(1)}, f32[128,256]{1,0:T(8,128)}, u32[]{:S(2)}) copy-start(f32[128,256]{1,0:T(8,128)} %get-tuple-element.20) | copy-start | bytes 393220
  3.0 6.0 %copy-start = (f32[1024,256]{1,0:T(8,128)S(1)}, f32[1024,256]{1,0:T(8,128)}, u32[]{:S(2)}) copy-start(f32[1024,256]{1,0:T(8,128)} %wave.3) | copy-start | bytes 3145732
  3.0 6.0 %copy-start.1 = (s32[8]{0:T(128)S(1)}, s32[8]{0:T(128)}, u32[]{:S(2)}) copy-start(s32[8]{0:T(128)} %refs_2_.3) | copy-start | bytes 100
  4.7 6.5 %copy-start.4 = (f32[128,256]{1,0:T(8,128)S(1)}, f32[128,256]{1,0:T(8,128)}, u32[]{:S(2)}) copy-start(f32[128,256]{1,0:T(8,128)} %get-tuple-element.33) | copy-start | bytes 393220
  4.7 6.6 %copy-start.2 = (s32[8]{0:T(128)S(1)}, s32[8]{0:T(128)}, u32[]{:S(2)}) copy-start(s32[8]{0:T(128)} %refs_0_.3) | copy-start | bytes 100
  4.7 16.1 %collective-permute-start.2 = (f32[8,256,256]{2,1,0:T(8,128)}, f32[8,256,256]{2,1,0:T(8,128)S(1)}, u32[]{:S(2)}, u32[]{:S(2)}) collective-permute-start(f32[8,256,256]{2,1,0:T(8,128)} %right_hbm.1), channel_id=1, source_target_pairs={{0,1},{1,0},{2,3},{3,2},{4,5},{5,4},{6,7},{7,6},{8,9},{9,8},{10,11... | collective-permute-start | bytes 6291464 | tf_op jit(solution)/shard_map/ppermute | solution.py:319
  4.9 15.9 %collective-permute-start.1 = (f32[4,8,128,128]{3,2,1,0:T(8,128)S(1)}, f32[4,8,128,128]{3,2,1,0:T(8,128)S(1)}, u32[]{:S(2)}, u32[]{:S(2)}) collective-permute-start(f32[4,8,128,128]{3,2,1,0:T(8,128)S(1)} %pair_blocks.1), channel_id=1, source_target_pairs={{0,1},{1,0},{2,3},{3,2},{4,5},{5,4},{6,7},{7,6},{8,9},{9,8},{10,11... | collective-permute-start | bytes 6291464 | tf_op jit(solution)/shard_map/ppermute | solution.py:319
  5.3 13.7 %collective-permute-start.3 = (f32[128,256]{1,0:T(8,128)S(1)}, f32[128,256]{1,0:T(8,128)S(1)}, u32[]{:S(2)}, u32[]{:S(2)}) collective-permute-start(f32[128,256]{1,0:T(8,128)S(1)} %copy-done.5), channel_id=1, source_target_pairs={{8,0},{12,4},{0,8},{4,12},{9,1},{13,5},{1,9},{5,13},{10,2},{14,6},... | collective-permute-start | bytes 393224 | tf_op jit(solution)/shard_map/ppermute | solution.py:354
  11.2 11.6 %collective-permute-start.7 = (f32[128,256]{1,0:T(8,128)S(1)}, f32[128,256]{1,0:T(8,128)S(1)}, u32[]{:S(2)}, u32[]{:S(2)}) collective-permute-start(f32[128,256]{1,0:T(8,128)S(1)} %copy-done.4), channel_id=1, source_target_pairs={{8,0},{12,4},{0,8},{4,12},{9,1},{13,5},{1,9},{5,13},{10,2},{14,6},... | collective-permute-start | bytes 393224 | tf_op jit(solution)/shard_map/ppermute | solution.py:354
  11.3 3.0 %copy-start.3 = (f32[128,256]{1,0:T(8,128)S(1)}, f32[128,256]{1,0:T(8,128)}, u32[]{:S(2)}) copy-start(f32[128,256]{1,0:T(8,128)} %get-tuple-element.30) | copy-start | bytes 393220
  14.3 9.2 %collective-permute-start.5 = (f32[128,256]{1,0:T(8,128)S(1)}, f32[128,256]{1,0:T(8,128)S(1)}, u32[]{:S(2)}, u32[]{:S(2)}) collective-permute-start(f32[128,256]{1,0:T(8,128)S(1)} %copy-done.3), channel_id=1, source_target_pairs={{0,4},{4,8},{8,12},{5,1},{9,5},{13,9},{2,6},{6,10},{10,14},{7,3},{... | collective-permute-start | bytes 393224 | tf_op jit(solution)/shard_map/ppermute | solution.py:445
  19.0 5.0 %collective-permute-start.4 = (f32[1,128,256]{2,1,0:T(8,128)S(1)}, f32[1,128,256]{2,1,0:T(8,128)S(1)}, u32[]{:S(2)}, u32[]{:S(2)}) collective-permute-start(f32[1,128,256]{2,1,0:T(8,128)S(1)} %bitcast.4), channel_id=1, source_target_pairs={{0,2},{1,3},{2,0},{3,1},{4,6},{5,7},{6,4},{7,5},{8,10},{9,11},{10,... | collective-permute-start | bytes 393224 | tf_op jit(solution)/shard_map/ppermute | solution.py:319
  22.9 6.4 %collective-permute-start.8 = (f32[1,128,256]{2,1,0:T(8,128)S(1)}, f32[1,128,256]{2,1,0:T(8,128)S(1)}, u32[]{:S(2)}, u32[]{:S(2)}) collective-permute-start(f32[1,128,256]{2,1,0:T(8,128)S(1)} %bitcast.2), channel_id=1, source_target_pairs={{0,2},{1,3},{2,0},{3,1},{4,6},{5,7},{6,4},{7,5},{8,10},{9,11},{10,... | collective-permute-start | bytes 393224 | tf_op jit(solution)/shard_map/ppermute | solution.py:319
  26.3 10.4 %collective-permute-start.6 = (f32[256,256]{1,0:T(8,128)S(1)}, f32[256,256]{1,0:T(8,128)S(1)}, u32[]{:S(2)}, u32[]{:S(2)}) collective-permute-start(f32[256,256]{1,0:T(8,128)S(1)} %get-tuple-element.31.part), channel_id=1, source_target_pairs={{0,2},{1,3},{2,0},{3,1},{4,6},{5,7},{6,4},{7,5},{8,10},{9,11},{10,... | collective-permute-start | bytes 786440 | tf_op jit(solution)/shard_map/ppermute | solution.py:319
  31.0 9.0 %collective-permute-start.9 = (f32[272,256]{1,0:T(8,128)S(1)}, f32[272,256]{1,0:T(8,128)S(1)}, u32[]{:S(2)}, u32[]{:S(2)}) collective-permute-start(f32[272,256]{1,0:T(8,128)S(1)} %get-tuple-element.36.part_b), channel_id=1, source_target_pairs={{0,2},{1,3},{2,0},{3,1},{4,6},{5,7},{6,4},{7,5},{8,10},{9,11},{10,... | collective-permute-start | bytes 835592 | tf_op jit(solution)/shard_map/ppermute | solution.py:319
  31.1 1.2 %collective-permute-start.10 = (f32[16,128]{1,0:T(8,128)S(1)}, f32[16,128]{1,0:T(8,128)S(1)}, u32[]{:S(2)}, u32[]{:S(2)}) collective-permute-start(f32[16,128]{1,0:T(8,128)S(1)} %get-tuple-element.37), channel_id=1, source_target_pairs={{0,1},{1,0},{2,3},{3,2},{4,5},{5,4},{6,7},{7,6},{8,9},{9,8},{10,11... | collective-permute-start | bytes 24584 | tf_op jit(solution)/shard_map/ppermute | solution.py:319
  32.3 5.4 %collective-permute-start.13 = (f32[16,128]{1,0:T(8,128)S(1)}, f32[16,128]{1,0:T(8,128)S(1)}, u32[]{:S(2)}, u32[]{:S(2)}) collective-permute-start(f32[16,128]{1,0:T(8,128)S(1)} %add.3.sums), channel_id=1, source_target_pairs={{0,12},{1,15},{2,14},{3,13},{4,8},{5,11},{6,10},{7,9},{8,4},{9,7},... | collective-permute-start | bytes 24584 | tf_op jit(solution)/shard_map/ppermute | solution.py:326
  35.5 4.5 %collective-permute-start.12 = (f32[16,128]{1,0:T(8,128)S(1)}, f32[16,128]{1,0:T(8,128)S(1)}, u32[]{:S(2)}, u32[]{:S(2)}) collective-permute-start(f32[16,128]{1,0:T(8,128)S(1)} %add.3.sums), channel_id=1, source_target_pairs={{0,8},{1,11},{2,10},{3,9},{4,12},{5,15},{6,14},{7,13},{8,0},{9,3},... | collective-permute-start | bytes 24584 | tf_op jit(solution)/shard_map/ppermute | solution.py:326
  35.5 4.5 %collective-permute-start.11 = (f32[16,128]{1,0:T(8,128)S(1)}, f32[16,128]{1,0:T(8,128)S(1)}, u32[]{:S(2)}, u32[]{:S(2)}) collective-permute-start(f32[16,128]{1,0:T(8,128)S(1)} %add.3.sums), channel_id=1, source_target_pairs={{0,4},{1,7},{2,6},{3,5},{4,0},{5,3},{6,2},{7,1},{8,12},{9,15},{10,... | collective-permute-start | bytes 24584 | tf_op jit(solution)/shard_map/ppermute | solution.py:326
  40.1 2.3 %collective-permute-start.14 = (f32[560,256]{1,0:T(8,128)S(1)}, f32[560,256]{1,0:T(8,128)S(1)}, u32[]{:S(2)}, u32[]{:S(2)}) collective-permute-start(f32[560,256]{1,0:T(8,128)S(1)} %totals.1.total), channel_id=1, source_target_pairs={{0,1},{1,0},{2,3},{3,2},{4,5},{5,4},{6,7},{7,6},{8,9},{9,8},{10,11... | collective-permute-start | bytes 1720328 | tf_op jit(solution)/shard_map/ppermute | solution.py:319

commit v9 on v8

--- a/solution.py
+++ b/solution.py
@@ -259,6 +259,10 @@
     total[...] = part[...] + recv[...]
 
 
+def pass_kernel(source, target):
+    target[...] = source[...]
+
+
 def combine_kernel(total_a, part_b, recv_b, sums, first, second, third, total):
     at = total_a.shape[0]
     rows = 2 * at
@@ -383,10 +387,10 @@
         compiler_params=params(CUT_VMEM),
         cost_estimate=cost(1, 1),
         name="pair_blocks",
-    )(after(left_blocks, mine_a, cls_pair))
-    left_pair = swap(left_send, "mpo", 1)
+    )(after(left_blocks, mine_a))
+    left_pair = swap(after(left_send, cls_pair), "mpo", 1)
     far_a = far(mine_a)
-    right_pair = swap(after(right_blocks, left_send), "mpo", 1)
+    right_pair = swap(after(right_blocks, left_send, cls_pair), "mpo", 1)
 
     lists = [pltpu.SMEM((2 * terms,), jnp.int32)] * 2
 
@@ -439,11 +443,20 @@
         compiler_params=params(OWN_VMEM),
         cost_estimate=cost(1, 1),
         name="own_terms",
-    )(left_blocks, right_blocks, after(block_rows, mine_a), whole, wavefunction)
+    )(left_blocks, right_blocks, after(block_rows, mine_a, left_send, cls_pair), whole, wavefunction)
     far_b = far(after(mine_b, src))
     acc = near("own_near", term_charge, left, right, src)
     halo = lax.ppermute(after(halo, acc), ("sec", "mpo"), halo_pairs)
-    other_a = swap(after(far_a, acc), "mpo", 2)
+    far_a = pl.pallas_call(
+        pass_kernel,
+        out_shape=jax.ShapeDtypeStruct(far_a.shape, F32),
+        in_specs=[VMEM],
+        out_specs=VMEM,
+        compiler_params=params(NEAR_VMEM),
+        cost_estimate=cost(5e10, 1),
+        name="first_far",
+    )(after(far_a, acc))
+    other_a = swap(far_a, "mpo", 2)
     acc = near("pair_near", cls_pair, left_pair, right_pair, src, acc)
     other_b = swap(after(far_b, acc), "mpo", 2)
     part_a, sums = add_far(0, far_a, other_a, acc, halo)

time: 44.1 us -> 43.2 us (0.980)
  starting transfers between devices: 19.2 us -> 17.1 us
  Pallas kernels: 16.2 us -> 17 us
    ppermute x9, starting transfers between devices: 7.3 us -> 4.59 us  [swap(): return lax.ppermute(array, axis, pairs)]
    ppermute x9, waiting for transfers between devices: 3.24 us -> 5.16 us  [swap(): return lax.ppermute(array, axis, pairs)]
    ppermute x2, waiting for transfers between devices: 0.91 us -> 0.01 us  [far(): return lax.ppermute(array, 'sec', up + down)[None]]
    pallas_call x2, Pallas kernels: 5.05 us -> 5.66 us  [near(): pl.pallas_call(functools.partial(near_kernel, chained), out_shape=shape(h...]
    ppermute x2, starting transfers between devices: 3.75 us -> 4.35 us  [far(): return lax.ppermute(array, 'sec', up + down)[None]]
    ppermute x3, waiting for transfers between devices: 3.29 us -> 2.71 us  [far_parts(): parts.append(lax.ppermute(sums, ('sec', 'mpo'), pairs))]
  transfers between devices with their start and end apart: 15 -> 15, of which waited for: 6 -> 6; matrix products, arithmetic and copies ran while one was open for 0% -> 0% of each run, Pallas kernels for 30% -> 32%
where the time goes in v9:
time: 43.2 us; the launch traced here: 42.9 us
  starting transfers between devices  17.1 us (40%)
  Pallas kernels  17 us (39%)
  waiting for transfers between devices  7.88 us (18%)
  between operations  0.83 us (2%)
    pallas_call x2, Pallas kernels, near(): pl.pallas_call(functools.partial(near_kernel, chained), out_shape=shape(h...  5.66 us
    ppermute x9, waiting for transfers between devices, swap(): return lax.ppermute(array, axis, pairs)  5.16 us
    ppermute x9, starting transfers between devices, swap(): return lax.ppermute(array, axis, pairs)  4.59 us
    ppermute x3, starting transfers between devices, far_parts(): parts.append(lax.ppermute(sums, ('sec', 'mpo'), pairs))  4.39 us
    ppermute x2, starting transfers between devices, far(): return lax.ppermute(array, 'sec', up + down)[None]  4.35 us
    pallas_call x2, Pallas kernels, add_far(): pl.pallas_call(functools.partial(far_kernel, chunk, shift, secs), out_sha...  4.22 us
    ppermute x1, starting transfers between devices, local(): halo = lax.ppermute(after(halo, acc), ('sec', 'mpo'), halo_pairs)  3.77 us
    ppermute x3, waiting for transfers between devices, far_parts(): parts.append(lax.ppermute(sums, ('sec', 'mpo'), pairs))  2.71 us
  transfers between devices with their start and end apart: 15, of which 6 were waited for; matrix products, arithmetic and copies ran while one was open for 0% of the time, Pallas kernels for 32%

profile of v9, /device:TPU:0, one launch (start us, length us, event | category | flops | bytes accessed | tf_op | source)
XLA Modules:
  0.0 42.9 jit_solution(4445714596912470936)
XLA Ops:
  0.6 1.8 %prepare.1 = (f32[128,256]{1,0:T(8,128)}, f32[128,256]{1,0:T(8,128)}, f32[128,256]{1,0:T(8,128)}) custom-call(s32[8]{0:T(128)} %refs_2_.3, f32[1024,256]{1,0:T(8,128)} %wave.3), custom_call_target="tpu_custom_call" | custom-call | flops 1 | bytes 1 | tf_op jit(solution)/shard_map/prepare/pallas_call | solution.py:371
  2.4 0.0 copy-start.3
  2.5 0.0 copy-start
  2.5 0.0 copy-start.1
  2.5 4.1 %collective-permute-start.3 = (f32[128,256]{1,0:T(8,128)}, f32[128,256]{1,0:T(8,128)S(1)}, u32[]{:S(2)}, u32[]{:S(2)}) collective-permute-start(f32[128,256]{1,0:T(8,128)} %get-tuple-element.21), channel_id=1, source_target_pairs={{8,0},{12,4},{0,8},{4,12},{9,1},{13,5},{1,9},{5,13},{10,2},{14,6},... | collective-permute-start | bytes 393224 | tf_op jit(solution)/shard_map/ppermute | solution.py:358
  6.6 0.0 collective-permute-start
  6.6 1.6 %pair_blocks.1 = f32[4,8,128,128]{3,2,1,0:T(8,128)S(1)} custom-call(f32[8,8,128,128]{3,2,1,0:T(8,128)} %left_hbm.1), custom_call_target="tpu_custom_call" | custom-call | flops 1 | bytes 1 | tf_op jit(solution)/shard_map/pair_blocks/pallas_call | solution.py:381
  8.2 0.0 copy-start.5
  8.2 0.0 copy-start.2
  8.2 0.0 collective-permute-done.cls.refs_1_
  8.2 0.6 %collective-permute-start.1 = (f32[4,8,128,128]{3,2,1,0:T(8,128)S(1)}, f32[4,8,128,128]{3,2,1,0:T(8,128)S(1)}, u32[]{:S(2)}, u32[]{:S(2)}) collective-permute-start(f32[4,8,128,128]{3,2,1,0:T(8,128)S(1)} %pair_blocks.1), channel_id=1, source_target_pairs={{0,1},{1,0},{2,3},{3,2},{4,5},{5,4},{6,7},{7,6},{8,9},{9,8},{10,11... | collective-permute-start | bytes 6291464 | tf_op jit(solution)/shard_map/ppermute | solution.py:323
  8.8 0.0 copy-done.3
  8.8 0.1 collective-permute-start.2
  8.9 0.0 copy-done
  8.9 0.0 copy-done.1
  8.9 2.2 %own_terms.1 = (f32[4,8,128,128]{3,2,1,0:T(8,128)S(1)}, f32[8,256,256]{2,1,0:T(8,128)S(1)}, bf16[768,768]{1,0:T(8,128)(2,1)S(1)}, f32[1024,256]{1,0:T(8,128)S(1)}) custom-call(f32[8,8,128,128]{3,2,1,0:T(8,128)} %left_hbm.1, f32[8,256,256]{2,1,0:T(8,128)} %right_hbm.1, s32[8]{0:T(128)S(1)} %copy-done.1, f32[1024,256]{1,0:T(8,128)S(1)} %copy-done, ...), custom_call_target="tpu_custom_call" | custom-call | flops 1 | bytes 1 | tf_op jit(solution)/shard_map/own_terms/pallas_call | solution.py:432
  11.2 0.3 collective-permute-start.7
  11.4 0.0 copy-done.2
  11.4 2.1 %own_near.1.refs_0_ = f32[512,256]{1,0:T(8,128)S(1)} custom-call(s32[8]{0:T(128)S(1)} %copy-done.2, f32[4,8,128,128]{3,2,1,0:T(8,128)S(1)} %get-tuple-element.25.left.refs_3_, f32[8,256,256]{2,1,0:T(8,128)S(1)} %get-tuple-element.26.right.refs_4_, bf16[768,768]{1,0:T(8,128)(2,1)S(1)} %get-tuple-element.29.src), custom_call_target="tpu_custom_call" | custom-call | flops 1 | bytes 1 | tf_op jit(solution)/shard_map/own_near/pallas_call | solution.py:399
  13.5 3.8 %collective-permute-start.5 = (f32[128,256]{1,0:T(8,128)S(1)}, f32[128,256]{1,0:T(8,128)S(1)}, u32[]{:S(2)}, u32[]{:S(2)}) collective-permute-start(f32[128,256]{1,0:T(8,128)S(1)} %copy-done.4), channel_id=1, source_target_pairs={{0,4},{4,8},{8,12},{5,1},{9,5},{13,9},{2,6},{6,10},{10,14},{7,3},{... | collective-permute-start | bytes 393224 | tf_op jit(solution)/shard_map/ppermute | solution.py:449
  17.3 0.0 collective-permute-done.3
  17.3 1.6 %collective-permute-start.4 = (f32[1,128,256]{2,1,0:T(8,128)S(1)}, f32[1,128,256]{2,1,0:T(8,128)S(1)}, u32[]{:S(2)}, u32[]{:S(2)}) collective-permute-start(f32[1,128,256]{2,1,0:T(8,128)S(1)} %first_far.1.refs_8_), channel_id=1, source_target_pairs={{0,2},{1,3},{2,0},{3,1},{4,6},{5,7},{6,4},{7,5},{8,10},{9,11},{10,... | collective-permute-start | bytes 393224 | tf_op jit(solution)/shard_map/ppermute | solution.py:323
  18.9 0.0 collective-permute-done.1.left.refs_5_
  18.9 0.0 collective-permute-done.2.right.refs_6_
  18.9 3.6 %pair_near.1.refs_10_ = f32[512,256]{1,0:T(8,128)S(1)} custom-call(s32[8]{0:T(128)S(1)} %collective-permute-done.cls.refs_1_, f32[4,8,128,128]{3,2,1,0:T(8,128)S(1)} %collective-permute-done.1.left.refs_5_, f32[8,256,256]{2,1,0:T(8,128)S(1)} %collective-permute-done.2.right.refs_6_, bf16[768,768]{1,0:T(8,128)(2,1)S(1)} %get-tuple-element.29.src, ...), custom_call_target="tpu_custom_call" | custom-call | flops 1 | bytes 1 | tf_op jit(solution)/shard_map/pair_near/pallas_call | solution.py:399
  22.5 0.0 collective-permute-done.7
  22.5 0.2 collective-permute-start.8
  22.7 0.0 collective-permute-done.5.refs_11_
  22.7 0.0 collective-permute-done.4.refs_9_
  22.7 2.5 %far.2 = (f32[256,256]{1,0:T(8,128)S(1)}, f32[16,128]{1,0:T(8,128)S(1)}) custom-call(s32[8]{0:T(128)S(1)} %copy-done.2, s32[8]{0:T(128)S(1)} %collective-permute-done.cls.refs_1_, s32[8]{0:T(128)S(1)} %copy-done.1, f32[4,8,128,128]{3,2,1,0:T(8,128)S(1)} %get-tuple-element.25.left.refs_3_, f32[8,256,256]{2,1,0:T(8,128)S(1)} %get-tuple-element.26.right.refs_4_, ...), custom_call_target="tpu_custom_call" | custom-call | flops 1 | bytes 1 | tf_op jit(solution)/shard_map/far/pallas_call | solution.py:414
  25.3 1.9 %collective-permute-start.6 = (f32[256,256]{1,0:T(8,128)S(1)}, f32[256,256]{1,0:T(8,128)S(1)}, u32[]{:S(2)}, u32[]{:S(2)}) collective-permute-start(f32[256,256]{1,0:T(8,128)S(1)} %get-tuple-element.33.part), channel_id=1, source_target_pairs={{0,2},{1,3},{2,0},{3,1},{4,6},{5,7},{6,4},{7,5},{8,10},{9,11},{10,... | collective-permute-start | bytes 786440 | tf_op jit(solution)/shard_map/ppermute | solution.py:323
  27.2 0.6 %collective-permute-done.8.refs_9_ = f32[1,128,256]{2,1,0:T(8,128)S(1)} collective-permute-done((f32[1,128,256]{2,1,0:T(8,128)S(1)}, f32[1,128,256]{2,1,0:T(8,128)S(1)}, u32[]{:S(2)}, u32[]{:S(2)}) %collective-permute-start.8) | collective-permute-done | bytes 131104 | tf_op jit(solution)/shard_map/ppermute | solution.py:323
  27.8 1.7 %far.3 = (f32[272,256]{1,0:T(8,128)S(1)}, f32[16,128]{1,0:T(8,128)S(1)}) custom-call(s32[8]{0:T(128)S(1)} %copy-done.2, s32[8]{0:T(128)S(1)} %collective-permute-done.cls.refs_1_, s32[8]{0:T(128)S(1)} %copy-done.1, f32[4,8,128,128]{3,2,1,0:T(8,128)S(1)} %get-tuple-element.25.left.refs_3_, f32[8,256,256]{2,1,0:T(8,128)S(1)} %get-tuple-element.26.right.refs_4_, ...), custom_call_target="tpu_custom_call" | custom-call | flops 1 | bytes 1 | tf_op jit(solution)/shard_map/far/pallas_call | solution.py:414
  29.5 0.1 collective-permute-start.9
  29.6 0.1 collective-permute-start.10
  29.6 1.2 %collective-permute-done.10 = f32[16,128]{1,0:T(8,128)S(1)} collective-permute-done((f32[16,128]{1,0:T(8,128)S(1)}, f32[16,128]{1,0:T(8,128)S(1)}, u32[]{:S(2)}, u32[]{:S(2)}) %collective-permute-start.10) | collective-permute-done | bytes 8224 | tf_op jit(solution)/shard_map/ppermute | solution.py:323
  30.8 2.6 %collective-permute-start.13 = (f32[16,128]{1,0:T(8,128)S(1)}, f32[16,128]{1,0:T(8,128)S(1)}, u32[]{:S(2)}, u32[]{:S(2)}) collective-permute-start(f32[16,128]{1,0:T(8,128)S(1)} %add.3.sums), channel_id=1, source_target_pairs={{0,12},{1,15},{2,14},{3,13},{4,8},{5,11},{6,10},{7,9},{8,4},{9,7},... | collective-permute-start | bytes 24584 | tf_op jit(solution)/shard_map/ppermute | solution.py:330
  33.4 0.2 collective-permute-start.12
  33.6 1.6 %collective-permute-start.11 = (f32[16,128]{1,0:T(8,128)S(1)}, f32[16,128]{1,0:T(8,128)S(1)}, u32[]{:S(2)}, u32[]{:S(2)}) collective-permute-start(f32[16,128]{1,0:T(8,128)S(1)} %add.3.sums), channel_id=1, source_target_pairs={{0,4},{1,7},{2,6},{3,5},{4,0},{5,3},{6,2},{7,1},{8,12},{9,15},{10,... | collective-permute-start | bytes 24584 | tf_op jit(solution)/shard_map/ppermute | solution.py:330
  35.2 0.0 collective-permute-done.6.recv
  35.2 1.0 %collective-permute-done.13.third = f32[16,128]{1,0:T(8,128)S(1)} collective-permute-done((f32[16,128]{1,0:T(8,128)S(1)}, f32[16,128]{1,0:T(8,128)S(1)}, u32[]{:S(2)}, u32[]{:S(2)}) %collective-permute-start.13) | collective-permute-done | bytes 8224 | tf_op jit(solution)/shard_map/ppermute | solution.py:330
  36.2 1.7 %collective-permute-done.12.second = f32[16,128]{1,0:T(8,128)S(1)} collective-permute-done((f32[16,128]{1,0:T(8,128)S(1)}, f32[16,128]{1,0:T(8,128)S(1)}, u32[]{:S(2)}, u32[]{:S(2)}) %collective-permute-start.12) | collective-permute-done | bytes 8224 | tf_op jit(solution)/shard_map/ppermute | solution.py:330
  37.9 0.0 collective-permute-done.11.first
  37.9 1.4 %collective-permute-done.9.recv_b = f32[272,256]{1,0:T(8,128)S(1)} collective-permute-done((f32[272,256]{1,0:T(8,128)S(1)}, f32[272,256]{1,0:T(8,128)S(1)}, u32[]{:S(2)}, u32[]{:S(2)}) %collective-permute-start.9) | collective-permute-done | bytes 278560 | tf_op jit(solution)/shard_map/ppermute | solution.py:323
  39.4 0.1 totals.1.total
  39.4 0.1 collective-permute-start.14
  39.5 2.0 %collective-permute-done.14.total_pair = f32[560,256]{1,0:T(8,128)S(1)} collective-permute-done((f32[560,256]{1,0:T(8,128)S(1)}, f32[560,256]{1,0:T(8,128)S(1)}, u32[]{:S(2)}, u32[]{:S(2)}) %collective-permute-start.14) | collective-permute-done | bytes 573472 | tf_op jit(solution)/shard_map/ppermute | solution.py:323
  41.5 1.4 %residual.1 = (f32[1024,256]{1,0:T(8,128)}, f32[1024,256]{1,0:T(8,128)}) custom-call(f32[1024,256]{1,0:T(8,128)S(1)} %get-tuple-element.24.refs_7_.live, f32[560,256]{1,0:T(8,128)S(1)} %totals.1.total, f32[560,256]{1,0:T(8,128)S(1)} %collective-permute-done.14.total_pair), custom_call_target="tpu_custom_call" | custom-call | flops 1 | bytes 1 | tf_op jit(solution)/shard_map/residual/pallas_call | solution.py:495
  (6 shorter events, 0.0 us)
Async XLA Ops:
  2.4 6.4 %copy-start.3 = (f32[8,256,256]{2,1,0:T(8,128)S(1)}, f32[8,256,256]{2,1,0:T(8,128)}, u32[]{:S(2)}) copy-start(f32[8,256,256]{2,1,0:T(8,128)} %right_hbm.1) | copy-start | bytes 6291460
  2.5 6.4 %copy-start = (f32[1024,256]{1,0:T(8,128)S(1)}, f32[1024,256]{1,0:T(8,128)}, u32[]{:S(2)}) copy-start(f32[1024,256]{1,0:T(8,128)} %wave.3) | copy-start | bytes 3145732
  2.5 6.4 %copy-start.1 = (s32[8]{0:T(128)S(1)}, s32[8]{0:T(128)}, u32[]{:S(2)}) copy-start(s32[8]{0:T(128)} %refs_2_.3) | copy-start | bytes 100
  2.5 14.8 %collective-permute-start.3 = (f32[128,256]{1,0:T(8,128)}, f32[128,256]{1,0:T(8,128)S(1)}, u32[]{:S(2)}, u32[]{:S(2)}) collective-permute-start(f32[128,256]{1,0:T(8,128)} %get-tuple-element.21), channel_id=1, source_target_pairs={{8,0},{12,4},{0,8},{4,12},{9,1},{13,5},{1,9},{5,13},{10,2},{14,6},... | collective-permute-start | bytes 393224 | tf_op jit(solution)/shard_map/ppermute | solution.py:358
  6.6 1.6 %collective-permute-start = (s32[8]{0:T(128)}, s32[8]{0:T(128)S(1)}, u32[]{:S(2)}, u32[]{:S(2)}) collective-permute-start(s32[8]{0:T(128)} %refs_0_.3), channel_id=1, source_target_pairs={{0,1},{1,0},{2,3},{3,2},{4,5},{5,4},{6,7},{7,6},{8,9},{9,8},{10,11... | collective-permute-start | bytes 104 | tf_op jit(solution)/shard_map/ppermute | solution.py:323
  8.2 3.0 %copy-start.5 = (f32[128,256]{1,0:T(8,128)S(1)}, f32[128,256]{1,0:T(8,128)}, u32[]{:S(2)}) copy-start(f32[128,256]{1,0:T(8,128)} %get-tuple-element.35) | copy-start | bytes 393220
  8.2 3.2 %copy-start.2 = (s32[8]{0:T(128)S(1)}, s32[8]{0:T(128)}, u32[]{:S(2)}) copy-start(s32[8]{0:T(128)} %refs_0_.3) | copy-start | bytes 100
  8.2 10.7 %collective-permute-start.1 = (f32[4,8,128,128]{3,2,1,0:T(8,128)S(1)}, f32[4,8,128,128]{3,2,1,0:T(8,128)S(1)}, u32[]{:S(2)}, u32[]{:S(2)}) collective-permute-start(f32[4,8,128,128]{3,2,1,0:T(8,128)S(1)} %pair_blocks.1), channel_id=1, source_target_pairs={{0,1},{1,0},{2,3},{3,2},{4,5},{5,4},{6,7},{7,6},{8,9},{9,8},{10,11... | collective-permute-start | bytes 6291464 | tf_op jit(solution)/shard_map/ppermute | solution.py:323
  8.8 10.1 %collective-permute-start.2 = (f32[8,256,256]{2,1,0:T(8,128)S(1)}, f32[8,256,256]{2,1,0:T(8,128)S(1)}, u32[]{:S(2)}, u32[]{:S(2)}) collective-permute-start(f32[8,256,256]{2,1,0:T(8,128)S(1)} %copy-done.3), channel_id=1, source_target_pairs={{0,1},{1,0},{2,3},{3,2},{4,5},{5,4},{6,7},{7,6},{8,9},{9,8},{10,11... | collective-permute-start | bytes 6291464 | tf_op jit(solution)/shard_map/ppermute | solution.py:323
  11.2 11.3 %collective-permute-start.7 = (f32[128,256]{1,0:T(8,128)S(1)}, f32[128,256]{1,0:T(8,128)S(1)}, u32[]{:S(2)}, u32[]{:S(2)}) collective-permute-start(f32[128,256]{1,0:T(8,128)S(1)} %copy-done.5), channel_id=1, source_target_pairs={{8,0},{12,4},{0,8},{4,12},{9,1},{13,5},{1,9},{5,13},{10,2},{14,6},... | collective-permute-start | bytes 393224 | tf_op jit(solution)/shard_map/ppermute | solution.py:358
  11.4 2.1 %copy-start.4 = (f32[128,256]{1,0:T(8,128)S(1)}, f32[128,256]{1,0:T(8,128)}, u32[]{:S(2)}) copy-start(f32[128,256]{1,0:T(8,128)} %get-tuple-element.32) | copy-start | bytes 393220
  13.5 9.2 %collective-permute-start.5 = (f32[128,256]{1,0:T(8,128)S(1)}, f32[128,256]{1,0:T(8,128)S(1)}, u32[]{:S(2)}, u32[]{:S(2)}) collective-permute-start(f32[128,256]{1,0:T(8,128)S(1)} %copy-done.4), channel_id=1, source_target_pairs={{0,4},{4,8},{8,12},{5,1},{9,5},{13,9},{2,6},{6,10},{10,14},{7,3},{... | collective-permute-start | bytes 393224 | tf_op jit(solution)/shard_map/ppermute | solution.py:449
  17.3 5.4 %collective-permute-start.4 = (f32[1,128,256]{2,1,0:T(8,128)S(1)}, f32[1,128,256]{2,1,0:T(8,128)S(1)}, u32[]{:S(2)}, u32[]{:S(2)}) collective-permute-start(f32[1,128,256]{2,1,0:T(8,128)S(1)} %first_far.1.refs_8_), channel_id=1, source_target_pairs={{0,2},{1,3},{2,0},{3,1},{4,6},{5,7},{6,4},{7,5},{8,10},{9,11},{10,... | collective-permute-start | bytes 393224 | tf_op jit(solution)/shard_map/ppermute | solution.py:323
  22.5 5.3 %collective-permute-start.8 = (f32[1,128,256]{2,1,0:T(8,128)S(1)}, f32[1,128,256]{2,1,0:T(8,128)S(1)}, u32[]{:S(2)}, u32[]{:S(2)}) collective-permute-start(f32[1,128,256]{2,1,0:T(8,128)S(1)} %bitcast.2), channel_id=1, source_target_pairs={{0,2},{1,3},{2,0},{3,1},{4,6},{5,7},{6,4},{7,5},{8,10},{9,11},{10,... | collective-permute-start | bytes 393224 | tf_op jit(solution)/shard_map/ppermute | solution.py:323
  25.3 9.9 %collective-permute-start.6 = (f32[256,256]{1,0:T(8,128)S(1)}, f32[256,256]{1,0:T(8,128)S(1)}, u32[]{:S(2)}, u32[]{:S(2)}) collective-permute-start(f32[256,256]{1,0:T(8,128)S(1)} %get-tuple-element.33.part), channel_id=1, source_target_pairs={{0,2},{1,3},{2,0},{3,1},{4,6},{5,7},{6,4},{7,5},{8,10},{9,11},{10,... | collective-permute-start | bytes 786440 | tf_op jit(solution)/shard_map/ppermute | solution.py:323
  29.5 9.9 %collective-permute-start.9 = (f32[272,256]{1,0:T(8,128)S(1)}, f32[272,256]{1,0:T(8,128)S(1)}, u32[]{:S(2)}, u32[]{:S(2)}) collective-permute-start(f32[272,256]{1,0:T(8,128)S(1)} %get-tuple-element.38.part_b), channel_id=1, source_target_pairs={{0,2},{1,3},{2,0},{3,1},{4,6},{5,7},{6,4},{7,5},{8,10},{9,11},{10,... | collective-permute-start | bytes 835592 | tf_op jit(solution)/shard_map/ppermute | solution.py:323
  29.6 1.2 %collective-permute-start.10 = (f32[16,128]{1,0:T(8,128)S(1)}, f32[16,128]{1,0:T(8,128)S(1)}, u32[]{:S(2)}, u32[]{:S(2)}) collective-permute-start(f32[16,128]{1,0:T(8,128)S(1)} %get-tuple-element.39), channel_id=1, source_target_pairs={{0,1},{1,0},{2,3},{3,2},{4,5},{5,4},{6,7},{7,6},{8,9},{9,8},{10,11... | collective-permute-start | bytes 24584 | tf_op jit(solution)/shard_map/ppermute | solution.py:323
  30.8 5.4 %collective-permute-start.13 = (f32[16,128]{1,0:T(8,128)S(1)}, f32[16,128]{1,0:T(8,128)S(1)}, u32[]{:S(2)}, u32[]{:S(2)}) collective-permute-start(f32[16,128]{1,0:T(8,128)S(1)} %add.3.sums), channel_id=1, source_target_pairs={{0,12},{1,15},{2,14},{3,13},{4,8},{5,11},{6,10},{7,9},{8,4},{9,7},... | collective-permute-start | bytes 24584 | tf_op jit(solution)/shard_map/ppermute | solution.py:330
  33.4 4.5 %collective-permute-start.12 = (f32[16,128]{1,0:T(8,128)S(1)}, f32[16,128]{1,0:T(8,128)S(1)}, u32[]{:S(2)}, u32[]{:S(2)}) collective-permute-start(f32[16,128]{1,0:T(8,128)S(1)} %add.3.sums), channel_id=1, source_target_pairs={{0,8},{1,11},{2,10},{3,9},{4,12},{5,15},{6,14},{7,13},{8,0},{9,3},... | collective-permute-start | bytes 24584 | tf_op jit(solution)/shard_map/ppermute | solution.py:330
  33.6 4.3 %collective-permute-start.11 = (f32[16,128]{1,0:T(8,128)S(1)}, f32[16,128]{1,0:T(8,128)S(1)}, u32[]{:S(2)}, u32[]{:S(2)}) collective-permute-start(f32[16,128]{1,0:T(8,128)S(1)} %add.3.sums), channel_id=1, source_target_pairs={{0,4},{1,7},{2,6},{3,5},{4,0},{5,3},{6,2},{7,1},{8,12},{9,15},{10,... | collective-permute-start | bytes 24584 | tf_op jit(solution)/shard_map/ppermute | solution.py:330
  39.4 2.0 %collective-permute-start.14 = (f32[560,256]{1,0:T(8,128)S(1)}, f32[560,256]{1,0:T(8,128)S(1)}, u32[]{:S(2)}, u32[]{:S(2)}) collective-permute-start(f32[560,256]{1,0:T(8,128)S(1)} %totals.1.total), channel_id=1, source_target_pairs={{0,1},{1,0},{2,3},{3,2},{4,5},{5,4},{6,7},{7,6},{8,9},{9,8},{10,11... | collective-permute-start | bytes 1720328 | tf_op jit(solution)/shard_map/ppermute | solution.py:323
